TPU v7x, 32 devices: a whole 2x2x4 slice. The times are simulated.
32 devices in a mesh: scan: 8 (over z, y), lat: 4 (over x, core).
Axes of the slice: x: 2, y: 2, z: 4, core: 2. Of those that a mesh axis runs over, the one named last changes fastest.
Arguments:
- observed: bfloat16 [96, 256, 512], P('scan', 'lat'), may hold values from 0.099609375 to 4
- estimate: float32 [96, 256, 512], P('scan', 'lat'), may hold values from 0.1 to 4
- column_weights: float32 [512, 512], replicated, may hold values from 0 to 0.5, as said below
- plane_taps: float32 [7], replicated, may hold values from 0.1 to 1
- row_taps: float32 [7], replicated, may hold values from 0.1 to 1
- shear_planes: int32 [512], replicated, may hold values from 1 to 95, as said below
Outputs:
- deskewed: float32 [96, 256, 512], P('scan', 'lat')
Inputs may be any that keep to these rules, and one draw needn't show every extreme that they name: `shear_planes`: never falls from one column to the next; the first column's offset is 1 and the last column's is 95. `column_weights`: zero more than 8 columns away from the diagonal, positive within.
All inputs are finite; a program needn't handle non-finite values.
Results may differ from a plain program's by a relative error of at most 0.0003.
Values sent between devices are 32-bit elements; how exact they have to be, the bound alone decides.
No kernel may reach another device: no remote copies, remote signals or barrier semaphores. Data moves between devices by JAX's collectives and lax.ppermute only.
A program may use at most 64 MiB of HBM per device.

v0:
```python
import jax
import jax.numpy as jnp
from jax import lax
from jax.sharding import PartitionSpec as P

PLANE_HALF = 3
ROW_HALF = 3
SKEW = 2


def padded_2(cells, sides, width):
    for axis, dim in sides:
        count = lax.axis_size(axis)
        ends = count - 1
        head = lax.slice_in_dim(cells, 0, width, axis=dim)
        tail = lax.slice_in_dim(cells, cells.shape[dim] - width, cells.shape[dim], axis=dim)
        cells = jnp.concatenate(
            [
                lax.ppermute(tail, axis, [(i, (i + 1) % count) for i in range(ends)]),
                cells,
                lax.ppermute(head, axis, [((i + 1) % count, i) for i in range(ends)]),
            ],
            axis=dim,
        )
    return cells


def column_mix(field, matrix):
    flat = field.reshape(-1, matrix.shape[0])
    mixed = jnp.dot(
        flat, matrix, precision=lax.Precision.HIGHEST, preferred_element_type=jnp.float32
    )
    return mixed.reshape(field.shape)


def row_pass(padded, kernel, direction):
    halfwidth = (kernel.shape[0] - 1) // 2
    row_count = padded.shape[1] - 2 * halfwidth
    summed = jnp.zeros((padded.shape[0], row_count, padded.shape[2]), jnp.float32)
    for offset in range(-halfwidth, halfwidth + 1):
        begin = halfwidth + direction * offset
        summed = summed + kernel[offset + halfwidth] * padded[:, begin : begin + row_count, :]
    return summed


def plane_pass(padded, kernel, direction):
    halfwidth = (kernel.shape[0] - 1) // 2
    plane_count = padded.shape[0] - 2 * halfwidth
    column_count = padded.shape[2]
    widened = jnp.pad(padded, ((0, 0), (0, 0), (halfwidth * SKEW, halfwidth * SKEW)))
    summed = jnp.zeros((plane_count, padded.shape[1], column_count), jnp.float32)
    for offset in range(-halfwidth, halfwidth + 1):
        begin = halfwidth + direction * offset
        column_start = halfwidth * SKEW - direction * offset * SKEW
        summed = (
            summed
            + kernel[offset + halfwidth]
            * widened[begin : begin + plane_count, :, column_start : column_start + column_count]
        )
    return summed


def row_rim(field):
    return padded_2(field, (("lat", 1),), ROW_HALF)


def plane_rim(field):
    return padded_2(field, (("scan", 0),), PLANE_HALF)


def shift_down(field, amount):
    filler = jnp.zeros((amount,) + field.shape[1:], field.dtype)
    return jnp.concatenate([filler, field[: field.shape[0] - amount]], 0)


def shear_columns(field, offsets):
    plane_count = field.shape[0]
    for bit_place in range((plane_count - 1).bit_length()):
        amount = 1 << bit_place
        chosen = (offsets >> bit_place & 1 == 1)[None, None, :]
        moved = shift_down(field, amount)
        field = jnp.where(chosen, moved, field)
    return field


def on_device(observed, estimate, column_weights, plane_taps, row_taps, shear_planes):
    plane_count, row_count, column_count = estimate.shape
    mixed_cols = column_mix(estimate, column_weights)
    row_blur = row_pass(row_rim(mixed_cols), row_taps, 1)
    blurred = plane_pass(plane_rim(row_blur), plane_taps, 1)
    quotient = observed.astype(jnp.float32) / blurred
    back_planes = plane_pass(plane_rim(quotient), plane_taps, -1)
    back_rows = row_pass(row_rim(back_planes), row_taps, -1)
    correction = column_mix(back_rows, column_weights.T)
    updated = estimate * correction
    group_cols = column_count // lax.axis_size("scan")
    own_shear = lax.dynamic_slice_in_dim(
        shear_planes, lax.axis_index("scan") * group_cols, group_cols
    )
    settled = shear_columns(
        lax.all_to_all(updated, "scan", split_axis=2, concat_axis=0, tiled=True), own_shear
    )
    return lax.all_to_all(settled, "scan", split_axis=0, concat_axis=2, tiled=True)


def solution(mesh):
    placed = (P("scan", "lat", None), P("scan", "lat", None), P(), P(), P(), P())
    return jax.shard_map(
        on_device, mesh=mesh, in_specs=placed, out_specs=P("scan", "lat", None), check_vma=False
    )
```

profile of v0, /device:TPU:29, one launch (start us, length us, event | category | flops | bytes accessed | tf_op | source)
XLA Modules:
  0.0 224.9 jit_solution(4397426099994959872)
XLA Ops:
  1.2 4.0 %fusion.60 = f32[12,64,512]{2,1,0:T(8,128)S(1)} fusion(f32[12,64,512]{2,1,0:T(8,128)} %param.7, f32[512,512]{1,0:T(8,128)S(1)} %copy-done), kind=kOutput, calls=%fused_computation.97 | convolution fusion | flops 2415919104 | bytes 4194304 | tf_op jit(solution)/shard_map/dot_general | solution.py:30
  5.3 3.7 %collective-permute-start = (f32[12,3,512]{2,1,0:T(4,128)S(1)}, f32[12,3,512]{2,1,0:T(4,128)S(1)}, u32[]{:S(2)}, u32[]{:S(2)}) collective-permute-start(f32[12,3,512]{2,1,0:T(4,128)S(1)} %get-tuple-element.13), channel_id=1, source_target_pairs={{0,1},{1,2},{2,3},{4,5},{5,6},{6,7},{8,9},{9,10},{10,11},{12,13},{... | collective-permute-start | bytes 221192 | tf_op jit(solution)/shard_map/ppermute | solution.py:19
  11.6 3.3 %collective-permute-done.1 = f32[12,3,512]{2,1,0:T(4,128)S(1)} collective-permute-done((f32[12,3,512]{2,1,0:T(4,128)S(1)}, f32[12,3,512]{2,1,0:T(4,128)S(1)}, u32[]{:S(2)}, u32[]{:S(2)}) %collective-permute-start.1) | collective-permute-done | bytes 73760 | tf_op jit(solution)/shard_map/ppermute | solution.py:21
  14.9 6.0 %fusion.23 = f32[12,64,512]{2,1,0:T(8,128)S(1)} fusion(f32[12,64,512]{2,1,0:T(8,128)S(1)} %fusion.60, f32[12,3,512]{2,1,0:T(4,128)S(1)} %collective-permute-done.1, f32[12,3,512]{2,1,0:T(4,128)S(1)} %collective-permute-done, f32[]{:T(128)} %bitcast.8, f32[]{:T(128)} %bitcast.7, f32[]{:T(128)} %bitcast.6, f32[]{:T(128)} %bitcast.5, f32[]{:T(128)} %bitcast.4, ...), kind=kLoop, calls=%fused_computation.48 | loop fusion | flops 7471104 | bytes 3293212 | tf_op jit(solution)/shard_map/add | solution.py:42
  22.4 4.0 %collective-permute-start.3 = (f32[3,64,512]{2,1,0:T(8,128)S(1)}, f32[3,64,512]{2,1,0:T(8,128)S(1)}, u32[]{:S(2)}, u32[]{:S(2)}) collective-permute-start(f32[3,64,512]{2,1,0:T(8,128)S(1)} %get-tuple-element.12), channel_id=1, source_target_pairs={{4,0},{8,4},{12,8},{16,12},{20,16},{24,20},{28,24},{5,1},{9,5},{13... | collective-permute-start | bytes 1179656 | tf_op jit(solution)/shard_map/ppermute | solution.py:21
  27.1 4.5 %collective-permute-done.2 = f32[3,64,512]{2,1,0:T(8,128)S(1)} collective-permute-done((f32[3,64,512]{2,1,0:T(8,128)S(1)}, f32[3,64,512]{2,1,0:T(8,128)S(1)}, u32[]{:S(2)}, u32[]{:S(2)}) %collective-permute-start.2) | collective-permute-done | bytes 393248 | tf_op jit(solution)/shard_map/ppermute | solution.py:19
  31.5 7.7 %collective-permute-done.3 = f32[3,64,512]{2,1,0:T(8,128)S(1)} collective-permute-done((f32[3,64,512]{2,1,0:T(8,128)S(1)}, f32[3,64,512]{2,1,0:T(8,128)S(1)}, u32[]{:S(2)}, u32[]{:S(2)}) %collective-permute-start.3) | collective-permute-done | bytes 393248 | tf_op jit(solution)/shard_map/ppermute | solution.py:21
  40.1 6.6 %fusion.47 = f32[12,64,512]{2,1,0:T(8,128)S(1)} fusion(f32[18,64,524]{2,1,0:T(8,128)S(1)} %select_maximum_fusion.2, f32[12,64,512]{2,1,0:T(8,128)S(1)} %fusion.23, bf16[12,64,512]{2,1,0:T(8,128)(2,1)S(1)} %copy-done.3, f32[]{:T(128)} %bitcast.14, f32[]{:T(128)} %bitcast.13, f32[]{:T(128)} %bitcast.12, f32[]{:T(128)} %bitcast.11, f32[]{:T(128)} %bitcast.10, ...), kind=kLoop, calls=%fused_computation.79 | loop fusion | flops 5898240 | bytes 13369372 | tf_op jit(solution)/shard_map/div | solution.py:91
  48.1 4.6 %collective-permute-start.5 = (f32[3,64,512]{2,1,0:T(8,128)S(1)}, f32[3,64,512]{2,1,0:T(8,128)S(1)}, u32[]{:S(2)}, u32[]{:S(2)}) collective-permute-start(f32[3,64,512]{2,1,0:T(8,128)S(1)} %get-tuple-element.10), channel_id=1, source_target_pairs={{4,0},{8,4},{12,8},{16,12},{20,16},{24,20},{28,24},{5,1},{9,5},{13... | collective-permute-start | bytes 1179656 | tf_op jit(solution)/shard_map/ppermute | solution.py:21
  52.6 7.2 %collective-permute-done.4 = f32[3,64,512]{2,1,0:T(8,128)S(1)} collective-permute-done((f32[3,64,512]{2,1,0:T(8,128)S(1)}, f32[3,64,512]{2,1,0:T(8,128)S(1)}, u32[]{:S(2)}, u32[]{:S(2)}) %collective-permute-start.4) | collective-permute-done | bytes 393248 | tf_op jit(solution)/shard_map/ppermute | solution.py:19
  59.8 9.0 %collective-permute-done.5 = f32[3,64,512]{2,1,0:T(8,128)S(1)} collective-permute-done((f32[3,64,512]{2,1,0:T(8,128)S(1)}, f32[3,64,512]{2,1,0:T(8,128)S(1)}, u32[]{:S(2)}, u32[]{:S(2)}) %collective-permute-start.5) | collective-permute-done | bytes 393248 | tf_op jit(solution)/shard_map/ppermute | solution.py:21
  69.7 6.7 %fusion.40 = f32[12,64,512]{2,1,0:T(8,128)S(1)} fusion(f32[18,64,524]{2,1,0:T(8,128)S(1)} %select_maximum_fusion, f32[12,64,512]{2,1,0:T(8,128)S(1)} %fusion.47, f32[]{:T(128)} %bitcast.14, f32[]{:T(128)} %bitcast.13, f32[]{:T(128)} %bitcast.12, f32[]{:T(128)} %bitcast.11, f32[]{:T(128)} %bitcast.10, f32[]{:T(128)} %bitcast.9, f32[]{:T(128)} %bitcast.1), kind=kLoop, calls=%fused_computation.66 | loop fusion | flops 5111808 | bytes 12582940 | tf_op jit(solution)/shard_map/add | solution.py:56
  78.8 3.4 %collective-permute-start.7 = (f32[12,3,512]{2,1,0:T(4,128)S(1)}, f32[12,3,512]{2,1,0:T(4,128)S(1)}, u32[]{:S(2)}, u32[]{:S(2)}) collective-permute-start(f32[12,3,512]{2,1,0:T(4,128)S(1)} %get-tuple-element.8), channel_id=1, source_target_pairs={{0,1},{1,2},{2,3},{4,5},{5,6},{6,7},{8,9},{9,10},{10,11},{12,13},{... | collective-permute-start | bytes 221192 | tf_op jit(solution)/shard_map/ppermute | solution.py:19
  83.6 8.4 %fusion.56 = f32[12,64,512]{2,1,0:T(8,128)S(1)} fusion(f32[12,64,512]{2,1,0:T(8,128)S(1)} %copy-done.2, f32[12,64,512]{2,1,0:T(8,128)S(1)} %fusion.40, f32[12,3,512]{2,1,0:T(4,128)S(1)} %collective-permute-done.7, f32[12,3,512]{2,1,0:T(4,128)S(1)} %collective-permute-done.6, f32[512,512]{1,0:T(8,128)S(1)} %copy-done, f32[]{:T(128)} %bitcast.8, f32[]{:T(128)} %bitcast.7, ...), kind=kOutput, calls=%fused_computation.95 | convolution fusion | flops 2423783424 | bytes 5914652 | tf_op jit(solution)/shard_map/dot_general | solution.py:30
  92.1 3.7 %copy.10 = f32[12,64,512]{1,0,2:T(8,128)} copy(f32[12,64,512]{2,1,0:T(8,128)S(1)} %fusion.56) | data formatting | bytes 3145728 | tf_op jit(solution)/shard_map/mul | solution.py:95
  95.8 6.8 %reshape.16 = f32[8,1,49152]{2,1,0:T(1,128)} reshape(f32[512,12,64]{2,1,0:T(8,128)} %bitcast.34) | data formatting | bytes 3145728
  102.6 6.5 %all-to-all-start = ((f32[8,1,49152]{2,1,0:T(1,128)}), f32[8,1,49152]{2,1,0:T(1,128)S(1)}, u32[]{:S(2)}, u32[]{:S(2)}) async-start(f32[8,1,49152]{2,1,0:T(1,128)} %reshape.16), calls=%async_computation | async-start | bytes 3145728 | tf_op jit(solution)/shard_map/all_to_all | solution.py:101
  109.8 33.9 %all-to-all-done = f32[8,1,49152]{2,1,0:T(1,128)S(1)} async-done(((f32[8,1,49152]{2,1,0:T(1,128)}), f32[8,1,49152]{2,1,0:T(1,128)S(1)}, u32[]{:S(2)}, u32[]{:S(2)}) %all-to-all-start) | async-done | bytes 1572896 | tf_op jit(solution)/shard_map/all_to_all | solution.py:101
  144.3 4.4 %reduce = f32[8,49152]{1,0:T(8,128)S(1)} reduce(f32[8,1,49152]{2,1,0:T(1,128)S(1)} %all-to-all-done, f32[]{:T(128)} %broadcast.60), dimensions={1}, to_apply=%all_to_all.26.reduce_sub_computation | reduce | bytes 3145732 | tf_op jit(solution)/shard_map/all_to_all | solution.py:101
  151.9 3.9 %copy.11 = f32[12,64,8,64]{3,1,0,2:T(8,128)S(1)} copy(f32[12,64,8,64]{1,0,3,2:T(8,128)} %bitcast.33) | data formatting | bytes 3145728 | tf_op jit(solution)/shard_map/all_to_all | solution.py:101
  167.0 41.0 %all_to_all.36 = f32[8,1,49152]{2,1,0:T(1,128)S(1)} all-to-all(f32[8,1,49152]{2,1,0:T(1,128)} %reshape.18), channel_id=1, replica_groups=mesh['scan'=8,'lat'=4] {'scan'}, dimensions={0} | all-to-all | bytes 3145728 | tf_op jit(solution)/shard_map/all_to_all | solution.py:103
  208.1 4.4 %reduce.1 = f32[8,49152]{1,0:T(8,128)S(1)} reduce(f32[8,1,49152]{2,1,0:T(1,128)S(1)} %all_to_all.36, f32[]{:T(128)} %broadcast.60), dimensions={1}, to_apply=%all_to_all.30.reduce_sub_computation | reduce | bytes 3145732 | tf_op jit(solution)/shard_map/all_to_all | solution.py:103
  215.3 5.8 %copy.12 = f32[12,64,8,64]{3,2,1,0:T(8,128)} copy(f32[12,64,8,64]{3,1,0,2:T(8,128)} %bitcast.35) | data formatting | bytes 3145728 | tf_op jit(solution)/shard_map/all_to_all | solution.py:103
  221.2 3.7 %all_to_all.33 = f32[12,64,512]{2,1,0:T(8,128)} reshape(f32[12,64,8,64]{3,2,1,0:T(8,128)} %copy.12) | data formatting | bytes 3145728 | tf_op jit(solution)/shard_map/all_to_all | solution.py:103
  (47 shorter events, 31.4 us)
Async XLA Ops:
  0.0 1.2 copy-start
  0.0 10.9 %copy-start.4 = (f32[7]{0:T(128)S(1)}, f32[7]{0:T(128)}, u32[]{:S(2)}) copy-start(f32[7]{0:T(128)} %param.10) | copy-start | bytes 88
  5.3 6.3 %collective-permute-start = (f32[12,3,512]{2,1,0:T(4,128)S(1)}, f32[12,3,512]{2,1,0:T(4,128)S(1)}, u32[]{:S(2)}, u32[]{:S(2)}) collective-permute-start(f32[12,3,512]{2,1,0:T(4,128)S(1)} %get-tuple-element.13), channel_id=1, source_target_pairs={{0,1},{1,2},{2,3},{4,5},{5,6},{6,7},{8,9},{9,10},{10,11},{12,13},{... | collective-permute-start | bytes 221192 | tf_op jit(solution)/shard_map/ppermute | solution.py:19
  9.0 5.9 %collective-permute-start.1 = (f32[12,3,512]{2,1,0:T(4,128)S(1)}, f32[12,3,512]{2,1,0:T(4,128)S(1)}, u32[]{:S(2)}, u32[]{:S(2)}) collective-permute-start(f32[12,3,512]{2,1,0:T(4,128)S(1)} %get-tuple-element.14), channel_id=1, source_target_pairs={{1,0},{2,1},{3,2},{5,4},{6,5},{7,6},{9,8},{10,9},{11,10},{13,12},{... | collective-permute-start | bytes 221192 | tf_op jit(solution)/shard_map/ppermute | solution.py:21
  21.0 5.4 %copy-start.5 = (f32[7]{0:T(128)S(1)}, f32[7]{0:T(128)}, u32[]{:S(2)}) copy-start(f32[7]{0:T(128)} %param.9) | copy-start | bytes 88
  21.1 10.5 %collective-permute-start.2 = (f32[3,64,512]{2,1,0:T(8,128)S(1)}, f32[3,64,512]{2,1,0:T(8,128)S(1)}, u32[]{:S(2)}, u32[]{:S(2)}) collective-permute-start(f32[3,64,512]{2,1,0:T(8,128)S(1)} %get-tuple-element.11), channel_id=1, source_target_pairs={{0,4},{4,8},{8,12},{12,16},{16,20},{20,24},{24,28},{1,5},{5,9},{9,... | collective-permute-start | bytes 1179656 | tf_op jit(solution)/shard_map/ppermute | solution.py:19
  22.4 16.9 %collective-permute-start.3 = (f32[3,64,512]{2,1,0:T(8,128)S(1)}, f32[3,64,512]{2,1,0:T(8,128)S(1)}, u32[]{:S(2)}, u32[]{:S(2)}) collective-permute-start(f32[3,64,512]{2,1,0:T(8,128)S(1)} %get-tuple-element.12), channel_id=1, source_target_pairs={{4,0},{8,4},{12,8},{16,12},{20,16},{24,20},{28,24},{5,1},{9,5},{13... | collective-permute-start | bytes 1179656 | tf_op jit(solution)/shard_map/ppermute | solution.py:21
  27.1 13.0 %copy-start.3 = (bf16[12,64,512]{2,1,0:T(8,128)(2,1)S(1)}, bf16[12,64,512]{2,1,0:T(8,128)(2,1)}, u32[]{:S(2)}) copy-start(bf16[12,64,512]{2,1,0:T(8,128)(2,1)} %param.6) | copy-start | bytes 2359300
  46.8 13.1 %collective-permute-start.4 = (f32[3,64,512]{2,1,0:T(8,128)S(1)}, f32[3,64,512]{2,1,0:T(8,128)S(1)}, u32[]{:S(2)}, u32[]{:S(2)}) collective-permute-start(f32[3,64,512]{2,1,0:T(8,128)S(1)} %get-tuple-element.9), channel_id=1, source_target_pairs={{0,4},{4,8},{8,12},{12,16},{16,20},{20,24},{24,28},{1,5},{5,9},{9,... | collective-permute-start | bytes 1179656 | tf_op jit(solution)/shard_map/ppermute | solution.py:19
  48.1 20.8 %collective-permute-start.5 = (f32[3,64,512]{2,1,0:T(8,128)S(1)}, f32[3,64,512]{2,1,0:T(8,128)S(1)}, u32[]{:S(2)}, u32[]{:S(2)}) collective-permute-start(f32[3,64,512]{2,1,0:T(8,128)S(1)} %get-tuple-element.10), channel_id=1, source_target_pairs={{4,0},{8,4},{12,8},{16,12},{20,16},{24,20},{28,24},{5,1},{9,5},{13... | collective-permute-start | bytes 1179656 | tf_op jit(solution)/shard_map/ppermute | solution.py:21
  69.7 13.9 %copy-start.2 = (f32[12,64,512]{2,1,0:T(8,128)S(1)}, f32[12,64,512]{2,1,0:T(8,128)}, u32[]{:S(2)}) copy-start(f32[12,64,512]{2,1,0:T(8,128)} %param.7) | copy-start | bytes 4718596
  76.4 5.9 %collective-permute-start.6 = (f32[12,3,512]{2,1,0:T(4,128)S(1)}, f32[12,3,512]{2,1,0:T(4,128)S(1)}, u32[]{:S(2)}, u32[]{:S(2)}) collective-permute-start(f32[12,3,512]{2,1,0:T(4,128)S(1)} %get-tuple-element.7), channel_id=1, source_target_pairs={{1,0},{2,1},{3,2},{5,4},{6,5},{7,6},{9,8},{10,9},{11,10},{13,12},{... | collective-permute-start | bytes 221192 | tf_op jit(solution)/shard_map/ppermute | solution.py:21
  78.8 4.8 %collective-permute-start.7 = (f32[12,3,512]{2,1,0:T(4,128)S(1)}, f32[12,3,512]{2,1,0:T(4,128)S(1)}, u32[]{:S(2)}, u32[]{:S(2)}) collective-permute-start(f32[12,3,512]{2,1,0:T(4,128)S(1)} %get-tuple-element.8), channel_id=1, source_target_pairs={{0,1},{1,2},{2,3},{4,5},{5,6},{6,7},{8,9},{9,10},{10,11},{12,13},{... | collective-permute-start | bytes 221192 | tf_op jit(solution)/shard_map/ppermute | solution.py:19
  102.6 41.2 %all-to-all-start = ((f32[8,1,49152]{2,1,0:T(1,128)}), f32[8,1,49152]{2,1,0:T(1,128)S(1)}, u32[]{:S(2)}, u32[]{:S(2)}) async-start(f32[8,1,49152]{2,1,0:T(1,128)} %reshape.16), calls=%async_computation | async-start | bytes 3145728 | tf_op jit(solution)/shard_map/all_to_all | solution.py:101
  215.3 9.6 %copy-start.1 = (f32[512,512]{1,0:T(8,128)S(1)}, f32[512,512]{1,0:T(8,128)}, u32[]{:S(2)}) copy-start(f32[512,512]{1,0:T(8,128)} %param.8) | copy-start | bytes 3145732
where the time goes:
time: 229 us; the launch traced here: 225 us
  waiting for transfers between devices  67.1 us (29%)
  blocking collectives  41 us (18%)
  local copies, waits for them, and re-layouts  38.7 us (17%)
  other arithmetic  36.4 us (16%)
  starting transfers between devices  29 us (13%)
  matrix products  12.5 us (5%)
    all_to_all x1, blocking collectives, on_device(): lax.all_to_all(settled, 'scan', split_axis=0, concat_axis=2, tiled=True)  41 us
    all_to_all x1, waiting for transfers between devices, on_device(): lax.all_to_all(updated, 'scan', split_axis=2, concat_axis=0, tiled=True)  33.9 us
    ppermute x4, waiting for transfers between devices, padded_2(): lax.ppermute(head, axis, [((i + 1) % count, i) for i in range(ends)])  20.2 us
    unnamed x16, local copies, waits for them, and re-layouts  17.4 us
    ppermute x4, waiting for transfers between devices, padded_2(): lax.ppermute(tail, axis, [(i, (i + 1) % count) for i in range(ends)])  12.9 us
    ppermute x4, starting transfers between devices, padded_2(): lax.ppermute(head, axis, [((i + 1) % count, i) for i in range(ends)])  12.9 us
    dot_general x2, matrix products, column_mix(): jnp.dot(flat, matrix, precision=lax.Precision.HIGHEST, preferred_element_...  12.5 us
    ppermute x4, starting transfers between devices, padded_2(): lax.ppermute(tail, axis, [(i, (i + 1) % count) for i in range(ends)])  9.62 us
  transfers between devices with their start and end apart: 9, of which 8 were waited for; matrix products, arithmetic and copies ran while one was open for 1% of the time, Pallas kernels for 0%

commit v1 on v0

v1 whole, which is shorter than its diff:
```python
import functools

import jax
import jax.numpy as jnp
from jax import lax
from jax.experimental import pallas as pl
from jax.experimental.pallas import tpu as pltpu
from jax.sharding import PartitionSpec as P

PLANE_HALF = 3
ROW_HALF = 3
SKEW = 2
LANES = 128
EDGE = 8
F32 = jnp.float32
BF16 = jnp.bfloat16
VMEM = pl.BlockSpec(memory_space=pltpu.VMEM)
SMEM = pl.BlockSpec(memory_space=pltpu.SMEM)
LIMIT = 48 * 1024 * 1024


def run(body, outs, ins, operands, scratch=(), aliases=None, cost=None):
    return pl.pallas_call(
        body,
        out_shape=outs,
        in_specs=ins,
        out_specs=jax.tree.map(lambda _: VMEM, outs),
        scratch_shapes=list(scratch),
        input_output_aliases=aliases or {},
        compiler_params=pltpu.CompilerParams(vmem_limit_bytes=LIMIT),
        cost_estimate=cost,
    )(*operands)


def halves(x):
    high = x.astype(BF16)
    return high, (x - high.astype(F32)).astype(BF16)


def product(x, high_w, low_w, dims):
    high, low = halves(x)
    dot = functools.partial(
        lax.dot_general, dimension_numbers=(dims, ((), ())), preferred_element_type=F32
    )
    return dot(high, high_w) + (dot(high, low_w) + dot(low, high_w))


def fill_rows(pad, top, mid, bottom):
    planes, rows, cols = mid.shape
    pad[:, 0:EDGE, :] = jnp.zeros((planes, EDGE, cols), F32)
    pad[:, EDGE + rows :, :] = jnp.zeros((planes, EDGE, cols), F32)
    pad[:, EDGE - ROW_HALF : EDGE, :] = top[...]
    pad[:, EDGE : EDGE + rows, :] = mid[...]
    pad[:, EDGE + rows : EDGE + rows + ROW_HALF, :] = bottom[...]


def row_sum(pad, plane, rows, taps, direction):
    total = None
    for k in range(2 * ROW_HALF + 1):
        tap = taps[k] if direction > 0 else taps[2 * ROW_HALF - k]
        term = tap * pad[plane, pl.ds(EDGE - ROW_HALF + k, rows), :]
        total = term if total is None else total + term
    return total


def mix_body(est, top, bottom, weights, taps, blur, low3, high3, pad, mixed):
    planes, rows, cols = est.shape
    fill_rows(pad, top, est, bottom)
    high_w, low_w = halves(weights[...])
    group = 4 if planes % 4 == 0 else 1

    def mix(g, _):
        x = pad[pl.ds(g * group, group)].reshape(group * (rows + 2 * EDGE), cols)
        y = product(x, high_w, low_w, ((1,), (0,)))
        mixed[pl.ds(g * group, group)] = y.reshape(group, rows + 2 * EDGE, cols)
        return 0

    lax.fori_loop(0, planes // group, mix, 0)

    def blur_rows(p, _):
        blur[p] = row_sum(mixed, p, rows, taps, 1)
        return 0

    lax.fori_loop(0, planes, blur_rows, 0)
    low3[...] = blur[0:PLANE_HALF]
    high3[...] = blur[planes - PLANE_HALF : planes]


def skewed(x, place):
    rows, cols = x.shape
    wide = jnp.concatenate([x, jnp.zeros((rows, LANES), F32)], axis=1)
    return pltpu.roll(wide, SKEW * place, 1) if place else wide


def unskewed(x, place):
    width = x.shape[1]
    moved = pltpu.roll(x, (width - SKEW * place) % width, 1) if place else x
    return moved[:, : width - LANES]


def plane_sum(field, index, row, taps, direction):
    total = None
    for k in range(2 * PLANE_HALF + 1):
        tap = taps[k] if direction > 0 else taps[2 * PLANE_HALF - k]
        term = tap * field[index + k, pl.ds(row, 8), :]
        total = term if total is None else total + term
    return total


def quotient_body(blur, left, right, observed, taps, ratio, low3, high3, skew, wide):
    planes, rows, cols = blur.shape
    for l in range(PLANE_HALF):
        skew[l] = skewed(left[l], l)
        skew[planes + PLANE_HALF + l] = skewed(right[l], planes + PLANE_HALF + l)
    for l in range(planes):
        skew[PLANE_HALF + l] = skewed(blur[l], PLANE_HALF + l)
        wide[l] = skewed(observed[l].astype(F32), PLANE_HALF + l)

    def plane(l, _):
        place = SKEW * (l + PLANE_HALF)
        lane = lax.broadcasted_iota(jnp.int32, (8, cols + LANES), 1)
        inside = (lane >= place) & (lane < place + cols)

        def tile(t, _):
            row = pl.multiple_of(t * 8, 8)
            blurred = plane_sum(skew, l, row, taps, 1)
            seen = wide[l, pl.ds(row, 8), :]
            ratio[l, pl.ds(row, 8), :] = jnp.where(
                inside, seen / jnp.where(inside, blurred, 1.0), 0.0
            )
            return 0

        return lax.fori_loop(0, rows // 8, tile, 0, unroll=2)

    lax.fori_loop(0, planes, plane, 0)
    for l in range(PLANE_HALF):
        low3[l] = unskewed(ratio[l], PLANE_HALF + l)
        high3[l] = unskewed(ratio[planes - PLANE_HALF + l], planes + l)


def back_body(ratio, left, right, taps, back, top, bottom, skew, wide):
    planes, rows, width = ratio.shape
    for l in range(PLANE_HALF):
        skew[l] = skewed(left[l], l)
        skew[planes + PLANE_HALF + l] = skewed(right[l], planes + PLANE_HALF + l)
    skew[PLANE_HALF : PLANE_HALF + planes] = ratio[...]

    def plane(l, _):
        def tile(t, _):
            row = pl.multiple_of(t * 8, 8)
            wide[l, pl.ds(row, 8), :] = plane_sum(skew, l, row, taps, -1)
            return 0

        return lax.fori_loop(0, rows // 8, tile, 0, unroll=2)

    lax.fori_loop(0, planes, plane, 0)
    for l in range(planes):
        back[l] = unskewed(wide[l], PLANE_HALF + l)
    top[...] = back[:, 0:ROW_HALF, :]
    bottom[...] = back[:, rows - ROW_HALF : rows, :]


def update_body(back, top, bottom, weights, taps, est, turn, out, pad, rows_out):
    planes, rows, cols = est.shape
    fill_rows(pad, top, back, bottom)
    high_w, low_w = halves(weights[...])

    def sum_rows(p, _):
        rows_out[p] = row_sum(pad, p, rows, taps, -1)
        return 0

    lax.fori_loop(0, planes, sum_rows, 0)
    group = 4 if planes % 4 == 0 else 1

    def mix(g, _):
        x = rows_out[pl.ds(g * group, group)].reshape(group * rows, cols)
        y = product(x, high_w, low_w, ((1,), (1,)))
        rows_out[pl.ds(g * group, group)] = y.reshape(group, rows, cols)
        return 0

    lax.fori_loop(0, planes // group, mix, 0)

    def rotate(t, _):
        row = pl.multiple_of(t * 8, 8)
        for c in range(0, cols, 2 * LANES):
            tile = (pl.ds(row, 8), pl.ds(c, 2 * LANES))
            field = [rows_out[(p, *tile)] * est[(p, *tile)] for p in range(planes)]
            bits = jnp.broadcast_to(turn[:, c : c + 2 * LANES], (8, 2 * LANES))
            for bit in range((planes - 1).bit_length()):
                chosen = (bits >> bit & 1) == 1
                field = [
                    jnp.where(chosen, field[(q - (1 << bit)) % planes], field[q])
                    for q in range(planes)
                ]
            for q in range(planes):
                out[(q, *tile)] = field[q]
        return 0

    lax.fori_loop(0, rows // 8, rotate, 0)


class Packing:
    def __init__(self, count, planes, rows, cols):
        self.count, self.planes, self.rows, self.cols = count, planes, rows, cols
        share = max(cols // count, 1)
        self.parts = 2 if rows % 16 == 0 else 1
        self.messages = []
        for d in range(1, count):
            room = share * 5 // 4
            if d == count - 1:
                room = share * 3 // 2
            if d == 1:
                room = share * 9 // 4
            pieces = -(-room // LANES)
            width = min(-(-room // (8 * pieces)) * 8, LANES)
            self.messages.append((d, pieces, width))

    def segments(self, pieces):
        return [
            (m, h, q)
            for m in range(pieces)
            for h in range(self.parts)
            for q in range(self.planes)
        ]

    def shape(self, pieces, width):
        total = pieces * self.parts * self.planes * width
        return (self.rows // self.parts, -(-total // LANES) * LANES)


def lane_of(shape):
    return lax.broadcasted_iota(jnp.int32, shape, 1)


def pack_body(packing, edges, turned, field, *outs):
    plan = packing
    part_rows = plan.rows // plan.parts
    last = plan.cols // LANES - 1
    step = turned[0]

    def tiles(t, _):
        lane = lane_of((8, LANES))
        for (d, pieces, width), out in zip(plan.messages, outs):
            done = {}
            for k, (m, h, q) in enumerate(plan.segments(pieces)):
                low = edges[d * plan.planes + q] + (step * pieces + m) * width
                tile = jnp.minimum(low // LANES, last)
                row = pl.multiple_of(h * part_rows + t * 8, 8)
                first = field[
                    q, pl.ds(row, 8), pl.ds(pl.multiple_of(tile * LANES, LANES), LANES)
                ]
                second = field[
                    q,
                    pl.ds(row, 8),
                    pl.ds(pl.multiple_of(jnp.minimum(tile + 1, last) * LANES, LANES), LANES),
                ]
                begin = k * width
                offset = begin % LANES
                window = jnp.where(lane >= low % LANES, first, second)
                window = pltpu.roll(window, (offset - low) % LANES, 1)
                target = begin // LANES
                done[target] = (
                    window
                    if offset == 0
                    else jnp.where(lane >= offset, window, done[target])
                )
                if offset + width > LANES:
                    done[target + 1] = window
                for full in [x for x in done if (x + 1) * LANES <= begin + width]:
                    out[pl.ds(pl.multiple_of(t * 8, 8), 8), full * LANES : (full + 1) * LANES] = (
                        done.pop(full)
                    )
            for rest in list(done):
                out[pl.ds(pl.multiple_of(t * 8, 8), 8), rest * LANES : (rest + 1) * LANES] = (
                    done.pop(rest)
                )
        return 0

    lax.fori_loop(0, part_rows // 8, tiles, 0)


def unpack_body(packing, first_round, edges, turned, base, *refs):
    plan = packing
    ins, out = refs[:-1], refs[-1]
    part_rows = plan.rows // plan.parts
    count = plan.cols // LANES
    step = turned[0]

    def tiles(t, _):
        lane = lane_of((8, LANES))
        for h in range(plan.parts):
            for q in range(plan.planes):
                rows = pl.ds(pl.multiple_of(h * part_rows + t * 8, 8), 8)
                found = []
                for c in range(count):
                    x = base[q, rows, c * LANES : (c + 1) * LANES]
                    if first_round:
                        x = jnp.where(lane + c * LANES < edges[plan.planes + q], x, 0.0)
                    found.append(x)
                for (d, pieces, width), message in zip(plan.messages, ins):
                    for m in range(pieces):
                        k = plan.segments(pieces).index((m, h, q))
                        low = edges[d * plan.planes + q] + (step * pieces + m) * width
                        high = jnp.minimum(edges[(d + 1) * plan.planes + q], low + width)
                        begin = k * width
                        offset = begin % LANES
                        target = begin // LANES
                        here = pl.ds(pl.multiple_of(t * 8, 8), 8)
                        window = message[here, target * LANES : (target + 1) * LANES]
                        if offset + width > LANES:
                            window = jnp.where(
                                lane >= offset,
                                window,
                                message[here, (target + 1) * LANES : (target + 2) * LANES],
                            )
                        window = pltpu.roll(window, (low - offset) % LANES, 1)
                        for c in range(count):
                            inside = (lane >= low - c * LANES) & (lane < high - c * LANES)
                            found[c] = jnp.where(inside, window, found[c])
                for c in range(count):
                    out[q, rows, c * LANES : (c + 1) * LANES] = found[c]
        return 0

    lax.fori_loop(0, part_rows // 8, tiles, 0)


def to_next(x, axis):
    count = lax.axis_size(axis)
    return lax.ppermute(x, axis, [(i, i + 1) for i in range(count - 1)])


def to_last(x, axis):
    count = lax.axis_size(axis)
    return lax.ppermute(x, axis, [(i + 1, i) for i in range(count - 1)])


def like(*shape):
    return jax.ShapeDtypeStruct(shape, F32)


def on_device(observed, estimate, column_weights, plane_taps, row_taps, shear_planes):
    planes, rows, cols = estimate.shape
    count = lax.axis_size("scan")
    padded = pltpu.VMEM((planes, rows + 2 * EDGE, cols), F32)
    width = cols + LANES
    tall = pltpu.VMEM((planes + 2 * PLANE_HALF, rows, width), F32)
    wide = pltpu.VMEM((planes, rows, width), F32)

    top = to_next(estimate[:, rows - ROW_HALF :, :], "lat")
    bottom = to_last(estimate[:, :ROW_HALF, :], "lat")
    levels = jnp.arange((count + 1) * planes, dtype=jnp.int32) - planes
    edges = jnp.sum(shear_planes[None, :] <= levels[:, None], axis=1, dtype=jnp.int32)
    turn = (shear_planes % planes)[None, :]

    blur, low3, high3 = run(
        mix_body,
        (like(planes, rows, cols), like(PLANE_HALF, rows, cols), like(PLANE_HALF, rows, cols)),
        [VMEM, VMEM, VMEM, VMEM, SMEM],
        (estimate, top, bottom, column_weights, row_taps),
        [padded, padded],
    )
    left, right = to_next(high3, "scan"), to_last(low3, "scan")
    ratio, low3, high3 = run(
        quotient_body,
        (like(planes, rows, width), like(PLANE_HALF, rows, cols), like(PLANE_HALF, rows, cols)),
        [VMEM, VMEM, VMEM, VMEM, SMEM],
        (blur, left, right, observed, plane_taps),
        [tall, wide],
    )
    left, right = to_next(high3, "scan"), to_last(low3, "scan")
    back, top, bottom = run(
        back_body,
        (like(planes, rows, cols), like(planes, ROW_HALF, cols), like(planes, ROW_HALF, cols)),
        [VMEM, VMEM, VMEM, SMEM],
        (ratio, left, right, plane_taps),
        [tall, wide],
    )
    above, below = to_next(bottom, "lat"), to_last(top, "lat")
    turned = run(
        update_body,
        like(planes, rows, cols),
        [VMEM, VMEM, VMEM, VMEM, SMEM, VMEM, VMEM],
        (back, above, below, column_weights, row_taps, estimate, turn),
        [padded, pltpu.VMEM((planes, rows, cols), F32)],
    )

    plan = Packing(count, planes, rows, cols)

    def exchange(step, base, first_round):
        packed = run(
            functools.partial(pack_body, plan),
            tuple(like(*plan.shape(m, w)) for _, m, w in plan.messages),
            [SMEM, SMEM, VMEM],
            (edges, step, turned),
        )
        moved = [
            lax.ppermute(x, "scan", [(i, i + d) for i in range(count - d)])
            for (d, _, _), x in zip(plan.messages, packed)
        ]
        return run(
            functools.partial(unpack_body, plan, first_round),
            like(planes, rows, cols),
            [SMEM, SMEM, VMEM] + [VMEM] * len(moved),
            (edges, step, base, *moved),
        )

    table = edges.reshape(count + 1, planes)
    rooms = jnp.array([m * w for _, m, w in plan.messages], jnp.int32)
    widest = jnp.max(table[2:] - table[1:-1], axis=1)
    rounds = jnp.max((widest + rooms - 1) // rooms)
    first = exchange(jnp.zeros((1,), jnp.int32), turned, True)

    def more(state):
        return state[0] < rounds

    def again(state):
        return state[0] + 1, exchange(state[0][None], state[1], False)

    return lax.while_loop(more, again, (jnp.int32(1), first))[1]


def solution(mesh):
    placed = (P("scan", "lat", None), P("scan", "lat", None), P(), P(), P(), P())
    return jax.shard_map(
        on_device, mesh=mesh, in_specs=placed, out_specs=P("scan", "lat", None), check_vma=False
    )
```

time: 229 us -> 148 us (0.65); the launches traced: 225 us -> 147 us
  blocking collectives: 41 us -> 0 us
  other arithmetic: 36.4 us -> 1.11 us
  Pallas kernels: 0 us -> 34.6 us
  local copies, waits for them, and re-layouts: 38.7 us -> 4.47 us
  matrix products: 12.5 us -> 0 us
  waiting for transfers between devices: 67.1 us -> 77.5 us
    ppermute x8 -> x15, waiting for transfers between devices: 33.2 us -> 77.5 us  [the longest x7 40.3 us: exchange(): lax.ppermute(x, 'scan', [(i, i + d) for i in range(count - d)])]
    all_to_all x1 -> x0, blocking collectives: 41 us -> none  [on_device(): lax.all_to_all(settled, 'scan', split_axis=0, concat_axis=2, tiled=True)]
    pallas_call x0 -> x6, Pallas kernels: none -> 34.6 us  [run(): pl.pallas_call(body, out_shape=outs, in_specs=ins, out_specs=jax.tree.map...]
    all_to_all x1 -> x0, waiting for transfers between devices: 33.9 us -> none  [on_device(): lax.all_to_all(updated, 'scan', split_axis=2, concat_axis=0, tiled=True)]
    unnamed x16 -> x20, local copies, waits for them, and re-layouts: 17.4 us -> 3.32 us
    all_to_all x4 -> x0, local copies, waits for them, and re-layouts: 14 us -> none  [the longest x2 9.58 us: on_device(): lax.all_to_all(settled, 'scan', split_axis=0, concat_axis=2, tiled=True)]
    add x2 -> x0, other arithmetic: 12.7 us -> none  [the longest x1 6.68 us: plane_pass(): summed + kernel[offset + halfwidth] * widened[begin:begin + plane_count,...]
    dot_general x2 -> x0, matrix products: 12.5 us -> none  [column_mix(): jnp.dot(flat, matrix, precision=lax.Precision.HIGHEST, preferred_element_...]
  transfers between devices with their start and end apart: 9 -> 15, of which waited for: 8 -> 8; matrix products, arithmetic and copies ran while one was open for 1% -> 1% of each run, Pallas kernels for 0% -> 0%
where the time goes in v1:
time: 148 us; the launch traced here: 147 us
  waiting for transfers between devices  77.5 us (52%)
  Pallas kernels  34.6 us (23%)
  starting transfers between devices  28.3 us (19%)
  local copies, waits for them, and re-layouts  4.47 us (3%)
    ppermute x7, waiting for transfers between devices, exchange(): lax.ppermute(x, 'scan', [(i, i + d) for i in range(count - d)])  40.3 us
    pallas_call x6, Pallas kernels, run(): pl.pallas_call(body, out_shape=outs, in_specs=ins, out_specs=jax.tree.map...  34.6 us
    ppermute x4, waiting for transfers between devices, to_last(): return lax.ppermute(x, axis, [(i + 1, i) for i in range(count - 1)])  31.3 us
    ppermute x4, starting transfers between devices, to_last(): return lax.ppermute(x, axis, [(i + 1, i) for i in range(count - 1)])  11 us
    ppermute x7, starting transfers between devices, exchange(): lax.ppermute(x, 'scan', [(i, i + d) for i in range(count - d)])  9.04 us
    ppermute x4, starting transfers between devices, to_next(): return lax.ppermute(x, axis, [(i, i + 1) for i in range(count - 1)])  8.32 us
    ppermute x4, waiting for transfers between devices, to_next(): return lax.ppermute(x, axis, [(i, i + 1) for i in range(count - 1)])  5.92 us
    unnamed x20, local copies, waits for them, and re-layouts  3.32 us
  transfers between devices with their start and end apart: 15, of which 8 were waited for; matrix products, arithmetic and copies ran while one was open for 1% of the time, Pallas kernels for 0%

profile of v1, /device:TPU:29, one launch (start us, length us, event | category | flops | bytes accessed | tf_op | source)
XLA Modules:
  0.0 147.1 jit_solution(8016233145977104892)
XLA Ops:
  1.1 3.7 %collective-permute-start.7 = (f32[12,3,512]{2,1,0:T(4,128)S(1)}, f32[12,3,512]{2,1,0:T(4,128)S(1)}, u32[]{:S(2)}, u32[]{:S(2)}) collective-permute-start(f32[12,3,512]{2,1,0:T(4,128)S(1)} %get-tuple-element.84), channel_id=1, source_target_pairs={{0,1},{1,2},{2,3},{4,5},{5,6},{6,7},{8,9},{9,10},{10,11},{12,13},{... | collective-permute-start | bytes 221192 | tf_op jit(solution)/shard_map/ppermute | solution.py:329
  4.8 1.9 %collective-permute-start.8 = (f32[12,3,512]{2,1,0:T(4,128)S(1)}, f32[12,3,512]{2,1,0:T(4,128)S(1)}, u32[]{:S(2)}, u32[]{:S(2)}) collective-permute-start(f32[12,3,512]{2,1,0:T(4,128)S(1)} %get-tuple-element.83), channel_id=1, source_target_pairs={{1,0},{2,1},{3,2},{5,4},{6,5},{7,6},{9,8},{10,9},{11,10},{13,12},{... | collective-permute-start | bytes 221192 | tf_op jit(solution)/shard_map/ppermute | solution.py:334
  6.7 4.0 %collective-permute-done.8.bottom = f32[12,3,512]{2,1,0:T(4,128)S(1)} collective-permute-done((f32[12,3,512]{2,1,0:T(4,128)S(1)}, f32[12,3,512]{2,1,0:T(4,128)S(1)}, u32[]{:S(2)}, u32[]{:S(2)}) %collective-permute-start.8) | collective-permute-done | bytes 73760 | tf_op jit(solution)/shard_map/ppermute | solution.py:334
  10.7 1.4 copy-done
  14.0 4.8 %shard_map.73 = (f32[12,64,512]{2,1,0:T(8,128)S(1)}, f32[3,64,512]{2,1,0:T(8,128)S(1)}, f32[3,64,512]{2,1,0:T(8,128)S(1)}) custom-call(f32[12,64,512]{2,1,0:T(8,128)S(1)} %copy-done, f32[12,3,512]{2,1,0:T(4,128)S(1)} %collective-permute-done.7.top, f32[12,3,512]{2,1,0:T(4,128)S(1)} %collective-permute-done.8.bottom, f32[512,512]{1,0:T(8,128)S(1)} %copy-done.2, ...), custom_call_target="tpu_custom_call" | custom-call | tf_op jit(solution)/shard_map/pallas_call | solution.py:23
  18.8 2.2 %collective-permute-start.10 = (f32[3,64,512]{2,1,0:T(8,128)S(1)}, f32[3,64,512]{2,1,0:T(8,128)S(1)}, u32[]{:S(2)}, u32[]{:S(2)}) collective-permute-start(f32[3,64,512]{2,1,0:T(8,128)S(1)} %get-tuple-element.58), channel_id=1, source_target_pairs={{4,0},{8,4},{12,8},{16,12},{20,16},{24,20},{28,24},{5,1},{9,5},{13... | collective-permute-start | bytes 1179656 | tf_op jit(solution)/shard_map/ppermute | solution.py:334
  22.3 13.8 %collective-permute-done.10.right = f32[3,64,512]{2,1,0:T(8,128)S(1)} collective-permute-done((f32[3,64,512]{2,1,0:T(8,128)S(1)}, f32[3,64,512]{2,1,0:T(8,128)S(1)}, u32[]{:S(2)}, u32[]{:S(2)}) %collective-permute-start.10) | collective-permute-done | bytes 393248 | tf_op jit(solution)/shard_map/ppermute | solution.py:334
  36.1 3.6 %shard_map.74 = (f32[12,64,640]{2,1,0:T(8,128)S(1)}, f32[3,64,512]{2,1,0:T(8,128)S(1)}, f32[3,64,512]{2,1,0:T(8,128)S(1)}) custom-call(f32[12,64,512]{2,1,0:T(8,128)S(1)} %get-tuple-element.56.blur, f32[3,64,512]{2,1,0:T(8,128)S(1)} %collective-permute-done.9.left, f32[3,64,512]{2,1,0:T(8,128)S(1)} %collective-permute-done.10.right, ...), custom_call_target="tpu_custom_call" | custom-call | tf_op jit(solution)/shard_map/pallas_call | solution.py:23
  39.7 1.4 collective-permute-start.11
  41.1 4.5 %collective-permute-start.12 = (f32[3,64,512]{2,1,0:T(8,128)S(1)}, f32[3,64,512]{2,1,0:T(8,128)S(1)}, u32[]{:S(2)}, u32[]{:S(2)}) collective-permute-start(f32[3,64,512]{2,1,0:T(8,128)S(1)} %get-tuple-element.61), channel_id=1, source_target_pairs={{4,0},{8,4},{12,8},{16,12},{20,16},{24,20},{28,24},{5,1},{9,5},{13... | collective-permute-start | bytes 1179656 | tf_op jit(solution)/shard_map/ppermute | solution.py:334
  45.7 5.9 %collective-permute-done.11.left = f32[3,64,512]{2,1,0:T(8,128)S(1)} collective-permute-done((f32[3,64,512]{2,1,0:T(8,128)S(1)}, f32[3,64,512]{2,1,0:T(8,128)S(1)}, u32[]{:S(2)}, u32[]{:S(2)}) %collective-permute-start.11) | collective-permute-done | bytes 393248 | tf_op jit(solution)/shard_map/ppermute | solution.py:329
  51.6 10.2 %collective-permute-done.12.right = f32[3,64,512]{2,1,0:T(8,128)S(1)} collective-permute-done((f32[3,64,512]{2,1,0:T(8,128)S(1)}, f32[3,64,512]{2,1,0:T(8,128)S(1)}, u32[]{:S(2)}, u32[]{:S(2)}) %collective-permute-start.12) | collective-permute-done | bytes 393248 | tf_op jit(solution)/shard_map/ppermute | solution.py:334
  61.8 2.9 %shard_map.75 = (f32[12,64,512]{2,1,0:T(8,128)S(1)}, f32[12,3,512]{2,1,0:T(4,128)S(1)}, f32[12,3,512]{2,1,0:T(4,128)S(1)}) custom-call(f32[12,64,640]{2,1,0:T(8,128)S(1)} %get-tuple-element.59.ratio, f32[3,64,512]{2,1,0:T(8,128)S(1)} %collective-permute-done.11.left, f32[3,64,512]{2,1,0:T(8,128)S(1)} %collective-permute-done.12.right, f32[7]{0:T(128)S(1)} %copy-done.6), custom_call_target="tpu_custom_call" | custom-call | tf_op jit(solution)/shard_map/pallas_call | solution.py:23
  64.7 1.9 %collective-permute-start.13 = (f32[12,3,512]{2,1,0:T(4,128)S(1)}, f32[12,3,512]{2,1,0:T(4,128)S(1)}, u32[]{:S(2)}, u32[]{:S(2)}) collective-permute-start(f32[12,3,512]{2,1,0:T(4,128)S(1)} %get-tuple-element.63), channel_id=1, source_target_pairs={{0,1},{1,2},{2,3},{4,5},{5,6},{6,7},{8,9},{9,10},{10,11},{12,13},{... | collective-permute-start | bytes 221192 | tf_op jit(solution)/shard_map/ppermute | solution.py:329
  66.6 2.4 %collective-permute-start.14 = (f32[12,3,512]{2,1,0:T(4,128)S(1)}, f32[12,3,512]{2,1,0:T(4,128)S(1)}, u32[]{:S(2)}, u32[]{:S(2)}) collective-permute-start(f32[12,3,512]{2,1,0:T(4,128)S(1)} %get-tuple-element.64), channel_id=1, source_target_pairs={{1,0},{2,1},{3,2},{5,4},{6,5},{7,6},{9,8},{10,9},{11,10},{13,12},{... | collective-permute-start | bytes 221192 | tf_op jit(solution)/shard_map/ppermute | solution.py:334
  69.2 3.3 %collective-permute-done.14.bottom = f32[12,3,512]{2,1,0:T(4,128)S(1)} collective-permute-done((f32[12,3,512]{2,1,0:T(4,128)S(1)}, f32[12,3,512]{2,1,0:T(4,128)S(1)}, u32[]{:S(2)}, u32[]{:S(2)}) %collective-permute-start.14) | collective-permute-done | bytes 73760 | tf_op jit(solution)/shard_map/ppermute | solution.py:334
  72.5 5.0 %shard_map.76.field.base = f32[12,64,512]{2,1,0:T(8,128)S(1)} custom-call(f32[12,64,512]{2,1,0:T(8,128)S(1)} %get-tuple-element.62.back, f32[12,3,512]{2,1,0:T(4,128)S(1)} %collective-permute-done.13.top, f32[12,3,512]{2,1,0:T(4,128)S(1)} %collective-permute-done.14.bottom, f32[512,512]{1,0:T(8,128)S(1)} %copy-done.3, f32[7]{0:T(128)S(1)} %copy-done.5, ...), custom_call_target="tpu_custom_call" | custom-call | tf_op jit(solution)/shard_map/pallas_call | solution.py:23
  77.5 10.2 %shard_map.77 = (f32[32,3456]{1,0:T(8,128)S(1)}, f32[32,1920]{1,0:T(8,128)S(1)}, f32[32,1920]{1,0:T(8,128)S(1)}, f32[32,1920]{1,0:T(8,128)S(1)}, f32[32,1920]{1,...) custom-call(s32[108]{0:T(128)S(1)} %convert_reduce_fusion.edges, s32[1]{0:T(128)} %constant.30.clone.1.turned, ...), custom_call_target="tpu_custom_call" | custom-call | tf_op jit(solution)/shard_map/pallas_call | solution.py:23
  87.7 1.3 collective-permute-start.16
  89.0 1.3 collective-permute-start.17
  94.2 3.6 %collective-permute-done.16.refs_1_ = f32[32,1920]{1,0:T(8,128)S(1)} collective-permute-done((f32[32,1920]{1,0:T(8,128)S(1)}, f32[32,1920]{1,0:T(8,128)S(1)}, u32[]{:S(2)}, u32[]{:S(2)}) %collective-permute-start.16) | collective-permute-done | bytes 245792 | tf_op jit(solution)/shard_map/ppermute | solution.py:397
  99.1 9.6 %collective-permute-done.17.refs_2_ = f32[32,1920]{1,0:T(8,128)S(1)} collective-permute-done((f32[32,1920]{1,0:T(8,128)S(1)}, f32[32,1920]{1,0:T(8,128)S(1)}, u32[]{:S(2)}, u32[]{:S(2)}) %collective-permute-start.17) | collective-permute-done | bytes 245792 | tf_op jit(solution)/shard_map/ppermute | solution.py:397
  111.0 27.1 %collective-permute-done.18.refs_3_ = f32[32,1920]{1,0:T(8,128)S(1)} collective-permute-done((f32[32,1920]{1,0:T(8,128)S(1)}, f32[32,1920]{1,0:T(8,128)S(1)}, u32[]{:S(2)}, u32[]{:S(2)}) %collective-permute-start.18) | collective-permute-done | bytes 245792 | tf_op jit(solution)/shard_map/ppermute | solution.py:397
  138.2 8.1 %shard_map.78 = f32[12,64,512]{2,1,0:T(8,128)} custom-call(s32[108]{0:T(128)S(1)} %convert_reduce_fusion.edges, s32[1]{0:T(128)} %constant.30.clone.1.turned, f32[12,64,512]{2,1,0:T(8,128)} %copy-done.7, f32[32,3456]{1,0:T(8,128)S(1)} %collective-permute-done.15.refs_0_, f32[32,1920]{1,0:T(8,128)S(1)} %collective-permute-done.16.refs_1_, ...), custom_call_target="tpu_custom_call" | custom-call | tf_op jit(solution)/shard_map/pallas_call | solution.py:23
  (41 shorter events, 12.7 us)
Async XLA Ops:
  0.0 36.0 %copy-start.6 = (f32[7]{0:T(128)S(1)}, f32[7]{0:T(128)}, u32[]{:S(2)}) copy-start(f32[7]{0:T(128)} %taps.6) | copy-start | bytes 88
  1.1 5.6 %collective-permute-start.7 = (f32[12,3,512]{2,1,0:T(4,128)S(1)}, f32[12,3,512]{2,1,0:T(4,128)S(1)}, u32[]{:S(2)}, u32[]{:S(2)}) collective-permute-start(f32[12,3,512]{2,1,0:T(4,128)S(1)} %get-tuple-element.84), channel_id=1, source_target_pairs={{0,1},{1,2},{2,3},{4,5},{5,6},{6,7},{8,9},{9,10},{10,11},{12,13},{... | collective-permute-start | bytes 221192 | tf_op jit(solution)/shard_map/ppermute | solution.py:329
  4.8 5.9 %collective-permute-start.8 = (f32[12,3,512]{2,1,0:T(4,128)S(1)}, f32[12,3,512]{2,1,0:T(4,128)S(1)}, u32[]{:S(2)}, u32[]{:S(2)}) collective-permute-start(f32[12,3,512]{2,1,0:T(4,128)S(1)} %get-tuple-element.83), channel_id=1, source_target_pairs={{1,0},{2,1},{3,2},{5,4},{6,5},{7,6},{9,8},{10,9},{11,10},{13,12},{... | collective-permute-start | bytes 221192 | tf_op jit(solution)/shard_map/ppermute | solution.py:334
  10.7 1.4 copy-start
  12.1 1.2 copy-start.2
  14.0 22.1 %copy-start.4 = (bf16[12,64,512]{2,1,0:T(8,128)(2,1)S(1)}, bf16[12,64,512]{2,1,0:T(8,128)(2,1)}, u32[]{:S(2)}) copy-start(bf16[12,64,512]{2,1,0:T(8,128)(2,1)} %observed.1) | copy-start | bytes 2359300
  18.8 17.2 %collective-permute-start.10 = (f32[3,64,512]{2,1,0:T(8,128)S(1)}, f32[3,64,512]{2,1,0:T(8,128)S(1)}, u32[]{:S(2)}, u32[]{:S(2)}) collective-permute-start(f32[3,64,512]{2,1,0:T(8,128)S(1)} %get-tuple-element.58), channel_id=1, source_target_pairs={{4,0},{8,4},{12,8},{16,12},{20,16},{24,20},{28,24},{5,1},{9,5},{13... | collective-permute-start | bytes 1179656 | tf_op jit(solution)/shard_map/ppermute | solution.py:334
  21.0 15.1 %collective-permute-start.9 = (f32[3,64,512]{2,1,0:T(8,128)S(1)}, f32[3,64,512]{2,1,0:T(8,128)S(1)}, u32[]{:S(2)}, u32[]{:S(2)}) collective-permute-start(f32[3,64,512]{2,1,0:T(8,128)S(1)} %get-tuple-element.57), channel_id=1, source_target_pairs={{0,4},{4,8},{8,12},{12,16},{16,20},{20,24},{24,28},{1,5},{5,9},{9,... | collective-permute-start | bytes 1179656 | tf_op jit(solution)/shard_map/ppermute | solution.py:329
  36.0 9.6 %copy-start.9 = (s32[512]{0:T(512)S(1)}, s32[512]{0:T(512)}, u32[]{:S(2)}) copy-start(s32[512]{0:T(512)} %param.14) | copy-start | bytes 6148
  39.7 32.9 %copy-start.1 = (f32[12,64,512]{2,1,0:T(8,128)S(1)}, f32[12,64,512]{2,1,0:T(8,128)}, u32[]{:S(2)}) copy-start(f32[12,64,512]{2,1,0:T(8,128)} %est.3) | copy-start | bytes 4718596
  39.7 32.8 %copy-start.3 = (f32[512,512]{1,0:T(8,128)S(1)}, f32[512,512]{1,0:T(8,128)}, u32[]{:S(2)}) copy-start(f32[512,512]{1,0:T(8,128)} %weights.3) | copy-start | bytes 3145732
  39.7 11.9 %collective-permute-start.11 = (f32[3,64,512]{2,1,0:T(8,128)S(1)}, f32[3,64,512]{2,1,0:T(8,128)S(1)}, u32[]{:S(2)}, u32[]{:S(2)}) collective-permute-start(f32[3,64,512]{2,1,0:T(8,128)S(1)} %get-tuple-element.60), channel_id=1, source_target_pairs={{0,4},{4,8},{8,12},{12,16},{16,20},{20,24},{24,28},{1,5},{5,9},{9,... | collective-permute-start | bytes 1179656 | tf_op jit(solution)/shard_map/ppermute | solution.py:329
  41.1 20.6 %collective-permute-start.12 = (f32[3,64,512]{2,1,0:T(8,128)S(1)}, f32[3,64,512]{2,1,0:T(8,128)S(1)}, u32[]{:S(2)}, u32[]{:S(2)}) collective-permute-start(f32[3,64,512]{2,1,0:T(8,128)S(1)} %get-tuple-element.61), channel_id=1, source_target_pairs={{4,0},{8,4},{12,8},{16,12},{20,16},{24,20},{28,24},{5,1},{9,5},{13... | collective-permute-start | bytes 1179656 | tf_op jit(solution)/shard_map/ppermute | solution.py:334
  64.7 4.5 %collective-permute-start.13 = (f32[12,3,512]{2,1,0:T(4,128)S(1)}, f32[12,3,512]{2,1,0:T(4,128)S(1)}, u32[]{:S(2)}, u32[]{:S(2)}) collective-permute-start(f32[12,3,512]{2,1,0:T(4,128)S(1)} %get-tuple-element.63), channel_id=1, source_target_pairs={{0,1},{1,2},{2,3},{4,5},{5,6},{6,7},{8,9},{9,10},{10,11},{12,13},{... | collective-permute-start | bytes 221192 | tf_op jit(solution)/shard_map/ppermute | solution.py:329
  66.6 5.9 %collective-permute-start.14 = (f32[12,3,512]{2,1,0:T(4,128)S(1)}, f32[12,3,512]{2,1,0:T(4,128)S(1)}, u32[]{:S(2)}, u32[]{:S(2)}) collective-permute-start(f32[12,3,512]{2,1,0:T(4,128)S(1)} %get-tuple-element.64), channel_id=1, source_target_pairs={{1,0},{2,1},{3,2},{5,4},{6,5},{7,6},{9,8},{10,9},{11,10},{13,12},{... | collective-permute-start | bytes 221192 | tf_op jit(solution)/shard_map/ppermute | solution.py:334
  77.5 32.5 %copy-start.7 = (f32[12,64,512]{2,1,0:T(8,128)}, f32[12,64,512]{2,1,0:T(8,128)S(1)}, u32[]{:S(2)}) copy-start(f32[12,64,512]{2,1,0:T(8,128)S(1)} %shard_map.76.field.base) | copy-start | bytes 4718596
  77.5 32.7 %copy-start.10 = (s32[7]{0:T(128)S(1)}, s32[7]{0:T(128)}, u32[]{:S(2)}) copy-start(s32[7]{0:T(128)} %constant.34.clone) | copy-start | bytes 88
  87.7 10.1 %collective-permute-start.16 = (f32[32,1920]{1,0:T(8,128)S(1)}, f32[32,1920]{1,0:T(8,128)S(1)}, u32[]{:S(2)}, u32[]{:S(2)}) collective-permute-start(f32[32,1920]{1,0:T(8,128)S(1)} %get-tuple-element.66), channel_id=1, source_target_pairs={{0,8},{4,12},{8,16},{12,20},{16,24},{20,28},{1,9},{5,13},{9,17},{1... | collective-permute-start | bytes 737288 | tf_op jit(solution)/shard_map/ppermute | solution.py:397
  89.0 19.6 %collective-permute-start.17 = (f32[32,1920]{1,0:T(8,128)S(1)}, f32[32,1920]{1,0:T(8,128)S(1)}, u32[]{:S(2)}, u32[]{:S(2)}) collective-permute-start(f32[32,1920]{1,0:T(8,128)S(1)} %get-tuple-element.67), channel_id=1, source_target_pairs={{0,12},{4,16},{8,20},{12,24},{16,28},{1,13},{5,17},{9,21},{13,25},... | collective-permute-start | bytes 737288 | tf_op jit(solution)/shard_map/ppermute | solution.py:397
  90.3 47.8 %collective-permute-start.15 = (f32[32,3456]{1,0:T(8,128)S(1)}, f32[32,3456]{1,0:T(8,128)S(1)}, u32[]{:S(2)}, u32[]{:S(2)}) collective-permute-start(f32[32,3456]{1,0:T(8,128)S(1)} %get-tuple-element.65), channel_id=1, source_target_pairs={{0,4},{4,8},{8,12},{12,16},{16,20},{20,24},{24,28},{1,5},{5,9},{9,... | collective-permute-start | bytes 1327112 | tf_op jit(solution)/shard_map/ppermute | solution.py:397
  91.6 46.5 %collective-permute-start.21 = (f32[32,2304]{1,0:T(8,128)S(1)}, f32[32,2304]{1,0:T(8,128)S(1)}, u32[]{:S(2)}, u32[]{:S(2)}) collective-permute-start(f32[32,2304]{1,0:T(8,128)S(1)} %get-tuple-element.71), channel_id=1, source_target_pairs={{0,28},{1,29},{2,30},{3,31}} | collective-permute-start | bytes 884744 | tf_op jit(solution)/shard_map/ppermute | solution.py:397
  92.9 45.2 %collective-permute-start.18 = (f32[32,1920]{1,0:T(8,128)S(1)}, f32[32,1920]{1,0:T(8,128)S(1)}, u32[]{:S(2)}, u32[]{:S(2)}) collective-permute-start(f32[32,1920]{1,0:T(8,128)S(1)} %get-tuple-element.68), channel_id=1, source_target_pairs={{0,16},{4,20},{8,24},{12,28},{1,17},{5,21},{9,25},{13,29},{2,18},{... | collective-permute-start | bytes 737288 | tf_op jit(solution)/shard_map/ppermute | solution.py:397
  97.8 40.3 %collective-permute-start.19 = (f32[32,1920]{1,0:T(8,128)S(1)}, f32[32,1920]{1,0:T(8,128)S(1)}, u32[]{:S(2)}, u32[]{:S(2)}) collective-permute-start(f32[32,1920]{1,0:T(8,128)S(1)} %get-tuple-element.69), channel_id=1, source_target_pairs={{0,20},{4,24},{8,28},{1,21},{5,25},{9,29},{2,22},{6,26},{10,30},{3... | collective-permute-start | bytes 737288 | tf_op jit(solution)/shard_map/ppermute | solution.py:397
  108.7 29.4 %collective-permute-start.20 = (f32[32,1920]{1,0:T(8,128)S(1)}, f32[32,1920]{1,0:T(8,128)S(1)}, u32[]{:S(2)}, u32[]{:S(2)}) collective-permute-start(f32[32,1920]{1,0:T(8,128)S(1)} %get-tuple-element.70), channel_id=1, source_target_pairs={{0,24},{4,28},{1,25},{5,29},{2,26},{6,30},{3,27},{7,31}} | collective-permute-start | bytes 737288 | tf_op jit(solution)/shard_map/ppermute | solution.py:397
  (1 other events, 0.7 us)

commit v2 on v0

v2 whole, which is shorter than its diff:
```python
import functools

import jax
import jax.numpy as jnp
from jax import lax
from jax.experimental import pallas as pl
from jax.experimental.pallas import tpu as pltpu
from jax.sharding import PartitionSpec as P

PLANE_HALF = 3
ROW_HALF = 3
SKEW = 2
LANES = 128
LANE_BITS = 7
EDGE = 8
F32 = jnp.float32
BF16 = jnp.bfloat16
VMEM = pl.BlockSpec(memory_space=pltpu.VMEM)
SMEM = pl.BlockSpec(memory_space=pltpu.SMEM)
LIMIT = 20 * 1024 * 1024


def run(body, outs, ins, operands, scratch=(), aliases=None, cost=None):
    return pl.pallas_call(
        body,
        out_shape=outs,
        in_specs=ins,
        out_specs=jax.tree.map(lambda _: VMEM, outs),
        scratch_shapes=list(scratch),
        input_output_aliases=aliases or {},
        compiler_params=pltpu.CompilerParams(vmem_limit_bytes=LIMIT),
        cost_estimate=cost,
    )(*operands)


def halves(x):
    high = x.astype(BF16)
    return high, (x - high.astype(F32)).astype(BF16)


def product(x, high_w, low_w, dims):
    high, low = halves(x)
    dot = functools.partial(
        lax.dot_general, dimension_numbers=(dims, ((), ())), preferred_element_type=F32
    )
    return dot(high, high_w) + (dot(high, low_w) + dot(low, high_w))


def row_sum(field, plane, rows, taps, direction):
    total = None
    for k in range(2 * ROW_HALF + 1):
        tap = taps[k] if direction > 0 else taps[2 * ROW_HALF - k]
        term = tap * field[plane, pl.ds(k, rows), :]
        total = term if total is None else total + term
    return total


def strip_body(est, observed, upper, lower):
    planes, rows, cols = est.shape
    reach = 2 * ROW_HALF
    for l in range(planes):
        seek = (2 * planes + l) * ROW_HALF
        upper[l * reach : (l + 1) * reach, :] = est[l, 0:reach, :]
        lower[l * reach : (l + 1) * reach, :] = est[l, rows - reach : rows, :]
        seen = observed[l].astype(F32)
        upper[seek : seek + ROW_HALF, :] = seen[0:ROW_HALF]
        lower[seek : seek + ROW_HALF, :] = seen[rows - ROW_HALF : rows]


def own_body(est, weights, mixed, high_w, low_w):
    planes, rows, cols = est.shape
    high, low = halves(weights[...])
    high_w[...] = high
    low_w[...] = low
    x = est[...].reshape(planes * rows, cols)
    mixed[...] = product(x, high, low, ((1,), (0,))).reshape(planes, rows, cols)


def rim_body(chunks, place_of, mixed, above, below, high_w, low_w, taps, tall, *refs):
    rims, ends, edge = refs[:-2], refs[-2], refs[-1]
    odd = (place_of[0] & 1) == 1
    planes, rows, cols = mixed.shape
    reach = 2 * ROW_HALF
    ends[...] = jnp.zeros(ends.shape, F32)
    for l in range(planes):
        ends[l, 0:reach, :] = above[l * reach : (l + 1) * reach, :]
        ends[l, EDGE : EDGE + reach, :] = below[l * reach : (l + 1) * reach, :]
    x = ends[...].reshape(planes * 2 * EDGE, cols)
    ends[...] = product(x, high_w[...], low_w[...], ((1,), (0,))).reshape(ends.shape)
    tall[:, 0:reach, :] = ends[:, 0:reach, :]
    tall[:, reach : reach + rows, :] = mixed[...]
    tall[:, reach + rows : reach + rows + EDGE, :] = ends[:, EDGE:, :]
    tall[:, reach + rows + EDGE :, :] = jnp.zeros((planes, EDGE - reach, cols), F32)
    for l in range(PLANE_HALF):
        for side, base in enumerate((0, planes - PLANE_HALF)):
            edge[side] = row_sum(tall, base + l, rows + EDGE, taps, 1)
        for i, (begin, end) in enumerate(chunks):
            low, high = edge[0, begin:end, :], edge[1, begin:end, :]
            rims[2 * i][l] = jnp.where(odd, low, high)
            rims[2 * i + 1][l] = jnp.where(odd, high, low)


def frame_body(tall, observed, above, below, taps, blur, seen, frame):
    planes, rows, cols = observed.shape
    for l in range(planes):
        blur[l] = skewed(row_sum(tall, l, rows + EDGE, taps, 1), PLANE_HALF + l)
    frame[...] = jnp.zeros(frame.shape, F32)
    for l in range(planes):
        seek = (2 * planes + l) * ROW_HALF
        frame[0:ROW_HALF, :] = above[seek : seek + ROW_HALF, :]
        frame[ROW_HALF : ROW_HALF + rows, :] = observed[l].astype(F32)
        frame[ROW_HALF + rows : 2 * ROW_HALF + rows, :] = below[seek : seek + ROW_HALF, :]
        seen[l] = skewed(frame[...], PLANE_HALF + l)


def skewed(x, place):
    rows, cols = x.shape
    wide = jnp.concatenate([x, jnp.zeros((rows, LANES), F32)], axis=1)
    return pltpu.roll(wide, SKEW * place, 1) if place else wide


def unskewed(x, place):
    width = x.shape[1]
    moved = pltpu.roll(x, (width - SKEW * place) % width, 1) if place else x
    return moved[:, : width - LANES]


def set_sides(sides, pair, other, planes, odd):
    for l in range(PLANE_HALF):
        x, y = pair[l], other[l]
        sides[l] = skewed(jnp.where(odd, x, y), l)
        sides[PLANE_HALF + l] = skewed(jnp.where(odd, y, x), planes + PLANE_HALF + l)


def plane_sum(own, own_row, sides, row, plane, planes, taps, direction):
    total = None
    for k in range(2 * PLANE_HALF + 1):
        source = plane + k - PLANE_HALF
        if source < 0:
            x = sides[source + PLANE_HALF, pl.ds(row, 8), :]
        elif source >= planes:
            x = sides[source - planes + PLANE_HALF, pl.ds(row, 8), :]
        else:
            x = own[source, pl.ds(own_row, 8), :]
        term = (taps[k] if direction > 0 else taps[2 * PLANE_HALF - k]) * x
        total = term if total is None else total + term
    return total


def quotient_body(first, begin, size, place_of, blur, seen, left, right, plane_taps, row_taps, *refs):
    odd = (place_of[0] & 1) == 1
    refs = list(refs)
    before = None if first else refs.pop(0)
    spread, pair, other, tail, sides, ratio = refs
    planes = blur.shape[0]
    fresh = 0 if first else EDGE
    if not first:
        ratio[:, 0:EDGE, :] = before[...]
    set_sides(sides, left, right, planes, odd)
    for l in range(planes):

        def tile(t, _, l=l):
            row = pl.multiple_of(t * 8, 8)
            there = pl.multiple_of(row + begin + fresh, 8)
            blurred = plane_sum(blur, there, sides, row, l, planes, plane_taps, 1)
            ratio[l, pl.ds(pl.multiple_of(row + fresh, 8), 8), :] = seen[
                l, pl.ds(there, 8), :
            ] / jnp.where(blurred > 0, blurred, 1.0)
            return 0

        lax.fori_loop(0, (size + EDGE - fresh) // 8, tile, 0)

    def sum_rows(p, _):
        spread[p] = row_sum(ratio, p, size, row_taps, -1)
        return 0

    lax.fori_loop(0, planes, sum_rows, 0)
    tail[...] = ratio[:, size : size + EDGE, :]
    for l in range(PLANE_HALF):
        low = unskewed(spread[l], PLANE_HALF + l)
        high = unskewed(spread[planes - PLANE_HALF + l], planes + l)
        pair[l] = jnp.where(odd, low, high)
        other[l] = jnp.where(odd, high, low)


def update_body(
    sends, begin, edges, place_of, taps, spread, left, right, high_w, low_w, est, turn, *refs
):
    refs = list(refs)
    before = [refs.pop(0) for _ in range(1 if begin else 0)]
    turned, outs = refs[0], refs[1:-3]
    sides, wide, back = refs[-3:]
    planes, rows, cols = turned.shape
    set_sides(sides, left, right, planes, (place_of[0] & 1) == 1)
    for l in range(planes):

        def tile(t, _, l=l):
            row = pl.multiple_of(t * 8, 8)
            wide[pl.ds(row, 8), :] = plane_sum(spread, row, sides, row, l, planes, taps, -1)
            return 0

        lax.fori_loop(0, rows // 8, tile, 0)
        back[l] = unskewed(wide[...], PLANE_HALF + l)
    x = back[...].reshape(planes * rows, cols)
    y = product(x, high_w[...], low_w[...], ((1,), (1,)))
    back[...] = y.reshape(planes, rows, cols)

    def rotate(t, _):
        row = pl.multiple_of(t * 8, 8)
        for c in range(0, cols, 2 * LANES):
            here = (pl.ds(row, 8), pl.ds(c, 2 * LANES))
            there = (pl.ds(begin + row, 8), pl.ds(c, 2 * LANES))
            field = [back[(p, *here)] * est[(p, *there)] for p in range(planes)]
            bits = jnp.broadcast_to(turn[:, c : c + 2 * LANES], (8, 2 * LANES))
            for bit in range((planes - 1).bit_length()):
                chosen = (bits >> bit & 1) == 1
                field = [
                    jnp.where(chosen, field[(q - (1 << bit)) % planes], field[q])
                    for q in range(planes)
                ]
            for q in range(planes):
                turned[(q, *here)] = field[q]
        return 0

    lax.fori_loop(0, rows // 8, rotate, 0)
    for (plan, ds, whole), out in zip(sends, outs):
        fields = fields_of(before + [turned] if whole else [turned], plan.part_rows)
        for i, (d, skip) in enumerate(ds):
            pack(plan, edges, d, skip, fields, out, i)


class Packing:
    def __init__(self, planes, cols, parts, part_rows, width):
        self.planes, self.cols, self.parts, self.width = planes, cols, parts, width
        self.part_rows = part_rows
        tiles = -(-parts * planes * width // LANES)
        self.shape = (tiles * part_rows, LANES)


def lane_of(shape):
    return lax.broadcasted_iota(jnp.int32, shape, 1)


def pack(plan, edges, d, skip, fields, out, slot):
    tall = range(0, plan.part_rows, 8)
    last = plan.cols // LANES - 1
    lane = lane_of((8, LANES))
    done = {}
    for k in range(plan.parts * plan.planes):
        h, q = divmod(k, plan.planes)
        field, base = fields[h]
        low = edges[d * plan.planes + q] + skip
        tile = low >> LANE_BITS
        one = pl.multiple_of(jnp.minimum(tile, last) << LANE_BITS, LANES)
        two = pl.multiple_of(jnp.minimum(tile + 1, last) << LANE_BITS, LANES)
        begin = k * plan.width
        target, offset = divmod(begin, LANES)
        turn = (offset - low) & (LANES - 1)
        split = lane >= (low & (LANES - 1))
        windows = []
        for t in tall:
            rows = pl.ds(base + t, 8)
            first, second = (field[q, rows, pl.ds(c, LANES)] for c in (one, two))
            windows.append(pltpu.roll(jnp.where(split, first, second), turn, 1))
        if offset == 0:
            done[target] = windows
        else:
            done[target] = [
                jnp.where(lane >= offset, x, y) for x, y in zip(windows, done[target])
            ]
        if offset + plan.width > LANES:
            done[target + 1] = windows
        end = k + 1 == plan.parts * plan.planes
        for full in [x for x in done if end or (x + 1) * LANES <= begin + plan.width]:
            for t, x in zip(tall, done.pop(full)):
                out[slot, pl.ds(full * plan.part_rows + t, 8), :] = x


def place(sources, edges, me, bases, out, first_round, begin):
    plan = sources[0][0]
    tall = range(0, plan.part_rows, 8)
    count = plan.cols // LANES
    lane = lane_of((8, LANES))
    spots = [(h, t) for h in range(len(bases)) for t in tall]
    for q in range(plan.planes):
        found = {}
        bound = edges[plan.planes + q]
        for c in range(count):
            keep = lane < bound - c * LANES
            for h, t in spots:
                base, row = bases[h]
                x = base[q, row + t : row + t + 8, c * LANES : (c + 1) * LANES]
                found[h, t, c] = jnp.where(keep, x, 0.0) if first_round else x
        for plan, message, slot, d, skip, first_part in sources:
            low = edges[d * plan.planes + q] + skip
            high = jnp.minimum(edges[(d + 1) * plan.planes + q], low + plan.width)
            high = jnp.where(me >= d, high, 0)
            inside = [(lane >= low - c * LANES) & (lane < high - c * LANES) for c in range(count)]
            for h in range(len(bases)):
                k = (first_part + h) * plan.planes + q
                target, offset = divmod(k * plan.width, LANES)
                turn = (low - offset) & (LANES - 1)
                for t in tall:
                    row = target * plan.part_rows + t
                    window = message[slot, pl.ds(row, 8), :]
                    if offset + plan.width > LANES:
                        after = message[slot, pl.ds(row + plan.part_rows, 8), :]
                        window = jnp.where(lane >= offset, window, after)
                    window = pltpu.roll(window, turn, 1)
                    for c in range(count):
                        found[h, t, c] = jnp.where(inside[c], window, found[h, t, c])
        for (h, t, c), x in found.items():
            row = begin + h * plan.part_rows + t
            out[q, row : row + 8, c * LANES : (c + 1) * LANES] = x


def fields_of(refs, part_rows):
    return [(ref, row) for ref in refs for row in range(0, ref.shape[1], part_rows)]


def settle_first(sends, edges, place_of, base, *refs):
    sources = [
        (plan, ref, i, d, skip, 0)
        for (plan, ds, _), ref in zip(sends, refs)
        for i, (d, skip) in enumerate(ds)
    ]
    fields = fields_of([base], sends[0][0].part_rows)
    place(sources, edges, place_of[0], fields, refs[-1], True, 0)


def settle_last(sends, edges, place_of, settled, base, *refs):
    out, begin = refs[-1], settled.shape[1]
    part_rows = sends[0][0].part_rows
    sources, late = [], []
    for (plan, ds, whole), ref in zip(sends, refs):
        for i, (d, skip) in enumerate(ds):
            if whole:
                late.append((plan, ref, i, d, skip, 0))
            sources.append((plan, ref, i, d, skip, begin // part_rows if whole else 0))
    me = place_of[0]
    place(late, edges, me, fields_of([settled], part_rows), out, False, 0)
    place(sources, edges, me, fields_of([base], part_rows), out, True, begin)


def round_pack_body(count, plan, rooms, edges, place_of, step, *refs):
    out, fields = refs[-1], fields_of(refs[:-1], plan.part_rows)
    for d in range(1, count):
        slot = lax.rem(place_of[0] + d, count)
        pack(plan, edges, d, rooms[d - 1] + step[0] * plan.width, fields, out, slot)


def round_place_body(count, plan, rooms, edges, place_of, step, base, message, out):
    me = place_of[0]
    sources = [
        (plan, message, lax.rem(me + count - d, count), d, rooms[d - 1] + step[0] * plan.width, 0)
        for d in range(1, count)
    ]
    place(sources, edges, me, fields_of([base], plan.part_rows), out, False, 0)


def to_next(x, axis):
    count = lax.axis_size(axis)
    return lax.ppermute(x, axis, [(i, i + 1) for i in range(count - 1)])


def to_last(x, axis):
    count = lax.axis_size(axis)
    return lax.ppermute(x, axis, [(i + 1, i) for i in range(count - 1)])


def swaps(begin, count):
    ends = [(i, i + 1) for i in range(begin, count - 1, 2)]
    return ends + [(j, i) for i, j in ends]


def like(*shape):
    return jax.ShapeDtypeStruct(shape, F32)


def on_device(observed, estimate, column_weights, plane_taps, row_taps, shear_planes):
    planes, rows, cols = estimate.shape
    count = lax.axis_size("scan")
    width = cols + LANES
    half = rows // 2
    chunks = [(0, half), (half, rows)]
    fresh = [(begin + EDGE if begin else 0, end + EDGE) for begin, end in chunks]
    reach = 2 * ROW_HALF

    strip = like(3 * ROW_HALF * planes, cols)
    upper, lower = run(strip_body, (strip, strip), [VMEM, VMEM], (estimate, observed))
    above, below = to_next(lower, "lat"), to_last(upper, "lat")
    me = lax.axis_index("scan").astype(jnp.int32)[None]
    levels = jnp.arange((count + 1) * planes, dtype=jnp.int32) - planes
    edges = jnp.sum(shear_planes[None, :] <= levels[:, None], axis=1, dtype=jnp.int32)
    turn = (shear_planes % planes)[None, :]

    weight = jax.ShapeDtypeStruct(column_weights.shape, BF16)
    mixed, high_w, low_w = run(
        own_body,
        (like(planes, rows, cols), weight, weight),
        [VMEM, VMEM],
        (estimate, column_weights),
    )
    tall, *rims = run(
        functools.partial(rim_body, fresh),
        (
            like(planes, rows + 2 * EDGE, cols),
            *(like(PLANE_HALF, e - b, cols) for b, e in fresh for _ in range(2)),
        ),
        [SMEM, VMEM, VMEM, VMEM, VMEM, VMEM, SMEM],
        (me, mixed, above, below, high_w, low_w, row_taps),
        [
            pltpu.VMEM((planes, 2 * EDGE, cols), F32),
            pltpu.VMEM((2, rows + EDGE, cols), F32),
        ],
    )
    framed = like(planes, rows + EDGE, width)
    blur, seen = run(
        frame_body,
        (framed, framed),
        [VMEM, VMEM, VMEM, VMEM, SMEM],
        (tall, observed, above, below, row_taps),
        [pltpu.VMEM((rows + EDGE, cols), F32)],
    )

    def beside(pair, other):
        last = lax.ppermute(other, "scan", swaps(1, count))
        return lax.ppermute(pair, "scan", swaps(0, count)), last

    def beside(pair, other):
        last = lax.ppermute(other, "scan", swaps(1, count))
        return lax.ppermute(pair, "scan", swaps(0, count)), last

    def exchange(message):
        return lax.all_to_all(message, "scan", split_axis=0, concat_axis=0, tiled=True)

    share = max(cols // count, 8)
    part_rows = 16 if half % 16 == 0 else 8

    def packing(height, columns):
        parts = height // part_rows
        return Packing(planes, cols, parts, part_rows, min(-(-columns // 8) * 8, LANES))

    near, far = packing(rows, share * 9 // 8), packing(rows, share * 3 // 2)
    middle = packing(half, share * 5 // 4)
    later = packing(rows, share // 4)
    mid = [(middle, [(d, 0)], False) for d in range(2, count - 1)]
    wide = [
        (near, [(1, 0), (1, near.width)], True),
        (far, [(count - 1, 0)], True),
    ]
    rooms = [2 * near.width] + [middle.width] * (count - 3) + [far.width]

    tail = settled = None
    pieces = []
    left, right = beside(*rims[0:2])
    for i, (begin, end) in enumerate(chunks):
        size = end - begin
        last = i == len(chunks) - 1
        if pieces:
            left, right, pieces[-1] = lax.optimization_barrier((left, right, pieces[-1]))
        before = (tail,) if pieces else ()
        spread, low, high, tail = run(
            functools.partial(quotient_body, i == 0, begin, size),
            (
                like(planes, size, width),
                like(PLANE_HALF, size, cols),
                like(PLANE_HALF, size, cols),
                like(planes, EDGE, width),
            ),
            [SMEM, VMEM, VMEM, VMEM, VMEM, SMEM, SMEM] + [VMEM] * len(before),
            (me, blur, seen, left, right, plane_taps, row_taps, *before),
            [
                pltpu.VMEM((2 * PLANE_HALF, fresh[i][1] - fresh[i][0], width), F32),
                pltpu.VMEM((planes, size + EDGE, width), F32),
            ],
        )
        if last:
            sides = beside(low, high)
        else:
            ahead = lax.optimization_barrier((low, high, *rims[2 * i + 2 : 2 * i + 4]))
            sides = beside(*ahead[:2])
            left, right = beside(*ahead[2:])
        sends = mid + wide if last else mid
        turned, *packed = run(
            functools.partial(update_body, sends, begin),
            (
                like(planes, size, cols),
                *(like(len(ds), *plan.shape) for plan, ds, _ in sends),
            ),
            [SMEM, SMEM, SMEM] + [VMEM] * (7 + len(pieces)),
            (edges, me, plane_taps, spread, *sides, high_w, low_w, estimate, turn, *pieces),
            [
                pltpu.VMEM((2 * PLANE_HALF, size, width), F32),
                pltpu.VMEM((size, width), F32),
                pltpu.VMEM((planes, size, cols), F32),
            ],
        )
        pieces.append(turned)
        moved = [
            lax.ppermute(x, "scan", [(j, j + ds[0][0]) for j in range(count - ds[0][0])])
            for (_, ds, _), x in zip(sends, packed)
        ]
        ready = (settled,) if last else ()
        settled = run(
            functools.partial(settle_last if last else settle_first, sends),
            like(planes, end, cols),
            [SMEM, SMEM] + [VMEM] * (1 + len(ready) + len(moved)),
            (edges, me, *ready, turned, *moved),
        )

    table = edges.reshape(count + 1, planes)
    row = lax.broadcasted_iota(jnp.int32, (count - 1, planes), 0)
    room = jnp.where(row == 0, rooms[0], jnp.where(row == count - 2, rooms[-1], middle.width))
    rest = table[2:] - table[1:-1] - room
    rounds = jnp.max((rest + later.width - 1) // later.width)

    def again(state):
        step = state[0][None]
        message = run(
            functools.partial(round_pack_body, count, later, rooms),
            like(count, *later.shape),
            [SMEM, SMEM, SMEM] + [VMEM] * len(pieces),
            (edges, me, step, *pieces),
        )
        base = run(
            functools.partial(round_place_body, count, later, rooms),
            like(planes, rows, cols),
            [SMEM, SMEM, SMEM, VMEM, VMEM],
            (edges, me, step, state[1], exchange(message)),
        )
        return state[0] + 1, base

    return lax.while_loop(lambda state: state[0] < rounds, again, (jnp.int32(0), settled))[1]


def solution(mesh):
    placed = (P("scan", "lat", None), P("scan", "lat", None), P(), P(), P(), P())
    return jax.shard_map(
        on_device, mesh=mesh, in_specs=placed, out_specs=P("scan", "lat", None), check_vma=False
    )
```

time: 229 us -> 110 us (0.48); the launches traced: 225 us -> 109 us
  blocking collectives: 41 us -> 0 us
  other arithmetic: 36.4 us -> 1 us
  local copies, waits for them, and re-layouts: 38.7 us -> 5.02 us
  Pallas kernels: 0 us -> 25.5 us
  waiting for transfers between devices: 67.1 us -> 45.7 us
  matrix products: 12.5 us -> 0 us
    all_to_all x1 -> x0, blocking collectives: 41 us -> none  [on_device(): lax.all_to_all(settled, 'scan', split_axis=0, concat_axis=2, tiled=True)]
    all_to_all x1 -> x0, waiting for transfers between devices: 33.9 us -> none  [on_device(): lax.all_to_all(updated, 'scan', split_axis=2, concat_axis=0, tiled=True)]
    pallas_call x0 -> x10, Pallas kernels: none -> 25.5 us  [run(): pl.pallas_call(body, out_shape=outs, in_specs=ins, out_specs=jax.tree.map...]
    all_to_all x4 -> x0, local copies, waits for them, and re-layouts: 14 us -> none  [the longest x2 9.58 us: on_device(): lax.all_to_all(settled, 'scan', split_axis=0, concat_axis=2, tiled=True)]
    add x2 -> x0, other arithmetic: 12.7 us -> none  [the longest x1 6.68 us: plane_pass(): summed + kernel[offset + halfwidth] * widened[begin:begin + plane_count,...]
    ppermute x8 -> x22, waiting for transfers between devices: 33.2 us -> 45.7 us  [the longest x12 28.7 us: on_device(): lax.ppermute(x, 'scan', [(j, j + ds[0][0]) for j in range(count - ds[0][0...]
    dot_general x2 -> x0, matrix products: 12.5 us -> none  [column_mix(): jnp.dot(flat, matrix, precision=lax.Precision.HIGHEST, preferred_element_...]
    unnamed x16 -> x22, local copies, waits for them, and re-layouts: 17.4 us -> 4.94 us
  transfers between devices with their start and end apart: 9 -> 22, of which waited for: 8 -> 6; matrix products, arithmetic and copies ran while one was open for 1% -> 1% of each run, Pallas kernels for 0% -> 13%
where the time goes in v2:
time: 110 us; the launch traced here: 109 us
  waiting for transfers between devices  45.7 us (42%)
  starting transfers between devices  31.2 us (28%)
  Pallas kernels  25.5 us (23%)
  local copies, waits for them, and re-layouts  5.02 us (5%)
    ppermute x12, waiting for transfers between devices, on_device(): lax.ppermute(x, 'scan', [(j, j + ds[0][0]) for j in range(count - ds[0][0...  28.7 us
    pallas_call x10, Pallas kernels, run(): pl.pallas_call(body, out_shape=outs, in_specs=ins, out_specs=jax.tree.map...  25.5 us
    ppermute x12, starting transfers between devices, on_device(): lax.ppermute(x, 'scan', [(j, j + ds[0][0]) for j in range(count - ds[0][0...  15.7 us
    ppermute x4, waiting for transfers between devices, beside(): return (lax.ppermute(pair, 'scan', swaps(0, count)), last)  14.3 us
    ppermute x4, starting transfers between devices, beside(): return (lax.ppermute(pair, 'scan', swaps(0, count)), last)  7.12 us
    unnamed x22, local copies, waits for them, and re-layouts  4.94 us
    ppermute x1, starting transfers between devices, to_next(): return lax.ppermute(x, axis, [(i, i + 1) for i in range(count - 1)])  3.81 us
    ppermute x1, waiting for transfers between devices, to_last(): return lax.ppermute(x, axis, [(i + 1, i) for i in range(count - 1)])  2.71 us
  transfers between devices with their start and end apart: 22, of which 6 were waited for; matrix products, arithmetic and copies ran while one was open for 1% of the time, Pallas kernels for 13%

profile of v2, /device:TPU:29, one launch (start us, length us, event | category | flops | bytes accessed | tf_op | source)
XLA Modules:
  0.0 109.3 jit_solution(8868632098399776974)
XLA Ops:
  0.0 1.4 %copy-done = f32[12,64,512]{2,1,0:T(8,128)S(1)} copy-done((f32[12,64,512]{2,1,0:T(8,128)S(1)}, f32[12,64,512]{2,1,0:T(8,128)}, u32[]{:S(2)}) %copy-start) | copy-done | bytes 1572888
  2.6 3.8 %collective-permute-start = (f32[108,512]{1,0:T(8,128)S(1)}, f32[108,512]{1,0:T(8,128)S(1)}, u32[]{:S(2)}, u32[]{:S(2)}) collective-permute-start(f32[108,512]{1,0:T(8,128)S(1)} %get-tuple-element.84), channel_id=1, source_target_pairs={{0,1},{1,2},{2,3},{4,5},{5,6},{6,7},{8,9},{9,10},{10,11},{12,13},{... | collective-permute-start | bytes 663560 | tf_op jit(solution)/shard_map/ppermute | solution.py:363
  6.5 1.9 %collective-permute-start.1 = (f32[108,512]{1,0:T(8,128)S(1)}, f32[108,512]{1,0:T(8,128)S(1)}, u32[]{:S(2)}, u32[]{:S(2)}) collective-permute-start(f32[108,512]{1,0:T(8,128)S(1)} %get-tuple-element.85), channel_id=1, source_target_pairs={{1,0},{2,1},{3,2},{5,4},{6,5},{7,6},{9,8},{10,9},{11,10},{13,12},{... | collective-permute-start | bytes 663560 | tf_op jit(solution)/shard_map/ppermute | solution.py:368
  9.6 1.4 %shard_map.64 = (f32[12,64,512]{2,1,0:T(8,128)S(1)}, bf16[512,512]{1,0:T(8,128)(2,1)S(1)}, bf16[512,512]{1,0:T(8,128)(2,1)S(1)}) custom-call(f32[12,64,512]{2,1,0:T(8,128)S(1)} %copy-done.1, f32[512,512]{1,0:T(8,128)S(1)} %copy-done.4), custom_call_target="tpu_custom_call" | custom-call | tf_op jit(solution)/shard_map/pallas_call | solution.py:24
  11.1 2.7 %collective-permute-done.1.below = f32[108,512]{1,0:T(8,128)S(1)} collective-permute-done((f32[108,512]{1,0:T(8,128)S(1)}, f32[108,512]{1,0:T(8,128)S(1)}, u32[]{:S(2)}, u32[]{:S(2)}) %collective-permute-start.1) | collective-permute-done | bytes 221216 | tf_op jit(solution)/shard_map/ppermute | solution.py:368
  13.8 2.0 %shard_map.66 = (f32[12,80,512]{2,1,0:T(8,128)S(1)}, f32[3,40,512]{2,1,0:T(8,128)S(1)}, f32[3,40,512]{2,1,0:T(8,128)S(1)}, f32[3,32,512]{2,1,0:T(8,128)S(1)}, f32[3,32,512]{2,1,0:T(8,128)S(1)}) custom-call(s32[1]{0:T(128)} %bitcast.1.place_of, f32[12,64,512]{2,1,0:T(8,128)S(1)} %get-tuple-element.83.mixed, f32[108,512]{1,0:T(8,128)S(1)} %collective-permute-done.above, ...), custom_call_target="tpu_custom_call" | custom-call | tf_op jit(solution)/shard_map/pallas_call | solution.py:24
  17.0 2.7 %shard_map.67 = (f32[12,72,640]{2,1,0:T(8,128)S(1)}, f32[12,72,640]{2,1,0:T(8,128)S(1)}) custom-call(f32[12,80,512]{2,1,0:T(8,128)S(1)} %get-tuple-element.88.tall, bf16[12,64,512]{2,1,0:T(8,128)(2,1)S(1)} %copy-done.3, f32[108,512]{1,0:T(8,128)S(1)} %collective-permute-done.above, f32[108,512]{1,0:T(8,128)S(1)} %collective-permute-done.1.below, f32[7]{0:T(128)S(1)} %copy-done.6), custom_call_target="tpu_custom_call" | custom-call | tf_op jit(solution)/shard_map/pallas_call | solution.py:24
  19.7 4.8 %collective-permute-done.2.left = f32[3,40,512]{2,1,0:T(8,128)S(1)} collective-permute-done((f32[3,40,512]{2,1,0:T(8,128)S(1)}, f32[3,40,512]{2,1,0:T(8,128)S(1)}, u32[]{:S(2)}, u32[]{:S(2)}) %collective-permute-start.2) | collective-permute-done | bytes 245792 | tf_op jit(solution)/shard_map/ppermute | solution.py:432
  24.5 3.5 %shard_map.68 = (f32[12,32,640]{2,1,0:T(8,128)S(1)}, f32[3,32,512]{2,1,0:T(8,128)S(1)}, f32[3,32,512]{2,1,0:T(8,128)S(1)}, f32[12,8,640]{2,1,0:T(8,128)S(1)}) custom-call(s32[1]{0:T(128)} %bitcast.1.place_of, f32[12,72,640]{2,1,0:T(8,128)S(1)} %get-tuple-element.89.blur, f32[12,72,640]{2,1,0:T(8,128)S(1)} %get-tuple-element.90.seen, ...), custom_call_target="tpu_custom_call" | custom-call | tf_op jit(solution)/shard_map/pallas_call | solution.py:24
  28.1 2.0 %collective-permute-start.4 = (f32[3,32,512]{2,1,0:T(8,128)S(1)}, f32[3,32,512]{2,1,0:T(8,128)S(1)}, u32[]{:S(2)}, u32[]{:S(2)}) collective-permute-start(f32[3,32,512]{2,1,0:T(8,128)S(1)} %get-tuple-element.98), channel_id=1, source_target_pairs={{0,4},{8,12},{16,20},{24,28},{4,0},{12,8},{20,16},{28,24},{1,5},{9... | collective-permute-start | bytes 589832 | tf_op jit(solution)/shard_map/ppermute | solution.py:432
  30.7 2.7 %collective-permute-start.11 = (f32[3,32,512]{2,1,0:T(8,128)S(1)}, f32[3,32,512]{2,1,0:T(8,128)S(1)}, u32[]{:S(2)}, u32[]{:S(2)}) collective-permute-start(f32[3,32,512]{2,1,0:T(8,128)S(1)} %get-tuple-element.106), channel_id=1, source_target_pairs={{0,4},{8,12},{16,20},{24,28},{4,0},{12,8},{20,16},{28,24},{1,5},{9... | collective-permute-start | bytes 589832 | tf_op jit(solution)/shard_map/ppermute | solution.py:432
  34.0 8.7 %collective-permute-done.4.left = f32[3,32,512]{2,1,0:T(8,128)S(1)} collective-permute-done((f32[3,32,512]{2,1,0:T(8,128)S(1)}, f32[3,32,512]{2,1,0:T(8,128)S(1)}, u32[]{:S(2)}, u32[]{:S(2)}) %collective-permute-start.4) | collective-permute-done | bytes 196640 | tf_op jit(solution)/shard_map/ppermute | solution.py:432
  42.7 3.9 %shard_map.69 = (f32[12,32,512]{2,1,0:T(8,128)S(1)}, f32[1,240,128]{2,1,0:T(8,128)S(1)}, f32[1,240,128]{2,1,0:T(8,128)S(1)}, f32[1,240,128]{2,1,0:T(8,128)S(1)},...) custom-call(s32[108]{0:T(128)S(1)} %convert_reduce_fusion.edges, s32[1]{0:T(128)} %bitcast.1.place_of, ...), custom_call_target="tpu_custom_call" | custom-call | tf_op jit(solution)/shard_map/pallas_call | solution.py:24
  46.7 3.9 %shard_map.71 = (f32[12,32,640]{2,1,0:T(8,128)S(1)}, f32[3,32,512]{2,1,0:T(8,128)S(1)}, f32[3,32,512]{2,1,0:T(8,128)S(1)}, f32[12,8,640]{2,1,0:T(8,128)}) custom-call(s32[1]{0:T(128)} %bitcast.1.place_of, f32[12,72,640]{2,1,0:T(8,128)S(1)} %get-tuple-element.89.blur, f32[12,72,640]{2,1,0:T(8,128)S(1)} %get-tuple-element.90.seen, ...), custom_call_target="tpu_custom_call" | custom-call | tf_op jit(solution)/shard_map/pallas_call | solution.py:24
  50.6 2.2 %collective-permute-start.13 = (f32[3,32,512]{2,1,0:T(8,128)S(1)}, f32[3,32,512]{2,1,0:T(8,128)S(1)}, u32[]{:S(2)}, u32[]{:S(2)}) collective-permute-start(f32[3,32,512]{2,1,0:T(8,128)S(1)} %get-tuple-element.112), channel_id=1, source_target_pairs={{0,4},{8,12},{16,20},{24,28},{4,0},{12,8},{20,16},{28,24},{1,5},{9... | collective-permute-start | bytes 589832 | tf_op jit(solution)/shard_map/ppermute | solution.py:432
  53.4 1.3 %collective-permute-start.10 = (f32[1,240,128]{2,1,0:T(8,128)S(1)}, f32[1,240,128]{2,1,0:T(8,128)S(1)}, u32[]{:S(2)}, u32[]{:S(2)}) collective-permute-start(f32[1,240,128]{2,1,0:T(8,128)S(1)} %get-tuple-element.105), channel_id=1, source_target_pairs={{0,24},{4,28},{1,25},{5,29},{2,26},{6,30},{3,27},{7,31}} | collective-permute-start | bytes 368648 | tf_op jit(solution)/shard_map/ppermute | solution.py:501
  54.7 1.3 %collective-permute-start.6 = (f32[1,240,128]{2,1,0:T(8,128)S(1)}, f32[1,240,128]{2,1,0:T(8,128)S(1)}, u32[]{:S(2)}, u32[]{:S(2)}) collective-permute-start(f32[1,240,128]{2,1,0:T(8,128)S(1)} %get-tuple-element.101), channel_id=1, source_target_pairs={{0,8},{4,12},{8,16},{12,20},{16,24},{20,28},{1,9},{5,13},{9,17},{1... | collective-permute-start | bytes 368648 | tf_op jit(solution)/shard_map/ppermute | solution.py:501
  60.7 5.2 %shard_map.72 = (f32[12,32,512]{2,1,0:T(8,128)}, f32[1,240,128]{2,1,0:T(8,128)S(1)}, f32[1,240,128]{2,1,0:T(8,128)S(1)}, f32[1,240,128]{2,1,0:T(8,128)S(1)}, f32...) custom-call(s32[108]{0:T(128)S(1)} %convert_reduce_fusion.edges, ...), custom_call_target="tpu_custom_call" | custom-call | tf_op jit(solution)/shard_map/pallas_call | solution.py:24
  69.8 13.1 %collective-permute-done.8.refs_2_ = f32[1,240,128]{2,1,0:T(8,128)S(1)} collective-permute-done((f32[1,240,128]{2,1,0:T(8,128)S(1)}, f32[1,240,128]{2,1,0:T(8,128)S(1)}, u32[]{:S(2)}, u32[]{:S(2)}) %collective-permute-start.8) | collective-permute-done | bytes 122912 | tf_op jit(solution)/shard_map/ppermute | solution.py:501
  84.2 1.3 %collective-permute-start.17 = (f32[1,240,128]{2,1,0:T(8,128)S(1)}, f32[1,240,128]{2,1,0:T(8,128)S(1)}, u32[]{:S(2)}, u32[]{:S(2)}) collective-permute-start(f32[1,240,128]{2,1,0:T(8,128)S(1)} %get-tuple-element.118), channel_id=1, source_target_pairs={{0,16},{4,20},{8,24},{12,28},{1,17},{5,21},{9,25},{13,29},{2,18},{... | collective-permute-start | bytes 368648 | tf_op jit(solution)/shard_map/ppermute | solution.py:501
  86.8 1.5 %collective-permute-start.19 = (f32[1,240,128]{2,1,0:T(8,128)S(1)}, f32[1,240,128]{2,1,0:T(8,128)S(1)}, u32[]{:S(2)}, u32[]{:S(2)}) collective-permute-start(f32[1,240,128]{2,1,0:T(8,128)S(1)} %get-tuple-element.120), channel_id=1, source_target_pairs={{0,24},{4,28},{1,25},{5,29},{2,26},{6,30},{3,27},{7,31}} | collective-permute-start | bytes 368648 | tf_op jit(solution)/shard_map/ppermute | solution.py:501
  89.2 1.6 %shard_map.70.settled = f32[12,32,512]{2,1,0:T(8,128)S(1)} custom-call(s32[108]{0:T(128)S(1)} %convert_reduce_fusion.edges, s32[1]{0:T(128)} %bitcast.1.place_of, f32[12,32,512]{2,1,0:T(8,128)} %copy-done.8, f32[1,240,128]{2,1,0:T(8,128)S(1)} %collective-permute-done.6.refs_0_, f32[1,240,128]{2,1,0:T(8,128)S(1)} %collective-permute-done.7.refs_1_, ...), custom_call_target="tpu_custom_call" | custom-call | tf_op jit(solution)/shard_map/pallas_call | solution.py:24
  90.7 15.5 %collective-permute-done.17.refs_2_ = f32[1,240,128]{2,1,0:T(8,128)S(1)} collective-permute-done((f32[1,240,128]{2,1,0:T(8,128)S(1)}, f32[1,240,128]{2,1,0:T(8,128)S(1)}, u32[]{:S(2)}, u32[]{:S(2)}) %collective-permute-start.17) | collective-permute-done | bytes 122912 | tf_op jit(solution)/shard_map/ppermute | solution.py:501
  106.3 1.3 %shard_map.73 = f32[12,64,512]{2,1,0:T(8,128)S(1)} custom-call(s32[108]{0:T(128)S(1)} %convert_reduce_fusion.edges, s32[1]{0:T(128)} %bitcast.1.place_of, f32[12,32,512]{2,1,0:T(8,128)S(1)} %shard_map.70.settled, f32[12,32,512]{2,1,0:T(8,128)S(1)} %copy-done.9, f32[1,240,128]{2,1,0:T(8,128)S(1)} %collective-permute-done.15.refs_0_, ...), custom_call_target="tpu_custom_call" | custom-call | tf_op jit(solution)/shard_map/pallas_call | solution.py:24
  (61 shorter events, 19.3 us)
Async XLA Ops:
  2.6 8.4 %collective-permute-start = (f32[108,512]{1,0:T(8,128)S(1)}, f32[108,512]{1,0:T(8,128)S(1)}, u32[]{:S(2)}, u32[]{:S(2)}) collective-permute-start(f32[108,512]{1,0:T(8,128)S(1)} %get-tuple-element.84), channel_id=1, source_target_pairs={{0,1},{1,2},{2,3},{4,5},{5,6},{6,7},{8,9},{9,10},{10,11},{12,13},{... | collective-permute-start | bytes 663560 | tf_op jit(solution)/shard_map/ppermute | solution.py:363
  6.5 7.3 %collective-permute-start.1 = (f32[108,512]{1,0:T(8,128)S(1)}, f32[108,512]{1,0:T(8,128)S(1)}, u32[]{:S(2)}, u32[]{:S(2)}) collective-permute-start(f32[108,512]{1,0:T(8,128)S(1)} %get-tuple-element.85), channel_id=1, source_target_pairs={{1,0},{2,1},{3,2},{5,4},{6,5},{7,6},{9,8},{10,9},{11,10},{13,12},{... | collective-permute-start | bytes 663560 | tf_op jit(solution)/shard_map/ppermute | solution.py:368
  15.8 8.7 %collective-permute-start.2 = (f32[3,40,512]{2,1,0:T(8,128)S(1)}, f32[3,40,512]{2,1,0:T(8,128)S(1)}, u32[]{:S(2)}, u32[]{:S(2)}) collective-permute-start(f32[3,40,512]{2,1,0:T(8,128)S(1)} %get-tuple-element.91), channel_id=1, source_target_pairs={{0,4},{8,12},{16,20},{24,28},{4,0},{12,8},{20,16},{28,24},{1,5},{9... | collective-permute-start | bytes 737288 | tf_op jit(solution)/shard_map/ppermute | solution.py:432
  16.1 8.4 %collective-permute-start.3 = (f32[3,40,512]{2,1,0:T(8,128)S(1)}, f32[3,40,512]{2,1,0:T(8,128)S(1)}, u32[]{:S(2)}, u32[]{:S(2)}) collective-permute-start(f32[3,40,512]{2,1,0:T(8,128)S(1)} %get-tuple-element.92), channel_id=1, source_target_pairs={{4,8},{12,16},{20,24},{8,4},{16,12},{24,20},{5,9},{13,17},{21,25},... | collective-permute-start | bytes 737288 | tf_op jit(solution)/shard_map/ppermute | solution.py:431
  28.1 14.7 %collective-permute-start.4 = (f32[3,32,512]{2,1,0:T(8,128)S(1)}, f32[3,32,512]{2,1,0:T(8,128)S(1)}, u32[]{:S(2)}, u32[]{:S(2)}) collective-permute-start(f32[3,32,512]{2,1,0:T(8,128)S(1)} %get-tuple-element.98), channel_id=1, source_target_pairs={{0,4},{8,12},{16,20},{24,28},{4,0},{12,8},{20,16},{28,24},{1,5},{9... | collective-permute-start | bytes 589832 | tf_op jit(solution)/shard_map/ppermute | solution.py:432
  30.0 12.7 %collective-permute-start.5 = (f32[3,32,512]{2,1,0:T(8,128)S(1)}, f32[3,32,512]{2,1,0:T(8,128)S(1)}, u32[]{:S(2)}, u32[]{:S(2)}) collective-permute-start(f32[3,32,512]{2,1,0:T(8,128)S(1)} %get-tuple-element.99), channel_id=1, source_target_pairs={{4,8},{12,16},{20,24},{8,4},{16,12},{24,20},{5,9},{13,17},{21,25},... | collective-permute-start | bytes 589832 | tf_op jit(solution)/shard_map/ppermute | solution.py:431
  30.7 16.0 %collective-permute-start.11 = (f32[3,32,512]{2,1,0:T(8,128)S(1)}, f32[3,32,512]{2,1,0:T(8,128)S(1)}, u32[]{:S(2)}, u32[]{:S(2)}) collective-permute-start(f32[3,32,512]{2,1,0:T(8,128)S(1)} %get-tuple-element.106), channel_id=1, source_target_pairs={{0,4},{8,12},{16,20},{24,28},{4,0},{12,8},{20,16},{28,24},{1,5},{9... | collective-permute-start | bytes 589832 | tf_op jit(solution)/shard_map/ppermute | solution.py:432
  33.4 13.3 %collective-permute-start.12 = (f32[3,32,512]{2,1,0:T(8,128)S(1)}, f32[3,32,512]{2,1,0:T(8,128)S(1)}, u32[]{:S(2)}, u32[]{:S(2)}) collective-permute-start(f32[3,32,512]{2,1,0:T(8,128)S(1)} %get-tuple-element.107), channel_id=1, source_target_pairs={{4,8},{12,16},{20,24},{8,4},{16,12},{24,20},{5,9},{13,17},{21,25},... | collective-permute-start | bytes 589832 | tf_op jit(solution)/shard_map/ppermute | solution.py:431
  46.6 19.2 %copy-start.8 = (f32[12,32,512]{2,1,0:T(8,128)}, f32[12,32,512]{2,1,0:T(8,128)S(1)}, u32[]{:S(2)}) copy-start(f32[12,32,512]{2,1,0:T(8,128)S(1)} %get-tuple-element.187.base.refs_0_) | copy-start | bytes 2359300
  50.6 7.5 %collective-permute-start.13 = (f32[3,32,512]{2,1,0:T(8,128)S(1)}, f32[3,32,512]{2,1,0:T(8,128)S(1)}, u32[]{:S(2)}, u32[]{:S(2)}) collective-permute-start(f32[3,32,512]{2,1,0:T(8,128)S(1)} %get-tuple-element.112), channel_id=1, source_target_pairs={{0,4},{8,12},{16,20},{24,28},{4,0},{12,8},{20,16},{28,24},{1,5},{9... | collective-permute-start | bytes 589832 | tf_op jit(solution)/shard_map/ppermute | solution.py:432
  52.8 6.6 %collective-permute-start.14 = (f32[3,32,512]{2,1,0:T(8,128)S(1)}, f32[3,32,512]{2,1,0:T(8,128)S(1)}, u32[]{:S(2)}, u32[]{:S(2)}) collective-permute-start(f32[3,32,512]{2,1,0:T(8,128)S(1)} %get-tuple-element.113), channel_id=1, source_target_pairs={{4,8},{12,16},{20,24},{8,4},{16,12},{24,20},{5,9},{13,17},{21,25},... | collective-permute-start | bytes 589832 | tf_op jit(solution)/shard_map/ppermute | solution.py:431
  53.4 12.4 %collective-permute-start.10 = (f32[1,240,128]{2,1,0:T(8,128)S(1)}, f32[1,240,128]{2,1,0:T(8,128)S(1)}, u32[]{:S(2)}, u32[]{:S(2)}) collective-permute-start(f32[1,240,128]{2,1,0:T(8,128)S(1)} %get-tuple-element.105), channel_id=1, source_target_pairs={{0,24},{4,28},{1,25},{5,29},{2,26},{6,30},{3,27},{7,31}} | collective-permute-start | bytes 368648 | tf_op jit(solution)/shard_map/ppermute | solution.py:501
  54.7 12.4 %collective-permute-start.6 = (f32[1,240,128]{2,1,0:T(8,128)S(1)}, f32[1,240,128]{2,1,0:T(8,128)S(1)}, u32[]{:S(2)}, u32[]{:S(2)}) collective-permute-start(f32[1,240,128]{2,1,0:T(8,128)S(1)} %get-tuple-element.101), channel_id=1, source_target_pairs={{0,8},{4,12},{8,16},{12,20},{16,24},{20,28},{1,9},{5,13},{9,17},{1... | collective-permute-start | bytes 368648 | tf_op jit(solution)/shard_map/ppermute | solution.py:501
  56.0 12.4 %collective-permute-start.7 = (f32[1,240,128]{2,1,0:T(8,128)S(1)}, f32[1,240,128]{2,1,0:T(8,128)S(1)}, u32[]{:S(2)}, u32[]{:S(2)}) collective-permute-start(f32[1,240,128]{2,1,0:T(8,128)S(1)} %get-tuple-element.102), channel_id=1, source_target_pairs={{0,12},{4,16},{8,20},{12,24},{16,28},{1,13},{5,17},{9,21},{13,25},... | collective-permute-start | bytes 368648 | tf_op jit(solution)/shard_map/ppermute | solution.py:501
  58.1 24.8 %collective-permute-start.8 = (f32[1,240,128]{2,1,0:T(8,128)S(1)}, f32[1,240,128]{2,1,0:T(8,128)S(1)}, u32[]{:S(2)}, u32[]{:S(2)}) collective-permute-start(f32[1,240,128]{2,1,0:T(8,128)S(1)} %get-tuple-element.103), channel_id=1, source_target_pairs={{0,16},{4,20},{8,24},{12,28},{1,17},{5,21},{9,25},{13,29},{2,18},{... | collective-permute-start | bytes 368648 | tf_op jit(solution)/shard_map/ppermute | solution.py:501
  59.4 24.8 %collective-permute-start.9 = (f32[1,240,128]{2,1,0:T(8,128)S(1)}, f32[1,240,128]{2,1,0:T(8,128)S(1)}, u32[]{:S(2)}, u32[]{:S(2)}) collective-permute-start(f32[1,240,128]{2,1,0:T(8,128)S(1)} %get-tuple-element.104), channel_id=1, source_target_pairs={{0,20},{4,24},{8,28},{1,21},{5,25},{9,29},{2,22},{6,26},{10,30},{3... | collective-permute-start | bytes 368648 | tf_op jit(solution)/shard_map/ppermute | solution.py:501
  65.8 19.7 %collective-permute-start.15 = (f32[1,240,128]{2,1,0:T(8,128)S(1)}, f32[1,240,128]{2,1,0:T(8,128)S(1)}, u32[]{:S(2)}, u32[]{:S(2)}) collective-permute-start(f32[1,240,128]{2,1,0:T(8,128)S(1)} %get-tuple-element.116), channel_id=1, source_target_pairs={{0,8},{4,12},{8,16},{12,20},{16,24},{20,28},{1,9},{5,13},{9,17},{1... | collective-permute-start | bytes 368648 | tf_op jit(solution)/shard_map/ppermute | solution.py:501
  67.1 19.7 %collective-permute-start.16 = (f32[1,240,128]{2,1,0:T(8,128)S(1)}, f32[1,240,128]{2,1,0:T(8,128)S(1)}, u32[]{:S(2)}, u32[]{:S(2)}) collective-permute-start(f32[1,240,128]{2,1,0:T(8,128)S(1)} %get-tuple-element.117), channel_id=1, source_target_pairs={{0,12},{4,16},{8,20},{12,24},{16,28},{1,13},{5,17},{9,21},{13,25},... | collective-permute-start | bytes 368648 | tf_op jit(solution)/shard_map/ppermute | solution.py:501
  68.5 37.8 %collective-permute-start.20 = (f32[2,432,128]{2,1,0:T(8,128)S(1)}, f32[2,432,128]{2,1,0:T(8,128)S(1)}, u32[]{:S(2)}, u32[]{:S(2)}) collective-permute-start(f32[2,432,128]{2,1,0:T(8,128)S(1)} %get-tuple-element.121), channel_id=1, source_target_pairs={{0,4},{4,8},{8,12},{12,16},{16,20},{20,24},{24,28},{1,5},{5,9},{9,... | collective-permute-start | bytes 1327112 | tf_op jit(solution)/shard_map/ppermute | solution.py:501
  82.9 23.4 %collective-permute-start.21 = (f32[1,576,128]{2,1,0:T(8,128)S(1)}, f32[1,576,128]{2,1,0:T(8,128)S(1)}, u32[]{:S(2)}, u32[]{:S(2)}) collective-permute-start(f32[1,576,128]{2,1,0:T(8,128)S(1)} %get-tuple-element.122), channel_id=1, source_target_pairs={{0,28},{1,29},{2,30},{3,31}} | collective-permute-start | bytes 884744 | tf_op jit(solution)/shard_map/ppermute | solution.py:501
  84.2 22.1 %collective-permute-start.17 = (f32[1,240,128]{2,1,0:T(8,128)S(1)}, f32[1,240,128]{2,1,0:T(8,128)S(1)}, u32[]{:S(2)}, u32[]{:S(2)}) collective-permute-start(f32[1,240,128]{2,1,0:T(8,128)S(1)} %get-tuple-element.118), channel_id=1, source_target_pairs={{0,16},{4,20},{8,24},{12,28},{1,17},{5,21},{9,25},{13,29},{2,18},{... | collective-permute-start | bytes 368648 | tf_op jit(solution)/shard_map/ppermute | solution.py:501
  85.5 20.8 %collective-permute-start.18 = (f32[1,240,128]{2,1,0:T(8,128)S(1)}, f32[1,240,128]{2,1,0:T(8,128)S(1)}, u32[]{:S(2)}, u32[]{:S(2)}) collective-permute-start(f32[1,240,128]{2,1,0:T(8,128)S(1)} %get-tuple-element.119), channel_id=1, source_target_pairs={{0,20},{4,24},{8,28},{1,21},{5,25},{9,29},{2,22},{6,26},{10,30},{3... | collective-permute-start | bytes 368648 | tf_op jit(solution)/shard_map/ppermute | solution.py:501
  86.8 19.5 %collective-permute-start.19 = (f32[1,240,128]{2,1,0:T(8,128)S(1)}, f32[1,240,128]{2,1,0:T(8,128)S(1)}, u32[]{:S(2)}, u32[]{:S(2)}) collective-permute-start(f32[1,240,128]{2,1,0:T(8,128)S(1)} %get-tuple-element.120), channel_id=1, source_target_pairs={{0,24},{4,28},{1,25},{5,29},{2,26},{6,30},{3,27},{7,31}} | collective-permute-start | bytes 368648 | tf_op jit(solution)/shard_map/ppermute | solution.py:501
  88.4 17.8 %copy-start.9 = (f32[12,32,512]{2,1,0:T(8,128)S(1)}, f32[12,32,512]{2,1,0:T(8,128)}, u32[]{:S(2)}) copy-start(f32[12,32,512]{2,1,0:T(8,128)} %get-tuple-element.188.base) | copy-start | bytes 2359300
  (9 other events, 41.1 us)

commit v3 on v2

--- a/solution.py
+++ b/solution.py
@@ -55,16 +55,20 @@
     return total
 
 
-def strip_body(est, observed, upper, lower):
+def strip_body(place_of, est, observed, pair, other):
     planes, rows, cols = est.shape
     reach = 2 * ROW_HALF
+    odd = (place_of[1] & 1) == 1
+
+    def put(begin, size, upper, lower):
+        pair[begin : begin + size, :] = jnp.where(odd, upper, lower)
+        other[begin : begin + size, :] = jnp.where(odd, lower, upper)
+
     for l in range(planes):
+        put(l * reach, reach, est[l, 0:reach, :], est[l, rows - reach : rows, :])
+        seen = observed[l].astype(F32)
         seek = (2 * planes + l) * ROW_HALF
-        upper[l * reach : (l + 1) * reach, :] = est[l, 0:reach, :]
-        lower[l * reach : (l + 1) * reach, :] = est[l, rows - reach : rows, :]
-        seen = observed[l].astype(F32)
-        upper[seek : seek + ROW_HALF, :] = seen[0:ROW_HALF]
-        lower[seek : seek + ROW_HALF, :] = seen[rows - ROW_HALF : rows]
+        put(seek, ROW_HALF, seen[0:ROW_HALF], seen[rows - ROW_HALF : rows])
 
 
 def own_body(est, weights, mixed, high_w, low_w):
@@ -76,15 +80,17 @@
     mixed[...] = product(x, high, low, ((1,), (0,))).reshape(planes, rows, cols)
 
 
-def rim_body(chunks, place_of, mixed, above, below, high_w, low_w, taps, tall, *refs):
+def rim_body(chunks, place_of, mixed, pair, other, high_w, low_w, taps, tall, *refs):
     rims, ends, edge = refs[:-2], refs[-2], refs[-1]
     odd = (place_of[0] & 1) == 1
     planes, rows, cols = mixed.shape
     reach = 2 * ROW_HALF
     ends[...] = jnp.zeros(ends.shape, F32)
+    odd_row = (place_of[1] & 1) == 1
     for l in range(planes):
-        ends[l, 0:reach, :] = above[l * reach : (l + 1) * reach, :]
-        ends[l, EDGE : EDGE + reach, :] = below[l * reach : (l + 1) * reach, :]
+        x, y = pair[l * reach : (l + 1) * reach, :], other[l * reach : (l + 1) * reach, :]
+        ends[l, 0:reach, :] = jnp.where(odd_row, x, y)
+        ends[l, EDGE : EDGE + reach, :] = jnp.where(odd_row, y, x)
     x = ends[...].reshape(planes * 2 * EDGE, cols)
     ends[...] = product(x, high_w[...], low_w[...], ((1,), (0,))).reshape(ends.shape)
     tall[:, 0:reach, :] = ends[:, 0:reach, :]
@@ -100,16 +106,18 @@
             rims[2 * i + 1][l] = jnp.where(odd, high, low)
 
 
-def frame_body(tall, observed, above, below, taps, blur, seen, frame):
+def frame_body(place_of, tall, observed, pair, other, taps, blur, seen, frame):
     planes, rows, cols = observed.shape
     for l in range(planes):
         blur[l] = skewed(row_sum(tall, l, rows + EDGE, taps, 1), PLANE_HALF + l)
     frame[...] = jnp.zeros(frame.shape, F32)
+    odd = (place_of[1] & 1) == 1
     for l in range(planes):
         seek = (2 * planes + l) * ROW_HALF
-        frame[0:ROW_HALF, :] = above[seek : seek + ROW_HALF, :]
+        x, y = pair[seek : seek + ROW_HALF, :], other[seek : seek + ROW_HALF, :]
+        frame[0:ROW_HALF, :] = jnp.where(odd, x, y)
         frame[ROW_HALF : ROW_HALF + rows, :] = observed[l].astype(F32)
-        frame[ROW_HALF + rows : 2 * ROW_HALF + rows, :] = below[seek : seek + ROW_HALF, :]
+        frame[ROW_HALF + rows : 2 * ROW_HALF + rows, :] = jnp.where(odd, y, x)
         seen[l] = skewed(frame[...], PLANE_HALF + l)
 
 
@@ -358,19 +366,9 @@
     place(sources, edges, me, fields_of([base], plan.part_rows), out, False, 0)
 
 
-def to_next(x, axis):
-    count = lax.axis_size(axis)
-    return lax.ppermute(x, axis, [(i, i + 1) for i in range(count - 1)])
-
-
-def to_last(x, axis):
-    count = lax.axis_size(axis)
-    return lax.ppermute(x, axis, [(i + 1, i) for i in range(count - 1)])
-
-
-def swaps(begin, count):
-    ends = [(i, i + 1) for i in range(begin, count - 1, 2)]
-    return ends + [(j, i) for i, j in ends]
+def swapped(x, axis, begin):
+    ends = [(i, i + 1) for i in range(begin, lax.axis_size(axis) - 1, 2)]
+    return lax.ppermute(x, axis, ends + [(j, i) for i, j in ends])
 
 
 def like(*shape):
@@ -381,15 +379,16 @@
     planes, rows, cols = estimate.shape
     count = lax.axis_size("scan")
     width = cols + LANES
-    half = rows // 2
+    half = rows * 4 // 64 * 8
     chunks = [(0, half), (half, rows)]
     fresh = [(begin + EDGE if begin else 0, end + EDGE) for begin, end in chunks]
     reach = 2 * ROW_HALF
 
     strip = like(3 * ROW_HALF * planes, cols)
-    upper, lower = run(strip_body, (strip, strip), [VMEM, VMEM], (estimate, observed))
-    above, below = to_next(lower, "lat"), to_last(upper, "lat")
-    me = lax.axis_index("scan").astype(jnp.int32)[None]
+    me = jnp.stack([lax.axis_index("scan"), lax.axis_index("lat")]).astype(jnp.int32)
+    pair, other = run(strip_body, (strip, strip), [SMEM, VMEM, VMEM], (me, estimate, observed))
+    below = swapped(other, "lat", 1)
+    above = swapped(pair, "lat", 0)
     levels = jnp.arange((count + 1) * planes, dtype=jnp.int32) - planes
     edges = jnp.sum(shear_planes[None, :] <= levels[:, None], axis=1, dtype=jnp.int32)
     turn = (shear_planes % planes)[None, :]
@@ -418,33 +417,37 @@
     blur, seen = run(
         frame_body,
         (framed, framed),
-        [VMEM, VMEM, VMEM, VMEM, SMEM],
-        (tall, observed, above, below, row_taps),
+        [SMEM, VMEM, VMEM, VMEM, VMEM, SMEM],
+        (me, tall, observed, above, below, row_taps),
         [pltpu.VMEM((rows + EDGE, cols), F32)],
     )
 
     def beside(pair, other):
-        last = lax.ppermute(other, "scan", swaps(1, count))
-        return lax.ppermute(pair, "scan", swaps(0, count)), last
+        last = swapped(other, "scan", 1)
+        return swapped(pair, "scan", 0), last
 
     def beside(pair, other):
-        last = lax.ppermute(other, "scan", swaps(1, count))
-        return lax.ppermute(pair, "scan", swaps(0, count)), last
+        last = swapped(other, "scan", 1)
+        return swapped(pair, "scan", 0), last
 
     def exchange(message):
         return lax.all_to_all(message, "scan", split_axis=0, concat_axis=0, tiled=True)
 
     share = max(cols // count, 8)
-    part_rows = 16 if half % 16 == 0 else 8
+    part_rows = 16 if half % 16 == 0 and rows % 16 == 0 else 8
 
     def packing(height, columns):
         parts = height // part_rows
         return Packing(planes, cols, parts, part_rows, min(-(-columns // 8) * 8, LANES))
 
     near, far = packing(rows, share * 9 // 8), packing(rows, share * 3 // 2)
-    middle = packing(half, share * 5 // 4)
     later = packing(rows, share // 4)
-    mid = [(middle, [(d, 0)], False) for d in range(2, count - 1)]
+    mids = []
+    for begin, end in chunks:
+        middle = packing(end - begin, share * 5 // 4)
+        middle_first = sorted(range(2, count - 1), key=lambda d: abs(2 * d - count - 1))
+        distances = middle_first if begin else range(2, count - 1)
+        mids.append([(middle, [(d, 0)], False) for d in distances])
     wide = [
         (near, [(1, 0), (1, near.width)], True),
         (far, [(count - 1, 0)], True),
@@ -476,12 +479,25 @@
             ],
         )
         if last:
+            heavy = [j for j, (_, ds, _) in enumerate(mids[0]) if abs(2 * ds[0][0] - count) == 2]
+            rest = [j for j in range(len(mids[0])) if j not in heavy]
+            low, high, early = lax.optimization_barrier((low, high, [moved[j] for j in heavy]))
             sides = beside(low, high)
+            sides, late = lax.optimization_barrier((sides, [moved[j] for j in rest]))
+            moved = [None] * len(mids[0])
+            for j, x in zip(heavy + rest, early + late):
+                moved[j] = x
+            settled = run(
+                functools.partial(settle_first, mids[0]),
+                like(planes, begin, cols),
+                [SMEM, SMEM] + [VMEM] * (1 + len(moved)),
+                (edges, me, pieces[0], *moved),
+            )
         else:
             ahead = lax.optimization_barrier((low, high, *rims[2 * i + 2 : 2 * i + 4]))
             sides = beside(*ahead[:2])
             left, right = beside(*ahead[2:])
-        sends = mid + wide if last else mid
+        sends = mids[i] + wide if last else mids[i]
         turned, *packed = run(
             functools.partial(update_body, sends, begin),
             (
@@ -501,13 +517,12 @@
             lax.ppermute(x, "scan", [(j, j + ds[0][0]) for j in range(count - ds[0][0])])
             for (_, ds, _), x in zip(sends, packed)
         ]
-        ready = (settled,) if last else ()
-        settled = run(
-            functools.partial(settle_last if last else settle_first, sends),
-            like(planes, end, cols),
-            [SMEM, SMEM] + [VMEM] * (1 + len(ready) + len(moved)),
-            (edges, me, *ready, turned, *moved),
-        )
+    settled = run(
+        functools.partial(settle_last, sends),
+        like(planes, rows, cols),
+        [SMEM, SMEM] + [VMEM] * (2 + len(moved)),
+        (edges, me, settled, turned, *moved),
+    )
 
     table = edges.reshape(count + 1, planes)
     row = lax.broadcasted_iota(jnp.int32, (count - 1, planes), 0)

time: 110 us -> 105 us (0.955)
  the two profiles are of different devices: /device:TPU:29 before, /device:TPU:21 now
where the time goes in v3:
time: 105 us; the launch traced here: 104 us
  starting transfers between devices  49.4 us (47%)
  Pallas kernels  26.1 us (25%)
  waiting for transfers between devices  23 us (22%)
  local copies, waits for them, and re-layouts  3.8 us (4%)
  other arithmetic  1.07 us (1%)
    ppermute x12, starting transfers between devices, on_device(): lax.ppermute(x, 'scan', [(j, j + ds[0][0]) for j in range(count - ds[0][0...  29.7 us
    pallas_call x10, Pallas kernels, run(): pl.pallas_call(body, out_shape=outs, in_specs=ins, out_specs=jax.tree.map...  26.1 us
    ppermute x10, starting transfers between devices, swapped(): return lax.ppermute(x, axis, ends + [(j, i) for i, j in ends])  19.8 us
    ppermute x10, waiting for transfers between devices, swapped(): return lax.ppermute(x, axis, ends + [(j, i) for i, j in ends])  12 us
    ppermute x12, waiting for transfers between devices, on_device(): lax.ppermute(x, 'scan', [(j, j + ds[0][0]) for j in range(count - ds[0][0...  11 us
    unnamed x22, local copies, waits for them, and re-layouts  3.72 us
  transfers between devices with their start and end apart: 22, of which 8 were waited for; matrix products, arithmetic and copies ran while one was open for 1% of the time, Pallas kernels for 13%

profile of v3, /device:TPU:21, one launch (start us, length us, event | category | flops | bytes accessed | tf_op | source)
XLA Modules:
  0.0 104.4 jit_solution(14699498848530114261)
XLA Ops:
  0.1 1.4 %copy-done = f32[12,64,512]{2,1,0:T(8,128)S(1)} copy-done((f32[12,64,512]{2,1,0:T(8,128)S(1)}, f32[12,64,512]{2,1,0:T(8,128)}, u32[]{:S(2)}) %copy-start) | copy-done | bytes 1572888
  4.0 3.0 %collective-permute-start.1 = (f32[108,512]{1,0:T(8,128)S(1)}, f32[108,512]{1,0:T(8,128)S(1)}, u32[]{:S(2)}, u32[]{:S(2)}) collective-permute-start(f32[108,512]{1,0:T(8,128)S(1)} %get-tuple-element.94), channel_id=1, source_target_pairs={{1,2},{2,1},{5,6},{6,5},{9,10},{10,9},{13,14},{14,13},{17,18},{18,... | collective-permute-start | bytes 663560 | tf_op jit(solution)/shard_map/ppermute | solution.py:371
  7.1 1.4 %shard_map.64 = (f32[12,64,512]{2,1,0:T(8,128)S(1)}, bf16[512,512]{1,0:T(8,128)(2,1)S(1)}, bf16[512,512]{1,0:T(8,128)(2,1)S(1)}) custom-call(f32[12,64,512]{2,1,0:T(8,128)S(1)} %copy-done, f32[512,512]{1,0:T(8,128)S(1)} %copy-done.4), custom_call_target="tpu_custom_call" | custom-call | tf_op jit(solution)/shard_map/pallas_call | solution.py:24
  8.5 3.1 %collective-permute-done.1.other = f32[108,512]{1,0:T(8,128)S(1)} collective-permute-done((f32[108,512]{1,0:T(8,128)S(1)}, f32[108,512]{1,0:T(8,128)S(1)}, u32[]{:S(2)}, u32[]{:S(2)}) %collective-permute-start.1) | collective-permute-done | bytes 221216 | tf_op jit(solution)/shard_map/ppermute | solution.py:371
  11.6 2.0 %shard_map.66 = (f32[12,80,512]{2,1,0:T(8,128)S(1)}, f32[3,40,512]{2,1,0:T(8,128)S(1)}, f32[3,40,512]{2,1,0:T(8,128)S(1)}, f32[3,32,512]{2,1,0:T(8,128)S(1)}, f32[3,32,512]{2,1,0:T(8,128)S(1)}) custom-call(s32[2]{0:T(128)S(1)} %pad_add_fusion.place_of, f32[12,64,512]{2,1,0:T(8,128)S(1)} %get-tuple-element.92.mixed, ...), custom_call_target="tpu_custom_call" | custom-call | tf_op jit(solution)/shard_map/pallas_call | solution.py:24
  13.9 4.1 %collective-permute-start.3 = (f32[3,40,512]{2,1,0:T(8,128)S(1)}, f32[3,40,512]{2,1,0:T(8,128)S(1)}, u32[]{:S(2)}, u32[]{:S(2)}) collective-permute-start(f32[3,40,512]{2,1,0:T(8,128)S(1)} %get-tuple-element.101), channel_id=1, source_target_pairs={{4,8},{12,16},{20,24},{8,4},{16,12},{24,20},{5,9},{13,17},{21,25},... | collective-permute-start | bytes 737288 | tf_op jit(solution)/shard_map/ppermute | solution.py:371
  18.2 2.7 %shard_map.67 = (f32[12,72,640]{2,1,0:T(8,128)S(1)}, f32[12,72,640]{2,1,0:T(8,128)S(1)}) custom-call(s32[2]{0:T(128)S(1)} %pad_add_fusion.place_of, f32[12,80,512]{2,1,0:T(8,128)S(1)} %get-tuple-element.97.tall, bf16[12,64,512]{2,1,0:T(8,128)(2,1)S(1)} %copy-done.3, f32[108,512]{1,0:T(8,128)S(1)} %collective-permute-done.pair, ...), custom_call_target="tpu_custom_call" | custom-call | tf_op jit(solution)/shard_map/pallas_call | solution.py:24
  20.9 1.5 %collective-permute-done.2.left = f32[3,40,512]{2,1,0:T(8,128)S(1)} collective-permute-done((f32[3,40,512]{2,1,0:T(8,128)S(1)}, f32[3,40,512]{2,1,0:T(8,128)S(1)}, u32[]{:S(2)}, u32[]{:S(2)}) %collective-permute-start.2) | collective-permute-done | bytes 245792 | tf_op jit(solution)/shard_map/ppermute | solution.py:371
  22.4 3.5 %shard_map.68 = (f32[12,32,640]{2,1,0:T(8,128)S(1)}, f32[3,32,512]{2,1,0:T(8,128)S(1)}, f32[3,32,512]{2,1,0:T(8,128)S(1)}, f32[12,8,640]{2,1,0:T(8,128)S(1)}) custom-call(s32[2]{0:T(128)S(1)} %pad_add_fusion.place_of, f32[12,72,640]{2,1,0:T(8,128)S(1)} %get-tuple-element.98.blur, f32[12,72,640]{2,1,0:T(8,128)S(1)} %get-tuple-element.99.seen, ...), custom_call_target="tpu_custom_call" | custom-call | tf_op jit(solution)/shard_map/pallas_call | solution.py:24
  27.2 2.9 %collective-permute-start.7 = (f32[3,32,512]{2,1,0:T(8,128)S(1)}, f32[3,32,512]{2,1,0:T(8,128)S(1)}, u32[]{:S(2)}, u32[]{:S(2)}) collective-permute-start(f32[3,32,512]{2,1,0:T(8,128)S(1)} %get-tuple-element.110), channel_id=1, source_target_pairs={{4,8},{12,16},{20,24},{8,4},{16,12},{24,20},{5,9},{13,17},{21,25},... | collective-permute-start | bytes 589832 | tf_op jit(solution)/shard_map/ppermute | solution.py:371
  30.5 2.9 %collective-permute-start.5 = (f32[3,32,512]{2,1,0:T(8,128)S(1)}, f32[3,32,512]{2,1,0:T(8,128)S(1)}, u32[]{:S(2)}, u32[]{:S(2)}) collective-permute-start(f32[3,32,512]{2,1,0:T(8,128)S(1)} %get-tuple-element.107), channel_id=1, source_target_pairs={{4,8},{12,16},{20,24},{8,4},{16,12},{24,20},{5,9},{13,17},{21,25},... | collective-permute-start | bytes 589832 | tf_op jit(solution)/shard_map/ppermute | solution.py:371
  33.7 7.3 %collective-permute-done.6.left = f32[3,32,512]{2,1,0:T(8,128)S(1)} collective-permute-done((f32[3,32,512]{2,1,0:T(8,128)S(1)}, f32[3,32,512]{2,1,0:T(8,128)S(1)}, u32[]{:S(2)}, u32[]{:S(2)}) %collective-permute-start.6) | collective-permute-done | bytes 196640 | tf_op jit(solution)/shard_map/ppermute | solution.py:371
  41.0 3.9 %shard_map.69 = (f32[12,32,512]{2,1,0:T(8,128)S(1)}, f32[1,240,128]{2,1,0:T(8,128)S(1)}, f32[1,240,128]{2,1,0:T(8,128)S(1)}, f32[1,240,128]{2,1,0:T(8,128)S(1)},...) custom-call(s32[108]{0:T(128)S(1)} %convert_reduce_fusion.edges, s32[2]{0:T(128)S(1)} %pad_add_fusion.place_of, ...), custom_call_target="tpu_custom_call" | custom-call | tf_op jit(solution)/shard_map/pallas_call | solution.py:24
  47.6 3.9 %shard_map.70 = (f32[12,32,640]{2,1,0:T(8,128)S(1)}, f32[3,32,512]{2,1,0:T(8,128)S(1)}, f32[3,32,512]{2,1,0:T(8,128)S(1)}, f32[12,8,640]{2,1,0:T(8,128)}) custom-call(s32[2]{0:T(128)S(1)} %pad_add_fusion.place_of, f32[12,72,640]{2,1,0:T(8,128)S(1)} %get-tuple-element.98.blur, f32[12,72,640]{2,1,0:T(8,128)S(1)} %get-tuple-element.99.seen, ...), custom_call_target="tpu_custom_call" | custom-call | tf_op jit(solution)/shard_map/pallas_call | solution.py:24
  51.6 3.1 %collective-permute-done.9.refs_3_ = f32[1,240,128]{2,1,0:T(8,128)S(1)} collective-permute-done((f32[1,240,128]{2,1,0:T(8,128)S(1)}, f32[1,240,128]{2,1,0:T(8,128)S(1)}, u32[]{:S(2)}, u32[]{:S(2)}) %collective-permute-start.9) | collective-permute-done | bytes 122912 | tf_op jit(solution)/shard_map/ppermute | solution.py:517
  54.7 4.0 %collective-permute-start.11 = (f32[3,32,512]{2,1,0:T(8,128)S(1)}, f32[3,32,512]{2,1,0:T(8,128)S(1)}, u32[]{:S(2)}, u32[]{:S(2)}) collective-permute-start(f32[3,32,512]{2,1,0:T(8,128)S(1)} %get-tuple-element.121), channel_id=1, source_target_pairs={{4,8},{12,16},{20,24},{8,4},{16,12},{24,20},{5,9},{13,17},{21,25},... | collective-permute-start | bytes 589832 | tf_op jit(solution)/shard_map/ppermute | solution.py:371
  58.7 1.9 %collective-permute-start.12 = (f32[1,240,128]{2,1,0:T(8,128)S(1)}, f32[1,240,128]{2,1,0:T(8,128)S(1)}, u32[]{:S(2)}, u32[]{:S(2)}) collective-permute-start(f32[1,240,128]{2,1,0:T(8,128)S(1)} %get-tuple-element.122), channel_id=1, source_target_pairs={{0,8},{4,12},{8,16},{12,20},{16,24},{20,28},{1,9},{5,13},{9,17},{1... | collective-permute-start | bytes 368648 | tf_op jit(solution)/shard_map/ppermute | solution.py:517
  62.6 2.5 %collective-permute-done.12.refs_0_ = f32[1,240,128]{2,1,0:T(8,128)S(1)} collective-permute-done((f32[1,240,128]{2,1,0:T(8,128)S(1)}, f32[1,240,128]{2,1,0:T(8,128)S(1)}, u32[]{:S(2)}, u32[]{:S(2)}) %collective-permute-start.12) | collective-permute-done | bytes 122912 | tf_op jit(solution)/shard_map/ppermute | solution.py:517
  65.1 2.1 %collective-permute-done.13.refs_2_ = f32[1,240,128]{2,1,0:T(8,128)S(1)} collective-permute-done((f32[1,240,128]{2,1,0:T(8,128)S(1)}, f32[1,240,128]{2,1,0:T(8,128)S(1)}, u32[]{:S(2)}, u32[]{:S(2)}) %collective-permute-start.13) | collective-permute-done | bytes 122912 | tf_op jit(solution)/shard_map/ppermute | solution.py:517
  67.2 5.2 %shard_map.72 = (f32[12,32,512]{2,1,0:T(8,128)}, f32[1,240,128]{2,1,0:T(8,128)S(1)}, f32[1,240,128]{2,1,0:T(8,128)S(1)}, f32[1,240,128]{2,1,0:T(8,128)S(1)}, f32...) custom-call(s32[108]{0:T(128)S(1)} %convert_reduce_fusion.edges, ...), custom_call_target="tpu_custom_call" | custom-call | tf_op jit(solution)/shard_map/pallas_call | solution.py:24
  75.0 4.5 %collective-permute-start.20 = (f32[2,432,128]{2,1,0:T(8,128)S(1)}, f32[2,432,128]{2,1,0:T(8,128)S(1)}, u32[]{:S(2)}, u32[]{:S(2)}) collective-permute-start(f32[2,432,128]{2,1,0:T(8,128)S(1)} %get-tuple-element.139), channel_id=1, source_target_pairs={{0,4},{4,8},{8,12},{12,16},{16,20},{20,24},{24,28},{1,5},{5,9},{9,... | collective-permute-start | bytes 1327112 | tf_op jit(solution)/shard_map/ppermute | solution.py:517
  82.2 13.4 %collective-permute-start.19 = (f32[1,240,128]{2,1,0:T(8,128)S(1)}, f32[1,240,128]{2,1,0:T(8,128)S(1)}, u32[]{:S(2)}, u32[]{:S(2)}) collective-permute-start(f32[1,240,128]{2,1,0:T(8,128)S(1)} %get-tuple-element.138), channel_id=1, source_target_pairs={{0,8},{4,12},{8,16},{12,20},{16,24},{20,28},{1,9},{5,13},{9,17},{1... | collective-permute-start | bytes 368648 | tf_op jit(solution)/shard_map/ppermute | solution.py:517
  96.6 1.5 %shard_map.71.settled = f32[12,32,512]{2,1,0:T(8,128)S(1)} custom-call(s32[108]{0:T(128)S(1)} %convert_reduce_fusion.edges, s32[2]{0:T(128)S(1)} %pad_add_fusion.place_of, f32[12,32,512]{2,1,0:T(8,128)} %copy-done.8, f32[1,240,128]{2,1,0:T(8,128)S(1)} %collective-permute-done.12.refs_0_, f32[1,240,128]{2,1,0:T(8,128)S(1)} %collective-permute-done.8.refs_1_, ...), custom_call_target="tpu_custom_call" | custom-call | tf_op jit(solution)/shard_map/pallas_call | solution.py:24
  98.1 3.2 %collective-permute-done.19.refs_4_ = f32[1,240,128]{2,1,0:T(8,128)S(1)} collective-permute-done((f32[1,240,128]{2,1,0:T(8,128)S(1)}, f32[1,240,128]{2,1,0:T(8,128)S(1)}, u32[]{:S(2)}, u32[]{:S(2)}) %collective-permute-start.19) | collective-permute-done | bytes 122912 | tf_op jit(solution)/shard_map/ppermute | solution.py:517
  (62 shorter events, 18.6 us)
Async XLA Ops:
  3.3 5.2 %collective-permute-start = (f32[108,512]{1,0:T(8,128)S(1)}, f32[108,512]{1,0:T(8,128)S(1)}, u32[]{:S(2)}, u32[]{:S(2)}) collective-permute-start(f32[108,512]{1,0:T(8,128)S(1)} %get-tuple-element.93), channel_id=1, source_target_pairs={{0,1},{2,3},{1,0},{3,2},{4,5},{6,7},{5,4},{7,6},{8,9},{10,11},{9,8... | collective-permute-start | bytes 663560 | tf_op jit(solution)/shard_map/ppermute | solution.py:371
  4.0 7.6 %collective-permute-start.1 = (f32[108,512]{1,0:T(8,128)S(1)}, f32[108,512]{1,0:T(8,128)S(1)}, u32[]{:S(2)}, u32[]{:S(2)}) collective-permute-start(f32[108,512]{1,0:T(8,128)S(1)} %get-tuple-element.94), channel_id=1, source_target_pairs={{1,2},{2,1},{5,6},{6,5},{9,10},{10,9},{13,14},{14,13},{17,18},{18,... | collective-permute-start | bytes 663560 | tf_op jit(solution)/shard_map/ppermute | solution.py:371
  13.7 8.7 %collective-permute-start.2 = (f32[3,40,512]{2,1,0:T(8,128)S(1)}, f32[3,40,512]{2,1,0:T(8,128)S(1)}, u32[]{:S(2)}, u32[]{:S(2)}) collective-permute-start(f32[3,40,512]{2,1,0:T(8,128)S(1)} %get-tuple-element.100), channel_id=1, source_target_pairs={{0,4},{8,12},{16,20},{24,28},{4,0},{12,8},{20,16},{28,24},{1,5},{9... | collective-permute-start | bytes 737288 | tf_op jit(solution)/shard_map/ppermute | solution.py:371
  13.9 8.4 %collective-permute-start.3 = (f32[3,40,512]{2,1,0:T(8,128)S(1)}, f32[3,40,512]{2,1,0:T(8,128)S(1)}, u32[]{:S(2)}, u32[]{:S(2)}) collective-permute-start(f32[3,40,512]{2,1,0:T(8,128)S(1)} %get-tuple-element.101), channel_id=1, source_target_pairs={{4,8},{12,16},{20,24},{8,4},{16,12},{24,20},{5,9},{13,17},{21,25},... | collective-permute-start | bytes 737288 | tf_op jit(solution)/shard_map/ppermute | solution.py:371
  22.3 18.7 %copy-start.1 = (f32[12,64,512]{2,1,0:T(8,128)S(1)}, f32[12,64,512]{2,1,0:T(8,128)}, u32[]{:S(2)}) copy-start(f32[12,64,512]{2,1,0:T(8,128)} %est.7) | copy-start | bytes 4718596
  25.9 15.1 %collective-permute-start.6 = (f32[3,32,512]{2,1,0:T(8,128)S(1)}, f32[3,32,512]{2,1,0:T(8,128)S(1)}, u32[]{:S(2)}, u32[]{:S(2)}) collective-permute-start(f32[3,32,512]{2,1,0:T(8,128)S(1)} %get-tuple-element.109), channel_id=1, source_target_pairs={{0,4},{8,12},{16,20},{24,28},{4,0},{12,8},{20,16},{28,24},{1,5},{9... | collective-permute-start | bytes 589832 | tf_op jit(solution)/shard_map/ppermute | solution.py:371
  27.2 13.8 %collective-permute-start.7 = (f32[3,32,512]{2,1,0:T(8,128)S(1)}, f32[3,32,512]{2,1,0:T(8,128)S(1)}, u32[]{:S(2)}, u32[]{:S(2)}) collective-permute-start(f32[3,32,512]{2,1,0:T(8,128)S(1)} %get-tuple-element.110), channel_id=1, source_target_pairs={{4,8},{12,16},{20,24},{8,4},{16,12},{24,20},{5,9},{13,17},{21,25},... | collective-permute-start | bytes 589832 | tf_op jit(solution)/shard_map/ppermute | solution.py:371
  30.2 17.4 %collective-permute-start.4 = (f32[3,32,512]{2,1,0:T(8,128)S(1)}, f32[3,32,512]{2,1,0:T(8,128)S(1)}, u32[]{:S(2)}, u32[]{:S(2)}) collective-permute-start(f32[3,32,512]{2,1,0:T(8,128)S(1)} %get-tuple-element.106), channel_id=1, source_target_pairs={{0,4},{8,12},{16,20},{24,28},{4,0},{12,8},{20,16},{28,24},{1,5},{9... | collective-permute-start | bytes 589832 | tf_op jit(solution)/shard_map/ppermute | solution.py:371
  30.5 17.0 %collective-permute-start.5 = (f32[3,32,512]{2,1,0:T(8,128)S(1)}, f32[3,32,512]{2,1,0:T(8,128)S(1)}, u32[]{:S(2)}, u32[]{:S(2)}) collective-permute-start(f32[3,32,512]{2,1,0:T(8,128)S(1)} %get-tuple-element.107), channel_id=1, source_target_pairs={{4,8},{12,16},{20,24},{8,4},{16,12},{24,20},{5,9},{13,17},{21,25},... | collective-permute-start | bytes 589832 | tf_op jit(solution)/shard_map/ppermute | solution.py:371
  44.9 22.3 %copy-start.8 = (f32[12,32,512]{2,1,0:T(8,128)}, f32[12,32,512]{2,1,0:T(8,128)S(1)}, u32[]{:S(2)}) copy-start(f32[12,32,512]{2,1,0:T(8,128)S(1)} %get-tuple-element.205.base.refs_0_) | copy-start | bytes 2359300
  44.9 6.6 %collective-permute-start.8 = (f32[1,240,128]{2,1,0:T(8,128)S(1)}, f32[1,240,128]{2,1,0:T(8,128)S(1)}, u32[]{:S(2)}, u32[]{:S(2)}) collective-permute-start(f32[1,240,128]{2,1,0:T(8,128)S(1)} %get-tuple-element.118), channel_id=1, source_target_pairs={{0,12},{4,16},{8,20},{12,24},{16,28},{1,13},{5,17},{9,21},{13,25},... | collective-permute-start | bytes 368648 | tf_op jit(solution)/shard_map/ppermute | solution.py:517
  46.2 8.4 %collective-permute-start.9 = (f32[1,240,128]{2,1,0:T(8,128)S(1)}, f32[1,240,128]{2,1,0:T(8,128)S(1)}, u32[]{:S(2)}, u32[]{:S(2)}) collective-permute-start(f32[1,240,128]{2,1,0:T(8,128)S(1)} %get-tuple-element.119), channel_id=1, source_target_pairs={{0,20},{4,24},{8,28},{1,21},{5,25},{9,29},{2,22},{6,26},{10,30},{3... | collective-permute-start | bytes 368648 | tf_op jit(solution)/shard_map/ppermute | solution.py:517
  54.7 12.6 %collective-permute-start.10 = (f32[3,32,512]{2,1,0:T(8,128)S(1)}, f32[3,32,512]{2,1,0:T(8,128)S(1)}, u32[]{:S(2)}, u32[]{:S(2)}) collective-permute-start(f32[3,32,512]{2,1,0:T(8,128)S(1)} %get-tuple-element.120), channel_id=1, source_target_pairs={{0,4},{8,12},{16,20},{24,28},{4,0},{12,8},{20,16},{28,24},{1,5},{9... | collective-permute-start | bytes 589832 | tf_op jit(solution)/shard_map/ppermute | solution.py:371
  54.7 12.6 %collective-permute-start.11 = (f32[3,32,512]{2,1,0:T(8,128)S(1)}, f32[3,32,512]{2,1,0:T(8,128)S(1)}, u32[]{:S(2)}, u32[]{:S(2)}) collective-permute-start(f32[3,32,512]{2,1,0:T(8,128)S(1)} %get-tuple-element.121), channel_id=1, source_target_pairs={{4,8},{12,16},{20,24},{8,4},{16,12},{24,20},{5,9},{13,17},{21,25},... | collective-permute-start | bytes 589832 | tf_op jit(solution)/shard_map/ppermute | solution.py:371
  58.7 6.4 %collective-permute-start.12 = (f32[1,240,128]{2,1,0:T(8,128)S(1)}, f32[1,240,128]{2,1,0:T(8,128)S(1)}, u32[]{:S(2)}, u32[]{:S(2)}) collective-permute-start(f32[1,240,128]{2,1,0:T(8,128)S(1)} %get-tuple-element.122), channel_id=1, source_target_pairs={{0,8},{4,12},{8,16},{12,20},{16,24},{20,28},{1,9},{5,13},{9,17},{1... | collective-permute-start | bytes 368648 | tf_op jit(solution)/shard_map/ppermute | solution.py:517
  60.6 6.6 %collective-permute-start.13 = (f32[1,240,128]{2,1,0:T(8,128)S(1)}, f32[1,240,128]{2,1,0:T(8,128)S(1)}, u32[]{:S(2)}, u32[]{:S(2)}) collective-permute-start(f32[1,240,128]{2,1,0:T(8,128)S(1)} %get-tuple-element.123), channel_id=1, source_target_pairs={{0,16},{4,20},{8,24},{12,28},{1,17},{5,21},{9,25},{13,29},{2,18},{... | collective-permute-start | bytes 368648 | tf_op jit(solution)/shard_map/ppermute | solution.py:517
  61.9 5.3 %collective-permute-start.14 = (f32[1,240,128]{2,1,0:T(8,128)S(1)}, f32[1,240,128]{2,1,0:T(8,128)S(1)}, u32[]{:S(2)}, u32[]{:S(2)}) collective-permute-start(f32[1,240,128]{2,1,0:T(8,128)S(1)} %get-tuple-element.124), channel_id=1, source_target_pairs={{0,24},{4,28},{1,25},{5,29},{2,26},{6,30},{3,27},{7,31}} | collective-permute-start | bytes 368648 | tf_op jit(solution)/shard_map/ppermute | solution.py:517
  72.4 9.1 %collective-permute-start.15 = (f32[1,240,128]{2,1,0:T(8,128)S(1)}, f32[1,240,128]{2,1,0:T(8,128)S(1)}, u32[]{:S(2)}, u32[]{:S(2)}) collective-permute-start(f32[1,240,128]{2,1,0:T(8,128)S(1)} %get-tuple-element.134), channel_id=1, source_target_pairs={{0,16},{4,20},{8,24},{12,28},{1,17},{5,21},{9,25},{13,29},{2,18},{... | collective-permute-start | bytes 368648 | tf_op jit(solution)/shard_map/ppermute | solution.py:517
  73.7 8.5 %collective-permute-start.16 = (f32[1,240,128]{2,1,0:T(8,128)S(1)}, f32[1,240,128]{2,1,0:T(8,128)S(1)}, u32[]{:S(2)}, u32[]{:S(2)}) collective-permute-start(f32[1,240,128]{2,1,0:T(8,128)S(1)} %get-tuple-element.135), channel_id=1, source_target_pairs={{0,20},{4,24},{8,28},{1,21},{5,25},{9,29},{2,22},{6,26},{10,30},{3... | collective-permute-start | bytes 368648 | tf_op jit(solution)/shard_map/ppermute | solution.py:517
  75.0 26.3 %collective-permute-start.20 = (f32[2,432,128]{2,1,0:T(8,128)S(1)}, f32[2,432,128]{2,1,0:T(8,128)S(1)}, u32[]{:S(2)}, u32[]{:S(2)}) collective-permute-start(f32[2,432,128]{2,1,0:T(8,128)S(1)} %get-tuple-element.139), channel_id=1, source_target_pairs={{0,4},{4,8},{8,12},{12,16},{16,20},{20,24},{24,28},{1,5},{5,9},{9,... | collective-permute-start | bytes 1327112 | tf_op jit(solution)/shard_map/ppermute | solution.py:517
  79.6 21.8 %collective-permute-start.21 = (f32[1,576,128]{2,1,0:T(8,128)S(1)}, f32[1,576,128]{2,1,0:T(8,128)S(1)}, u32[]{:S(2)}, u32[]{:S(2)}) collective-permute-start(f32[1,576,128]{2,1,0:T(8,128)S(1)} %get-tuple-element.140), channel_id=1, source_target_pairs={{0,28},{1,29},{2,30},{3,31}} | collective-permute-start | bytes 884744 | tf_op jit(solution)/shard_map/ppermute | solution.py:517
  80.2 17.9 %collective-permute-start.17 = (f32[1,240,128]{2,1,0:T(8,128)S(1)}, f32[1,240,128]{2,1,0:T(8,128)S(1)}, u32[]{:S(2)}, u32[]{:S(2)}) collective-permute-start(f32[1,240,128]{2,1,0:T(8,128)S(1)} %get-tuple-element.136), channel_id=1, source_target_pairs={{0,12},{4,16},{8,20},{12,24},{16,28},{1,13},{5,17},{9,21},{13,25},... | collective-permute-start | bytes 368648 | tf_op jit(solution)/shard_map/ppermute | solution.py:517
  81.6 16.6 %collective-permute-start.18 = (f32[1,240,128]{2,1,0:T(8,128)S(1)}, f32[1,240,128]{2,1,0:T(8,128)S(1)}, u32[]{:S(2)}, u32[]{:S(2)}) collective-permute-start(f32[1,240,128]{2,1,0:T(8,128)S(1)} %get-tuple-element.137), channel_id=1, source_target_pairs={{0,24},{4,28},{1,25},{5,29},{2,26},{6,30},{3,27},{7,31}} | collective-permute-start | bytes 368648 | tf_op jit(solution)/shard_map/ppermute | solution.py:517
  82.2 19.1 %collective-permute-start.19 = (f32[1,240,128]{2,1,0:T(8,128)S(1)}, f32[1,240,128]{2,1,0:T(8,128)S(1)}, u32[]{:S(2)}, u32[]{:S(2)}) collective-permute-start(f32[1,240,128]{2,1,0:T(8,128)S(1)} %get-tuple-element.138), channel_id=1, source_target_pairs={{0,8},{4,12},{8,16},{12,20},{16,24},{20,28},{1,9},{5,13},{9,17},{1... | collective-permute-start | bytes 368648 | tf_op jit(solution)/shard_map/ppermute | solution.py:517
  (9 other events, 45.4 us)

commit v4 on v3

--- a/solution.py
+++ b/solution.py
@@ -176,13 +176,13 @@
             ] / jnp.where(blurred > 0, blurred, 1.0)
             return 0
 
-        lax.fori_loop(0, (size + EDGE - fresh) // 8, tile, 0)
+        lax.fori_loop(0, (size + EDGE - fresh) // 8, tile, 0, unroll=True)
 
     def sum_rows(p, _):
         spread[p] = row_sum(ratio, p, size, row_taps, -1)
         return 0
 
-    lax.fori_loop(0, planes, sum_rows, 0)
+    lax.fori_loop(0, planes, sum_rows, 0, unroll=2)
     tail[...] = ratio[:, size : size + EDGE, :]
     for l in range(PLANE_HALF):
         low = unskewed(spread[l], PLANE_HALF + l)
@@ -207,7 +207,7 @@
             wide[pl.ds(row, 8), :] = plane_sum(spread, row, sides, row, l, planes, taps, -1)
             return 0
 
-        lax.fori_loop(0, rows // 8, tile, 0)
+        lax.fori_loop(0, rows // 8, tile, 0, unroll=True)
         back[l] = unskewed(wide[...], PLANE_HALF + l)
     x = back[...].reshape(planes * rows, cols)
     y = product(x, high_w[...], low_w[...], ((1,), (1,)))
@@ -230,7 +230,7 @@
                 turned[(q, *here)] = field[q]
         return 0
 
-    lax.fori_loop(0, rows // 8, rotate, 0)
+    lax.fori_loop(0, rows // 8, rotate, 0, unroll=2)
     for (plan, ds, whole), out in zip(sends, outs):
         fields = fields_of(before + [turned] if whole else [turned], plan.part_rows)
         for i, (d, skip) in enumerate(ds):
@@ -479,7 +479,7 @@
             ],
         )
         if last:
-            heavy = [j for j, (_, ds, _) in enumerate(mids[0]) if abs(2 * ds[0][0] - count) == 2]
+            heavy = [j for j, (_, ds, _) in enumerate(mids[0]) if abs(2 * ds[0][0] - count - 1) == 1]
             rest = [j for j in range(len(mids[0])) if j not in heavy]
             low, high, early = lax.optimization_barrier((low, high, [moved[j] for j in heavy]))
             sides = beside(low, high)

time: 105 us -> 103 us (0.981)
  the two profiles are of different devices: /device:TPU:21 before, /device:TPU:29 now
where the time goes in v4:
time: 103 us; the launch traced here: 102 us
  waiting for transfers between devices  47.3 us (46%)
  starting transfers between devices  27 us (26%)
  Pallas kernels  21.4 us (21%)
  local copies, waits for them, and re-layouts  3.8 us (4%)
  other arithmetic  1.07 us (1%)
    ppermute x12, waiting for transfers between devices, on_device(): lax.ppermute(x, 'scan', [(j, j + ds[0][0]) for j in range(count - ds[0][0...  32 us
    pallas_call x10, Pallas kernels, run(): pl.pallas_call(body, out_shape=outs, in_specs=ins, out_specs=jax.tree.map...  21.4 us
    ppermute x12, starting transfers between devices, on_device(): lax.ppermute(x, 'scan', [(j, j + ds[0][0]) for j in range(count - ds[0][0...  15.6 us
    ppermute x10, waiting for transfers between devices, swapped(): return lax.ppermute(x, axis, ends + [(j, i) for i, j in ends])  15.2 us
    ppermute x10, starting transfers between devices, swapped(): return lax.ppermute(x, axis, ends + [(j, i) for i, j in ends])  11.4 us
    unnamed x22, local copies, waits for them, and re-layouts  3.72 us
  transfers between devices with their start and end apart: 22, of which 11 were waited for; matrix products, arithmetic and copies ran while one was open for 1% of the time, Pallas kernels for 11%

profile of v4, /device:TPU:29, one launch (start us, length us, event | category | flops | bytes accessed | tf_op | source)
XLA Modules:
  0.0 101.5 jit_solution(15767613423198988553)
XLA Ops:
  0.1 1.4 %copy-done = f32[12,64,512]{2,1,0:T(8,128)S(1)} copy-done((f32[12,64,512]{2,1,0:T(8,128)S(1)}, f32[12,64,512]{2,1,0:T(8,128)}, u32[]{:S(2)}) %copy-start) | copy-done | bytes 1572888
  4.0 3.0 %collective-permute-start.1 = (f32[108,512]{1,0:T(8,128)S(1)}, f32[108,512]{1,0:T(8,128)S(1)}, u32[]{:S(2)}, u32[]{:S(2)}) collective-permute-start(f32[108,512]{1,0:T(8,128)S(1)} %get-tuple-element.94), channel_id=1, source_target_pairs={{1,2},{2,1},{5,6},{6,5},{9,10},{10,9},{13,14},{14,13},{17,18},{18,... | collective-permute-start | bytes 663560 | tf_op jit(solution)/shard_map/ppermute | solution.py:371
  7.1 1.4 %shard_map.64 = (f32[12,64,512]{2,1,0:T(8,128)S(1)}, bf16[512,512]{1,0:T(8,128)(2,1)S(1)}, bf16[512,512]{1,0:T(8,128)(2,1)S(1)}) custom-call(f32[12,64,512]{2,1,0:T(8,128)S(1)} %copy-done, f32[512,512]{1,0:T(8,128)S(1)} %copy-done.4), custom_call_target="tpu_custom_call" | custom-call | tf_op jit(solution)/shard_map/pallas_call | solution.py:24
  8.5 3.1 %collective-permute-done.1.other = f32[108,512]{1,0:T(8,128)S(1)} collective-permute-done((f32[108,512]{1,0:T(8,128)S(1)}, f32[108,512]{1,0:T(8,128)S(1)}, u32[]{:S(2)}, u32[]{:S(2)}) %collective-permute-start.1) | collective-permute-done | bytes 221216 | tf_op jit(solution)/shard_map/ppermute | solution.py:371
  11.6 2.0 %shard_map.66 = (f32[12,80,512]{2,1,0:T(8,128)S(1)}, f32[3,40,512]{2,1,0:T(8,128)S(1)}, f32[3,40,512]{2,1,0:T(8,128)S(1)}, f32[3,32,512]{2,1,0:T(8,128)S(1)}, f32[3,32,512]{2,1,0:T(8,128)S(1)}) custom-call(s32[2]{0:T(128)S(1)} %pad_add_fusion.place_of, f32[12,64,512]{2,1,0:T(8,128)S(1)} %get-tuple-element.92.mixed, ...), custom_call_target="tpu_custom_call" | custom-call | tf_op jit(solution)/shard_map/pallas_call | solution.py:24
  14.7 2.7 %shard_map.67 = (f32[12,72,640]{2,1,0:T(8,128)S(1)}, f32[12,72,640]{2,1,0:T(8,128)S(1)}) custom-call(s32[2]{0:T(128)S(1)} %pad_add_fusion.place_of, f32[12,80,512]{2,1,0:T(8,128)S(1)} %get-tuple-element.97.tall, bf16[12,64,512]{2,1,0:T(8,128)(2,1)S(1)} %copy-done.3, f32[108,512]{1,0:T(8,128)S(1)} %collective-permute-done.pair, ...), custom_call_target="tpu_custom_call" | custom-call | tf_op jit(solution)/shard_map/pallas_call | solution.py:24
  17.4 4.3 %collective-permute-done.2.left = f32[3,40,512]{2,1,0:T(8,128)S(1)} collective-permute-done((f32[3,40,512]{2,1,0:T(8,128)S(1)}, f32[3,40,512]{2,1,0:T(8,128)S(1)}, u32[]{:S(2)}, u32[]{:S(2)}) %collective-permute-start.2) | collective-permute-done | bytes 245792 | tf_op jit(solution)/shard_map/ppermute | solution.py:371
  21.7 2.6 %shard_map.68 = (f32[12,32,640]{2,1,0:T(8,128)S(1)}, f32[3,32,512]{2,1,0:T(8,128)S(1)}, f32[3,32,512]{2,1,0:T(8,128)S(1)}, f32[12,8,640]{2,1,0:T(8,128)S(1)}) custom-call(s32[2]{0:T(128)S(1)} %pad_add_fusion.place_of, f32[12,72,640]{2,1,0:T(8,128)S(1)} %get-tuple-element.98.blur, f32[12,72,640]{2,1,0:T(8,128)S(1)} %get-tuple-element.99.seen, ...), custom_call_target="tpu_custom_call" | custom-call | tf_op jit(solution)/shard_map/pallas_call | solution.py:24
  24.3 2.0 %collective-permute-start.6 = (f32[3,32,512]{2,1,0:T(8,128)S(1)}, f32[3,32,512]{2,1,0:T(8,128)S(1)}, u32[]{:S(2)}, u32[]{:S(2)}) collective-permute-start(f32[3,32,512]{2,1,0:T(8,128)S(1)} %get-tuple-element.109), channel_id=1, source_target_pairs={{0,4},{8,12},{16,20},{24,28},{4,0},{12,8},{20,16},{28,24},{1,5},{9... | collective-permute-start | bytes 589832 | tf_op jit(solution)/shard_map/ppermute | solution.py:371
  26.9 2.7 %collective-permute-start.4 = (f32[3,32,512]{2,1,0:T(8,128)S(1)}, f32[3,32,512]{2,1,0:T(8,128)S(1)}, u32[]{:S(2)}, u32[]{:S(2)}) collective-permute-start(f32[3,32,512]{2,1,0:T(8,128)S(1)} %get-tuple-element.106), channel_id=1, source_target_pairs={{0,4},{8,12},{16,20},{24,28},{4,0},{12,8},{20,16},{28,24},{1,5},{9... | collective-permute-start | bytes 589832 | tf_op jit(solution)/shard_map/ppermute | solution.py:371
  30.4 7.8 %collective-permute-done.6.left = f32[3,32,512]{2,1,0:T(8,128)S(1)} collective-permute-done((f32[3,32,512]{2,1,0:T(8,128)S(1)}, f32[3,32,512]{2,1,0:T(8,128)S(1)}, u32[]{:S(2)}, u32[]{:S(2)}) %collective-permute-start.6) | collective-permute-done | bytes 196640 | tf_op jit(solution)/shard_map/ppermute | solution.py:371
  38.2 2.5 %shard_map.69 = (f32[12,32,512]{2,1,0:T(8,128)S(1)}, f32[1,240,128]{2,1,0:T(8,128)S(1)}, f32[1,240,128]{2,1,0:T(8,128)S(1)}, f32[1,240,128]{2,1,0:T(8,128)S(1)},...) custom-call(s32[108]{0:T(128)S(1)} %convert_reduce_fusion.edges, s32[2]{0:T(128)S(1)} %pad_add_fusion.place_of, ...), custom_call_target="tpu_custom_call" | custom-call | tf_op jit(solution)/shard_map/pallas_call | solution.py:24
  40.7 1.3 %collective-permute-start.8 = (f32[1,240,128]{2,1,0:T(8,128)S(1)}, f32[1,240,128]{2,1,0:T(8,128)S(1)}, u32[]{:S(2)}, u32[]{:S(2)}) collective-permute-start(f32[1,240,128]{2,1,0:T(8,128)S(1)} %get-tuple-element.118), channel_id=1, source_target_pairs={{0,16},{4,20},{8,24},{12,28},{1,17},{5,21},{9,25},{13,29},{2,18},{... | collective-permute-start | bytes 368648 | tf_op jit(solution)/shard_map/ppermute | solution.py:517
  43.3 3.1 %shard_map.70 = (f32[12,32,640]{2,1,0:T(8,128)S(1)}, f32[3,32,512]{2,1,0:T(8,128)S(1)}, f32[3,32,512]{2,1,0:T(8,128)S(1)}, f32[12,8,640]{2,1,0:T(8,128)}) custom-call(s32[2]{0:T(128)S(1)} %pad_add_fusion.place_of, f32[12,72,640]{2,1,0:T(8,128)S(1)} %get-tuple-element.98.blur, f32[12,72,640]{2,1,0:T(8,128)S(1)} %get-tuple-element.99.seen, ...), custom_call_target="tpu_custom_call" | custom-call | tf_op jit(solution)/shard_map/pallas_call | solution.py:24
  47.2 6.4 %collective-permute-done.9.refs_3_ = f32[1,240,128]{2,1,0:T(8,128)S(1)} collective-permute-done((f32[1,240,128]{2,1,0:T(8,128)S(1)}, f32[1,240,128]{2,1,0:T(8,128)S(1)}, u32[]{:S(2)}, u32[]{:S(2)}) %collective-permute-start.9) | collective-permute-done | bytes 122912 | tf_op jit(solution)/shard_map/ppermute | solution.py:517
  58.2 5.6 %collective-permute-done.12.refs_0_ = f32[1,240,128]{2,1,0:T(8,128)S(1)} collective-permute-done((f32[1,240,128]{2,1,0:T(8,128)S(1)}, f32[1,240,128]{2,1,0:T(8,128)S(1)}, u32[]{:S(2)}, u32[]{:S(2)}) %collective-permute-start.12) | collective-permute-done | bytes 122912 | tf_op jit(solution)/shard_map/ppermute | solution.py:517
  64.2 3.5 %collective-permute-done.14.refs_4_ = f32[1,240,128]{2,1,0:T(8,128)S(1)} collective-permute-done((f32[1,240,128]{2,1,0:T(8,128)S(1)}, f32[1,240,128]{2,1,0:T(8,128)S(1)}, u32[]{:S(2)}, u32[]{:S(2)}) %collective-permute-start.14) | collective-permute-done | bytes 122912 | tf_op jit(solution)/shard_map/ppermute | solution.py:517
  67.7 3.7 %shard_map.72 = (f32[12,32,512]{2,1,0:T(8,128)}, f32[1,240,128]{2,1,0:T(8,128)S(1)}, f32[1,240,128]{2,1,0:T(8,128)S(1)}, f32[1,240,128]{2,1,0:T(8,128)S(1)}, f32...) custom-call(s32[108]{0:T(128)S(1)} %convert_reduce_fusion.edges, ...), custom_call_target="tpu_custom_call" | custom-call | tf_op jit(solution)/shard_map/pallas_call | solution.py:24
  76.6 1.5 %collective-permute-start.17 = (f32[1,240,128]{2,1,0:T(8,128)S(1)}, f32[1,240,128]{2,1,0:T(8,128)S(1)}, u32[]{:S(2)}, u32[]{:S(2)}) collective-permute-start(f32[1,240,128]{2,1,0:T(8,128)S(1)} %get-tuple-element.136), channel_id=1, source_target_pairs={{0,12},{4,16},{8,20},{12,24},{16,28},{1,13},{5,17},{9,21},{13,25},... | collective-permute-start | bytes 368648 | tf_op jit(solution)/shard_map/ppermute | solution.py:517
  78.1 1.8 %collective-permute-done.15.refs_0_ = f32[1,240,128]{2,1,0:T(8,128)S(1)} collective-permute-done((f32[1,240,128]{2,1,0:T(8,128)S(1)}, f32[1,240,128]{2,1,0:T(8,128)S(1)}, u32[]{:S(2)}, u32[]{:S(2)}) %collective-permute-start.15) | collective-permute-done | bytes 122912 | tf_op jit(solution)/shard_map/ppermute | solution.py:517
  81.2 10.4 %collective-permute-done.16.refs_1_ = f32[1,240,128]{2,1,0:T(8,128)S(1)} collective-permute-done((f32[1,240,128]{2,1,0:T(8,128)S(1)}, f32[1,240,128]{2,1,0:T(8,128)S(1)}, u32[]{:S(2)}, u32[]{:S(2)}) %collective-permute-start.16) | collective-permute-done | bytes 122912 | tf_op jit(solution)/shard_map/ppermute | solution.py:517
  93.8 1.6 %shard_map.71.settled = f32[12,32,512]{2,1,0:T(8,128)S(1)} custom-call(s32[108]{0:T(128)S(1)} %convert_reduce_fusion.edges, s32[2]{0:T(128)S(1)} %pad_add_fusion.place_of, f32[12,32,512]{2,1,0:T(8,128)} %copy-done.8, f32[1,240,128]{2,1,0:T(8,128)S(1)} %collective-permute-done.12.refs_0_, f32[1,240,128]{2,1,0:T(8,128)S(1)} %collective-permute-done.13.refs_1_, ...), custom_call_target="tpu_custom_call" | custom-call | tf_op jit(solution)/shard_map/pallas_call | solution.py:24
  95.4 3.1 %collective-permute-done.19.refs_4_ = f32[1,240,128]{2,1,0:T(8,128)S(1)} collective-permute-done((f32[1,240,128]{2,1,0:T(8,128)S(1)}, f32[1,240,128]{2,1,0:T(8,128)S(1)}, u32[]{:S(2)}, u32[]{:S(2)}) %collective-permute-start.19) | collective-permute-done | bytes 122912 | tf_op jit(solution)/shard_map/ppermute | solution.py:517
  98.5 1.3 %shard_map.73 = f32[12,64,512]{2,1,0:T(8,128)S(1)} custom-call(s32[108]{0:T(128)S(1)} %convert_reduce_fusion.edges, s32[2]{0:T(128)S(1)} %pad_add_fusion.place_of, f32[12,32,512]{2,1,0:T(8,128)S(1)} %shard_map.71.settled, f32[12,32,512]{2,1,0:T(8,128)S(1)} %copy-done.9, f32[1,240,128]{2,1,0:T(8,128)S(1)} %collective-permute-done.15.refs_0_, ...), custom_call_target="tpu_custom_call" | custom-call | tf_op jit(solution)/shard_map/pallas_call | solution.py:24
  (62 shorter events, 22.5 us)
Async XLA Ops:
  3.3 5.2 %collective-permute-start = (f32[108,512]{1,0:T(8,128)S(1)}, f32[108,512]{1,0:T(8,128)S(1)}, u32[]{:S(2)}, u32[]{:S(2)}) collective-permute-start(f32[108,512]{1,0:T(8,128)S(1)} %get-tuple-element.93), channel_id=1, source_target_pairs={{0,1},{2,3},{1,0},{3,2},{4,5},{6,7},{5,4},{7,6},{8,9},{10,11},{9,8... | collective-permute-start | bytes 663560 | tf_op jit(solution)/shard_map/ppermute | solution.py:371
  4.0 7.6 %collective-permute-start.1 = (f32[108,512]{1,0:T(8,128)S(1)}, f32[108,512]{1,0:T(8,128)S(1)}, u32[]{:S(2)}, u32[]{:S(2)}) collective-permute-start(f32[108,512]{1,0:T(8,128)S(1)} %get-tuple-element.94), channel_id=1, source_target_pairs={{1,2},{2,1},{5,6},{6,5},{9,10},{10,9},{13,14},{14,13},{17,18},{18,... | collective-permute-start | bytes 663560 | tf_op jit(solution)/shard_map/ppermute | solution.py:371
  13.7 8.0 %collective-permute-start.2 = (f32[3,40,512]{2,1,0:T(8,128)S(1)}, f32[3,40,512]{2,1,0:T(8,128)S(1)}, u32[]{:S(2)}, u32[]{:S(2)}) collective-permute-start(f32[3,40,512]{2,1,0:T(8,128)S(1)} %get-tuple-element.100), channel_id=1, source_target_pairs={{0,4},{8,12},{16,20},{24,28},{4,0},{12,8},{20,16},{28,24},{1,5},{9... | collective-permute-start | bytes 737288 | tf_op jit(solution)/shard_map/ppermute | solution.py:371
  13.9 7.7 %collective-permute-start.3 = (f32[3,40,512]{2,1,0:T(8,128)S(1)}, f32[3,40,512]{2,1,0:T(8,128)S(1)}, u32[]{:S(2)}, u32[]{:S(2)}) collective-permute-start(f32[3,40,512]{2,1,0:T(8,128)S(1)} %get-tuple-element.101), channel_id=1, source_target_pairs={{4,8},{12,16},{20,24},{8,4},{16,12},{24,20},{5,9},{13,17},{21,25},... | collective-permute-start | bytes 737288 | tf_op jit(solution)/shard_map/ppermute | solution.py:371
  21.7 16.5 %copy-start.1 = (f32[12,64,512]{2,1,0:T(8,128)S(1)}, f32[12,64,512]{2,1,0:T(8,128)}, u32[]{:S(2)}) copy-start(f32[12,64,512]{2,1,0:T(8,128)} %est.7) | copy-start | bytes 4718596
  24.3 13.9 %collective-permute-start.6 = (f32[3,32,512]{2,1,0:T(8,128)S(1)}, f32[3,32,512]{2,1,0:T(8,128)S(1)}, u32[]{:S(2)}, u32[]{:S(2)}) collective-permute-start(f32[3,32,512]{2,1,0:T(8,128)S(1)} %get-tuple-element.109), channel_id=1, source_target_pairs={{0,4},{8,12},{16,20},{24,28},{4,0},{12,8},{20,16},{28,24},{1,5},{9... | collective-permute-start | bytes 589832 | tf_op jit(solution)/shard_map/ppermute | solution.py:371
  26.3 11.9 %collective-permute-start.7 = (f32[3,32,512]{2,1,0:T(8,128)S(1)}, f32[3,32,512]{2,1,0:T(8,128)S(1)}, u32[]{:S(2)}, u32[]{:S(2)}) collective-permute-start(f32[3,32,512]{2,1,0:T(8,128)S(1)} %get-tuple-element.110), channel_id=1, source_target_pairs={{4,8},{12,16},{20,24},{8,4},{16,12},{24,20},{5,9},{13,17},{21,25},... | collective-permute-start | bytes 589832 | tf_op jit(solution)/shard_map/ppermute | solution.py:371
  26.9 16.4 %collective-permute-start.4 = (f32[3,32,512]{2,1,0:T(8,128)S(1)}, f32[3,32,512]{2,1,0:T(8,128)S(1)}, u32[]{:S(2)}, u32[]{:S(2)}) collective-permute-start(f32[3,32,512]{2,1,0:T(8,128)S(1)} %get-tuple-element.106), channel_id=1, source_target_pairs={{0,4},{8,12},{16,20},{24,28},{4,0},{12,8},{20,16},{28,24},{1,5},{9... | collective-permute-start | bytes 589832 | tf_op jit(solution)/shard_map/ppermute | solution.py:371
  29.6 13.7 %collective-permute-start.5 = (f32[3,32,512]{2,1,0:T(8,128)S(1)}, f32[3,32,512]{2,1,0:T(8,128)S(1)}, u32[]{:S(2)}, u32[]{:S(2)}) collective-permute-start(f32[3,32,512]{2,1,0:T(8,128)S(1)} %get-tuple-element.107), channel_id=1, source_target_pairs={{4,8},{12,16},{20,24},{8,4},{16,12},{24,20},{5,9},{13,17},{21,25},... | collective-permute-start | bytes 589832 | tf_op jit(solution)/shard_map/ppermute | solution.py:371
  40.7 27.0 %copy-start.8 = (f32[12,32,512]{2,1,0:T(8,128)}, f32[12,32,512]{2,1,0:T(8,128)S(1)}, u32[]{:S(2)}) copy-start(f32[12,32,512]{2,1,0:T(8,128)S(1)} %get-tuple-element.205.base.refs_0_) | copy-start | bytes 2359300
  40.7 6.5 %collective-permute-start.8 = (f32[1,240,128]{2,1,0:T(8,128)S(1)}, f32[1,240,128]{2,1,0:T(8,128)S(1)}, u32[]{:S(2)}, u32[]{:S(2)}) collective-permute-start(f32[1,240,128]{2,1,0:T(8,128)S(1)} %get-tuple-element.118), channel_id=1, source_target_pairs={{0,16},{4,20},{8,24},{12,28},{1,17},{5,21},{9,25},{13,29},{2,18},{... | collective-permute-start | bytes 368648 | tf_op jit(solution)/shard_map/ppermute | solution.py:517
  42.0 11.6 %collective-permute-start.9 = (f32[1,240,128]{2,1,0:T(8,128)S(1)}, f32[1,240,128]{2,1,0:T(8,128)S(1)}, u32[]{:S(2)}, u32[]{:S(2)}) collective-permute-start(f32[1,240,128]{2,1,0:T(8,128)S(1)} %get-tuple-element.119), channel_id=1, source_target_pairs={{0,20},{4,24},{8,28},{1,21},{5,25},{9,29},{2,22},{6,26},{10,30},{3... | collective-permute-start | bytes 368648 | tf_op jit(solution)/shard_map/ppermute | solution.py:517
  53.6 14.1 %collective-permute-start.10 = (f32[3,32,512]{2,1,0:T(8,128)S(1)}, f32[3,32,512]{2,1,0:T(8,128)S(1)}, u32[]{:S(2)}, u32[]{:S(2)}) collective-permute-start(f32[3,32,512]{2,1,0:T(8,128)S(1)} %get-tuple-element.120), channel_id=1, source_target_pairs={{0,4},{8,12},{16,20},{24,28},{4,0},{12,8},{20,16},{28,24},{1,5},{9... | collective-permute-start | bytes 589832 | tf_op jit(solution)/shard_map/ppermute | solution.py:371
  53.6 14.1 %collective-permute-start.11 = (f32[3,32,512]{2,1,0:T(8,128)S(1)}, f32[3,32,512]{2,1,0:T(8,128)S(1)}, u32[]{:S(2)}, u32[]{:S(2)}) collective-permute-start(f32[3,32,512]{2,1,0:T(8,128)S(1)} %get-tuple-element.121), channel_id=1, source_target_pairs={{4,8},{12,16},{20,24},{8,4},{16,12},{24,20},{5,9},{13,17},{21,25},... | collective-permute-start | bytes 589832 | tf_op jit(solution)/shard_map/ppermute | solution.py:371
  54.3 9.5 %collective-permute-start.12 = (f32[1,240,128]{2,1,0:T(8,128)S(1)}, f32[1,240,128]{2,1,0:T(8,128)S(1)}, u32[]{:S(2)}, u32[]{:S(2)}) collective-permute-start(f32[1,240,128]{2,1,0:T(8,128)S(1)} %get-tuple-element.122), channel_id=1, source_target_pairs={{0,8},{4,12},{8,16},{12,20},{16,24},{20,28},{1,9},{5,13},{9,17},{1... | collective-permute-start | bytes 368648 | tf_op jit(solution)/shard_map/ppermute | solution.py:517
  55.6 8.7 %collective-permute-start.13 = (f32[1,240,128]{2,1,0:T(8,128)S(1)}, f32[1,240,128]{2,1,0:T(8,128)S(1)}, u32[]{:S(2)}, u32[]{:S(2)}) collective-permute-start(f32[1,240,128]{2,1,0:T(8,128)S(1)} %get-tuple-element.123), channel_id=1, source_target_pairs={{0,12},{4,16},{8,20},{12,24},{16,28},{1,13},{5,17},{9,21},{13,25},... | collective-permute-start | bytes 368648 | tf_op jit(solution)/shard_map/ppermute | solution.py:517
  56.9 10.8 %collective-permute-start.14 = (f32[1,240,128]{2,1,0:T(8,128)S(1)}, f32[1,240,128]{2,1,0:T(8,128)S(1)}, u32[]{:S(2)}, u32[]{:S(2)}) collective-permute-start(f32[1,240,128]{2,1,0:T(8,128)S(1)} %get-tuple-element.124), channel_id=1, source_target_pairs={{0,24},{4,28},{1,25},{5,29},{2,26},{6,30},{3,27},{7,31}} | collective-permute-start | bytes 368648 | tf_op jit(solution)/shard_map/ppermute | solution.py:517
  71.4 8.5 %collective-permute-start.15 = (f32[1,240,128]{2,1,0:T(8,128)S(1)}, f32[1,240,128]{2,1,0:T(8,128)S(1)}, u32[]{:S(2)}, u32[]{:S(2)}) collective-permute-start(f32[1,240,128]{2,1,0:T(8,128)S(1)} %get-tuple-element.134), channel_id=1, source_target_pairs={{0,16},{4,20},{8,24},{12,28},{1,17},{5,21},{9,25},{13,29},{2,18},{... | collective-permute-start | bytes 368648 | tf_op jit(solution)/shard_map/ppermute | solution.py:517
  72.7 18.9 %collective-permute-start.16 = (f32[1,240,128]{2,1,0:T(8,128)S(1)}, f32[1,240,128]{2,1,0:T(8,128)S(1)}, u32[]{:S(2)}, u32[]{:S(2)}) collective-permute-start(f32[1,240,128]{2,1,0:T(8,128)S(1)} %get-tuple-element.135), channel_id=1, source_target_pairs={{0,20},{4,24},{8,28},{1,21},{5,25},{9,29},{2,22},{6,26},{10,30},{3... | collective-permute-start | bytes 368648 | tf_op jit(solution)/shard_map/ppermute | solution.py:517
  74.0 24.4 %collective-permute-start.20 = (f32[2,432,128]{2,1,0:T(8,128)S(1)}, f32[2,432,128]{2,1,0:T(8,128)S(1)}, u32[]{:S(2)}, u32[]{:S(2)}) collective-permute-start(f32[2,432,128]{2,1,0:T(8,128)S(1)} %get-tuple-element.139), channel_id=1, source_target_pairs={{0,4},{4,8},{8,12},{12,16},{16,20},{20,24},{24,28},{1,5},{5,9},{9,... | collective-permute-start | bytes 1327112 | tf_op jit(solution)/shard_map/ppermute | solution.py:517
  75.3 23.1 %collective-permute-start.21 = (f32[1,576,128]{2,1,0:T(8,128)S(1)}, f32[1,576,128]{2,1,0:T(8,128)S(1)}, u32[]{:S(2)}, u32[]{:S(2)}) collective-permute-start(f32[1,576,128]{2,1,0:T(8,128)S(1)} %get-tuple-element.140), channel_id=1, source_target_pairs={{0,28},{1,29},{2,30},{3,31}} | collective-permute-start | bytes 884744 | tf_op jit(solution)/shard_map/ppermute | solution.py:517
  76.6 18.7 %collective-permute-start.17 = (f32[1,240,128]{2,1,0:T(8,128)S(1)}, f32[1,240,128]{2,1,0:T(8,128)S(1)}, u32[]{:S(2)}, u32[]{:S(2)}) collective-permute-start(f32[1,240,128]{2,1,0:T(8,128)S(1)} %get-tuple-element.136), channel_id=1, source_target_pairs={{0,12},{4,16},{8,20},{12,24},{16,28},{1,13},{5,17},{9,21},{13,25},... | collective-permute-start | bytes 368648 | tf_op jit(solution)/shard_map/ppermute | solution.py:517
  79.9 15.5 %collective-permute-start.18 = (f32[1,240,128]{2,1,0:T(8,128)S(1)}, f32[1,240,128]{2,1,0:T(8,128)S(1)}, u32[]{:S(2)}, u32[]{:S(2)}) collective-permute-start(f32[1,240,128]{2,1,0:T(8,128)S(1)} %get-tuple-element.137), channel_id=1, source_target_pairs={{0,24},{4,28},{1,25},{5,29},{2,26},{6,30},{3,27},{7,31}} | collective-permute-start | bytes 368648 | tf_op jit(solution)/shard_map/ppermute | solution.py:517
  91.6 6.8 %collective-permute-start.19 = (f32[1,240,128]{2,1,0:T(8,128)S(1)}, f32[1,240,128]{2,1,0:T(8,128)S(1)}, u32[]{:S(2)}, u32[]{:S(2)}) collective-permute-start(f32[1,240,128]{2,1,0:T(8,128)S(1)} %get-tuple-element.138), channel_id=1, source_target_pairs={{0,8},{4,12},{8,16},{12,20},{16,24},{20,28},{1,9},{5,13},{9,17},{1... | collective-permute-start | bytes 368648 | tf_op jit(solution)/shard_map/ppermute | solution.py:517
  (9 other events, 41.2 us)

commit v5 on v4

--- a/solution.py
+++ b/solution.py
@@ -387,8 +387,8 @@
     strip = like(3 * ROW_HALF * planes, cols)
     me = jnp.stack([lax.axis_index("scan"), lax.axis_index("lat")]).astype(jnp.int32)
     pair, other = run(strip_body, (strip, strip), [SMEM, VMEM, VMEM], (me, estimate, observed))
+    above = swapped(pair, "lat", 0)
     below = swapped(other, "lat", 1)
-    above = swapped(pair, "lat", 0)
     levels = jnp.arange((count + 1) * planes, dtype=jnp.int32) - planes
     edges = jnp.sum(shear_planes[None, :] <= levels[:, None], axis=1, dtype=jnp.int32)
     turn = (shear_planes % planes)[None, :]
@@ -440,7 +440,7 @@
         parts = height // part_rows
         return Packing(planes, cols, parts, part_rows, min(-(-columns // 8) * 8, LANES))
 
-    near, far = packing(rows, share * 9 // 8), packing(rows, share * 3 // 2)
+    near, far = packing(rows, share), packing(rows, share * 3 // 2)
     later = packing(rows, share // 4)
     mids = []
     for begin, end in chunks:

time: 103 us -> 102 us (level)
  no operation moved by 1% of the time
where the time goes in v5:
time: 102 us; the launch traced here: 101 us
  waiting for transfers between devices  46.7 us (46%)
  starting transfers between devices  27 us (26%)
  Pallas kernels  21.4 us (21%)
  local copies, waits for them, and re-layouts  3.8 us (4%)
  other arithmetic  1.07 us (1%)
    ppermute x12, waiting for transfers between devices, on_device(): lax.ppermute(x, 'scan', [(j, j + ds[0][0]) for j in range(count - ds[0][0...  31.5 us
    pallas_call x10, Pallas kernels, run(): pl.pallas_call(body, out_shape=outs, in_specs=ins, out_specs=jax.tree.map...  21.4 us
    ppermute x12, starting transfers between devices, on_device(): lax.ppermute(x, 'scan', [(j, j + ds[0][0]) for j in range(count - ds[0][0...  15.7 us
    ppermute x10, waiting for transfers between devices, swapped(): return lax.ppermute(x, axis, ends + [(j, i) for i, j in ends])  15.2 us
    ppermute x10, starting transfers between devices, swapped(): return lax.ppermute(x, axis, ends + [(j, i) for i, j in ends])  11.4 us
    unnamed x22, local copies, waits for them, and re-layouts  3.72 us
  transfers between devices with their start and end apart: 22, of which 11 were waited for; matrix products, arithmetic and copies ran while one was open for 1% of the time, Pallas kernels for 11%

profile of v5, /device:TPU:29, one launch (start us, length us, event | category | flops | bytes accessed | tf_op | source)
XLA Modules:
  0.0 101.0 jit_solution(6196661847290646854)
XLA Ops:
  0.1 1.4 %copy-done = f32[12,64,512]{2,1,0:T(8,128)S(1)} copy-done((f32[12,64,512]{2,1,0:T(8,128)S(1)}, f32[12,64,512]{2,1,0:T(8,128)}, u32[]{:S(2)}) %copy-start) | copy-done | bytes 1572888
  4.0 3.0 %collective-permute-start.1 = (f32[108,512]{1,0:T(8,128)S(1)}, f32[108,512]{1,0:T(8,128)S(1)}, u32[]{:S(2)}, u32[]{:S(2)}) collective-permute-start(f32[108,512]{1,0:T(8,128)S(1)} %get-tuple-element.94), channel_id=1, source_target_pairs={{1,2},{2,1},{5,6},{6,5},{9,10},{10,9},{13,14},{14,13},{17,18},{18,... | collective-permute-start | bytes 663560 | tf_op jit(solution)/shard_map/ppermute | solution.py:371
  7.1 1.4 %shard_map.64 = (f32[12,64,512]{2,1,0:T(8,128)S(1)}, bf16[512,512]{1,0:T(8,128)(2,1)S(1)}, bf16[512,512]{1,0:T(8,128)(2,1)S(1)}) custom-call(f32[12,64,512]{2,1,0:T(8,128)S(1)} %copy-done, f32[512,512]{1,0:T(8,128)S(1)} %copy-done.4), custom_call_target="tpu_custom_call" | custom-call | tf_op jit(solution)/shard_map/pallas_call | solution.py:24
  8.5 3.1 %collective-permute-done.1.other = f32[108,512]{1,0:T(8,128)S(1)} collective-permute-done((f32[108,512]{1,0:T(8,128)S(1)}, f32[108,512]{1,0:T(8,128)S(1)}, u32[]{:S(2)}, u32[]{:S(2)}) %collective-permute-start.1) | collective-permute-done | bytes 221216 | tf_op jit(solution)/shard_map/ppermute | solution.py:371
  11.6 2.0 %shard_map.66 = (f32[12,80,512]{2,1,0:T(8,128)S(1)}, f32[3,40,512]{2,1,0:T(8,128)S(1)}, f32[3,40,512]{2,1,0:T(8,128)S(1)}, f32[3,32,512]{2,1,0:T(8,128)S(1)}, f32[3,32,512]{2,1,0:T(8,128)S(1)}) custom-call(s32[2]{0:T(128)S(1)} %pad_add_fusion.place_of, f32[12,64,512]{2,1,0:T(8,128)S(1)} %get-tuple-element.92.mixed, ...), custom_call_target="tpu_custom_call" | custom-call | tf_op jit(solution)/shard_map/pallas_call | solution.py:24
  14.7 2.7 %shard_map.67 = (f32[12,72,640]{2,1,0:T(8,128)S(1)}, f32[12,72,640]{2,1,0:T(8,128)S(1)}) custom-call(s32[2]{0:T(128)S(1)} %pad_add_fusion.place_of, f32[12,80,512]{2,1,0:T(8,128)S(1)} %get-tuple-element.97.tall, bf16[12,64,512]{2,1,0:T(8,128)(2,1)S(1)} %copy-done.3, f32[108,512]{1,0:T(8,128)S(1)} %collective-permute-done.pair, ...), custom_call_target="tpu_custom_call" | custom-call | tf_op jit(solution)/shard_map/pallas_call | solution.py:24
  17.4 4.3 %collective-permute-done.2.left = f32[3,40,512]{2,1,0:T(8,128)S(1)} collective-permute-done((f32[3,40,512]{2,1,0:T(8,128)S(1)}, f32[3,40,512]{2,1,0:T(8,128)S(1)}, u32[]{:S(2)}, u32[]{:S(2)}) %collective-permute-start.2) | collective-permute-done | bytes 245792 | tf_op jit(solution)/shard_map/ppermute | solution.py:371
  21.7 2.6 %shard_map.68 = (f32[12,32,640]{2,1,0:T(8,128)S(1)}, f32[3,32,512]{2,1,0:T(8,128)S(1)}, f32[3,32,512]{2,1,0:T(8,128)S(1)}, f32[12,8,640]{2,1,0:T(8,128)S(1)}) custom-call(s32[2]{0:T(128)S(1)} %pad_add_fusion.place_of, f32[12,72,640]{2,1,0:T(8,128)S(1)} %get-tuple-element.98.blur, f32[12,72,640]{2,1,0:T(8,128)S(1)} %get-tuple-element.99.seen, ...), custom_call_target="tpu_custom_call" | custom-call | tf_op jit(solution)/shard_map/pallas_call | solution.py:24
  24.3 2.0 %collective-permute-start.6 = (f32[3,32,512]{2,1,0:T(8,128)S(1)}, f32[3,32,512]{2,1,0:T(8,128)S(1)}, u32[]{:S(2)}, u32[]{:S(2)}) collective-permute-start(f32[3,32,512]{2,1,0:T(8,128)S(1)} %get-tuple-element.109), channel_id=1, source_target_pairs={{0,4},{8,12},{16,20},{24,28},{4,0},{12,8},{20,16},{28,24},{1,5},{9... | collective-permute-start | bytes 589832 | tf_op jit(solution)/shard_map/ppermute | solution.py:371
  26.9 2.7 %collective-permute-start.4 = (f32[3,32,512]{2,1,0:T(8,128)S(1)}, f32[3,32,512]{2,1,0:T(8,128)S(1)}, u32[]{:S(2)}, u32[]{:S(2)}) collective-permute-start(f32[3,32,512]{2,1,0:T(8,128)S(1)} %get-tuple-element.106), channel_id=1, source_target_pairs={{0,4},{8,12},{16,20},{24,28},{4,0},{12,8},{20,16},{28,24},{1,5},{9... | collective-permute-start | bytes 589832 | tf_op jit(solution)/shard_map/ppermute | solution.py:371
  30.4 7.8 %collective-permute-done.6.left = f32[3,32,512]{2,1,0:T(8,128)S(1)} collective-permute-done((f32[3,32,512]{2,1,0:T(8,128)S(1)}, f32[3,32,512]{2,1,0:T(8,128)S(1)}, u32[]{:S(2)}, u32[]{:S(2)}) %collective-permute-start.6) | collective-permute-done | bytes 196640 | tf_op jit(solution)/shard_map/ppermute | solution.py:371
  38.2 2.5 %shard_map.69 = (f32[12,32,512]{2,1,0:T(8,128)S(1)}, f32[1,240,128]{2,1,0:T(8,128)S(1)}, f32[1,240,128]{2,1,0:T(8,128)S(1)}, f32[1,240,128]{2,1,0:T(8,128)S(1)},...) custom-call(s32[108]{0:T(128)S(1)} %convert_reduce_fusion.edges, s32[2]{0:T(128)S(1)} %pad_add_fusion.place_of, ...), custom_call_target="tpu_custom_call" | custom-call | tf_op jit(solution)/shard_map/pallas_call | solution.py:24
  43.3 3.1 %shard_map.70 = (f32[12,32,640]{2,1,0:T(8,128)S(1)}, f32[3,32,512]{2,1,0:T(8,128)S(1)}, f32[3,32,512]{2,1,0:T(8,128)S(1)}, f32[12,8,640]{2,1,0:T(8,128)}) custom-call(s32[2]{0:T(128)S(1)} %pad_add_fusion.place_of, f32[12,72,640]{2,1,0:T(8,128)S(1)} %get-tuple-element.98.blur, f32[12,72,640]{2,1,0:T(8,128)S(1)} %get-tuple-element.99.seen, ...), custom_call_target="tpu_custom_call" | custom-call | tf_op jit(solution)/shard_map/pallas_call | solution.py:24
  47.2 6.4 %collective-permute-done.9.refs_3_ = f32[1,240,128]{2,1,0:T(8,128)S(1)} collective-permute-done((f32[1,240,128]{2,1,0:T(8,128)S(1)}, f32[1,240,128]{2,1,0:T(8,128)S(1)}, u32[]{:S(2)}, u32[]{:S(2)}) %collective-permute-start.9) | collective-permute-done | bytes 122912 | tf_op jit(solution)/shard_map/ppermute | solution.py:517
  58.2 5.6 %collective-permute-done.12.refs_0_ = f32[1,240,128]{2,1,0:T(8,128)S(1)} collective-permute-done((f32[1,240,128]{2,1,0:T(8,128)S(1)}, f32[1,240,128]{2,1,0:T(8,128)S(1)}, u32[]{:S(2)}, u32[]{:S(2)}) %collective-permute-start.12) | collective-permute-done | bytes 122912 | tf_op jit(solution)/shard_map/ppermute | solution.py:517
  64.2 3.5 %collective-permute-done.14.refs_4_ = f32[1,240,128]{2,1,0:T(8,128)S(1)} collective-permute-done((f32[1,240,128]{2,1,0:T(8,128)S(1)}, f32[1,240,128]{2,1,0:T(8,128)S(1)}, u32[]{:S(2)}, u32[]{:S(2)}) %collective-permute-start.14) | collective-permute-done | bytes 122912 | tf_op jit(solution)/shard_map/ppermute | solution.py:517
  67.7 3.7 %shard_map.72 = (f32[12,32,512]{2,1,0:T(8,128)}, f32[1,240,128]{2,1,0:T(8,128)S(1)}, f32[1,240,128]{2,1,0:T(8,128)S(1)}, f32[1,240,128]{2,1,0:T(8,128)S(1)}, f32...) custom-call(s32[108]{0:T(128)S(1)} %convert_reduce_fusion.edges, ...), custom_call_target="tpu_custom_call" | custom-call | tf_op jit(solution)/shard_map/pallas_call | solution.py:24
  75.3 1.3 %collective-permute-start.21 = (f32[1,576,128]{2,1,0:T(8,128)S(1)}, f32[1,576,128]{2,1,0:T(8,128)S(1)}, u32[]{:S(2)}, u32[]{:S(2)}) collective-permute-start(f32[1,576,128]{2,1,0:T(8,128)S(1)} %get-tuple-element.140), channel_id=1, source_target_pairs={{0,28},{1,29},{2,30},{3,31}} | collective-permute-start | bytes 884744 | tf_op jit(solution)/shard_map/ppermute | solution.py:517
  76.6 1.5 %collective-permute-start.17 = (f32[1,240,128]{2,1,0:T(8,128)S(1)}, f32[1,240,128]{2,1,0:T(8,128)S(1)}, u32[]{:S(2)}, u32[]{:S(2)}) collective-permute-start(f32[1,240,128]{2,1,0:T(8,128)S(1)} %get-tuple-element.136), channel_id=1, source_target_pairs={{0,12},{4,16},{8,20},{12,24},{16,28},{1,13},{5,17},{9,21},{13,25},... | collective-permute-start | bytes 368648 | tf_op jit(solution)/shard_map/ppermute | solution.py:517
  78.1 1.8 %collective-permute-done.15.refs_0_ = f32[1,240,128]{2,1,0:T(8,128)S(1)} collective-permute-done((f32[1,240,128]{2,1,0:T(8,128)S(1)}, f32[1,240,128]{2,1,0:T(8,128)S(1)}, u32[]{:S(2)}, u32[]{:S(2)}) %collective-permute-start.15) | collective-permute-done | bytes 122912 | tf_op jit(solution)/shard_map/ppermute | solution.py:517
  81.2 10.4 %collective-permute-done.16.refs_1_ = f32[1,240,128]{2,1,0:T(8,128)S(1)} collective-permute-done((f32[1,240,128]{2,1,0:T(8,128)S(1)}, f32[1,240,128]{2,1,0:T(8,128)S(1)}, u32[]{:S(2)}, u32[]{:S(2)}) %collective-permute-start.16) | collective-permute-done | bytes 122912 | tf_op jit(solution)/shard_map/ppermute | solution.py:517
  93.8 1.6 %shard_map.71.settled = f32[12,32,512]{2,1,0:T(8,128)S(1)} custom-call(s32[108]{0:T(128)S(1)} %convert_reduce_fusion.edges, s32[2]{0:T(128)S(1)} %pad_add_fusion.place_of, f32[12,32,512]{2,1,0:T(8,128)} %copy-done.8, f32[1,240,128]{2,1,0:T(8,128)S(1)} %collective-permute-done.12.refs_0_, f32[1,240,128]{2,1,0:T(8,128)S(1)} %collective-permute-done.13.refs_1_, ...), custom_call_target="tpu_custom_call" | custom-call | tf_op jit(solution)/shard_map/pallas_call | solution.py:24
  95.4 2.5 %collective-permute-done.19.refs_4_ = f32[1,240,128]{2,1,0:T(8,128)S(1)} collective-permute-done((f32[1,240,128]{2,1,0:T(8,128)S(1)}, f32[1,240,128]{2,1,0:T(8,128)S(1)}, u32[]{:S(2)}, u32[]{:S(2)}) %collective-permute-start.19) | collective-permute-done | bytes 122912 | tf_op jit(solution)/shard_map/ppermute | solution.py:517
  98.0 1.3 %shard_map.73 = f32[12,64,512]{2,1,0:T(8,128)S(1)} custom-call(s32[108]{0:T(128)S(1)} %convert_reduce_fusion.edges, s32[2]{0:T(128)S(1)} %pad_add_fusion.place_of, f32[12,32,512]{2,1,0:T(8,128)S(1)} %shard_map.71.settled, f32[12,32,512]{2,1,0:T(8,128)S(1)} %copy-done.9, f32[1,240,128]{2,1,0:T(8,128)S(1)} %collective-permute-done.15.refs_0_, ...), custom_call_target="tpu_custom_call" | custom-call | tf_op jit(solution)/shard_map/pallas_call | solution.py:24
  (62 shorter events, 22.5 us)
Async XLA Ops:
  3.3 5.2 %collective-permute-start = (f32[108,512]{1,0:T(8,128)S(1)}, f32[108,512]{1,0:T(8,128)S(1)}, u32[]{:S(2)}, u32[]{:S(2)}) collective-permute-start(f32[108,512]{1,0:T(8,128)S(1)} %get-tuple-element.93), channel_id=1, source_target_pairs={{0,1},{2,3},{1,0},{3,2},{4,5},{6,7},{5,4},{7,6},{8,9},{10,11},{9,8... | collective-permute-start | bytes 663560 | tf_op jit(solution)/shard_map/ppermute | solution.py:371
  4.0 7.6 %collective-permute-start.1 = (f32[108,512]{1,0:T(8,128)S(1)}, f32[108,512]{1,0:T(8,128)S(1)}, u32[]{:S(2)}, u32[]{:S(2)}) collective-permute-start(f32[108,512]{1,0:T(8,128)S(1)} %get-tuple-element.94), channel_id=1, source_target_pairs={{1,2},{2,1},{5,6},{6,5},{9,10},{10,9},{13,14},{14,13},{17,18},{18,... | collective-permute-start | bytes 663560 | tf_op jit(solution)/shard_map/ppermute | solution.py:371
  13.7 8.0 %collective-permute-start.2 = (f32[3,40,512]{2,1,0:T(8,128)S(1)}, f32[3,40,512]{2,1,0:T(8,128)S(1)}, u32[]{:S(2)}, u32[]{:S(2)}) collective-permute-start(f32[3,40,512]{2,1,0:T(8,128)S(1)} %get-tuple-element.100), channel_id=1, source_target_pairs={{0,4},{8,12},{16,20},{24,28},{4,0},{12,8},{20,16},{28,24},{1,5},{9... | collective-permute-start | bytes 737288 | tf_op jit(solution)/shard_map/ppermute | solution.py:371
  13.9 7.7 %collective-permute-start.3 = (f32[3,40,512]{2,1,0:T(8,128)S(1)}, f32[3,40,512]{2,1,0:T(8,128)S(1)}, u32[]{:S(2)}, u32[]{:S(2)}) collective-permute-start(f32[3,40,512]{2,1,0:T(8,128)S(1)} %get-tuple-element.101), channel_id=1, source_target_pairs={{4,8},{12,16},{20,24},{8,4},{16,12},{24,20},{5,9},{13,17},{21,25},... | collective-permute-start | bytes 737288 | tf_op jit(solution)/shard_map/ppermute | solution.py:371
  21.7 16.5 %copy-start.1 = (f32[12,64,512]{2,1,0:T(8,128)S(1)}, f32[12,64,512]{2,1,0:T(8,128)}, u32[]{:S(2)}) copy-start(f32[12,64,512]{2,1,0:T(8,128)} %est.7) | copy-start | bytes 4718596
  24.3 13.9 %collective-permute-start.6 = (f32[3,32,512]{2,1,0:T(8,128)S(1)}, f32[3,32,512]{2,1,0:T(8,128)S(1)}, u32[]{:S(2)}, u32[]{:S(2)}) collective-permute-start(f32[3,32,512]{2,1,0:T(8,128)S(1)} %get-tuple-element.109), channel_id=1, source_target_pairs={{0,4},{8,12},{16,20},{24,28},{4,0},{12,8},{20,16},{28,24},{1,5},{9... | collective-permute-start | bytes 589832 | tf_op jit(solution)/shard_map/ppermute | solution.py:371
  26.3 11.9 %collective-permute-start.7 = (f32[3,32,512]{2,1,0:T(8,128)S(1)}, f32[3,32,512]{2,1,0:T(8,128)S(1)}, u32[]{:S(2)}, u32[]{:S(2)}) collective-permute-start(f32[3,32,512]{2,1,0:T(8,128)S(1)} %get-tuple-element.110), channel_id=1, source_target_pairs={{4,8},{12,16},{20,24},{8,4},{16,12},{24,20},{5,9},{13,17},{21,25},... | collective-permute-start | bytes 589832 | tf_op jit(solution)/shard_map/ppermute | solution.py:371
  26.9 16.4 %collective-permute-start.4 = (f32[3,32,512]{2,1,0:T(8,128)S(1)}, f32[3,32,512]{2,1,0:T(8,128)S(1)}, u32[]{:S(2)}, u32[]{:S(2)}) collective-permute-start(f32[3,32,512]{2,1,0:T(8,128)S(1)} %get-tuple-element.106), channel_id=1, source_target_pairs={{0,4},{8,12},{16,20},{24,28},{4,0},{12,8},{20,16},{28,24},{1,5},{9... | collective-permute-start | bytes 589832 | tf_op jit(solution)/shard_map/ppermute | solution.py:371
  29.6 13.7 %collective-permute-start.5 = (f32[3,32,512]{2,1,0:T(8,128)S(1)}, f32[3,32,512]{2,1,0:T(8,128)S(1)}, u32[]{:S(2)}, u32[]{:S(2)}) collective-permute-start(f32[3,32,512]{2,1,0:T(8,128)S(1)} %get-tuple-element.107), channel_id=1, source_target_pairs={{4,8},{12,16},{20,24},{8,4},{16,12},{24,20},{5,9},{13,17},{21,25},... | collective-permute-start | bytes 589832 | tf_op jit(solution)/shard_map/ppermute | solution.py:371
  40.7 27.0 %copy-start.8 = (f32[12,32,512]{2,1,0:T(8,128)}, f32[12,32,512]{2,1,0:T(8,128)S(1)}, u32[]{:S(2)}) copy-start(f32[12,32,512]{2,1,0:T(8,128)S(1)} %get-tuple-element.205.base.refs_0_) | copy-start | bytes 2359300
  40.7 6.5 %collective-permute-start.8 = (f32[1,240,128]{2,1,0:T(8,128)S(1)}, f32[1,240,128]{2,1,0:T(8,128)S(1)}, u32[]{:S(2)}, u32[]{:S(2)}) collective-permute-start(f32[1,240,128]{2,1,0:T(8,128)S(1)} %get-tuple-element.118), channel_id=1, source_target_pairs={{0,16},{4,20},{8,24},{12,28},{1,17},{5,21},{9,25},{13,29},{2,18},{... | collective-permute-start | bytes 368648 | tf_op jit(solution)/shard_map/ppermute | solution.py:517
  42.0 11.6 %collective-permute-start.9 = (f32[1,240,128]{2,1,0:T(8,128)S(1)}, f32[1,240,128]{2,1,0:T(8,128)S(1)}, u32[]{:S(2)}, u32[]{:S(2)}) collective-permute-start(f32[1,240,128]{2,1,0:T(8,128)S(1)} %get-tuple-element.119), channel_id=1, source_target_pairs={{0,20},{4,24},{8,28},{1,21},{5,25},{9,29},{2,22},{6,26},{10,30},{3... | collective-permute-start | bytes 368648 | tf_op jit(solution)/shard_map/ppermute | solution.py:517
  53.6 14.1 %collective-permute-start.10 = (f32[3,32,512]{2,1,0:T(8,128)S(1)}, f32[3,32,512]{2,1,0:T(8,128)S(1)}, u32[]{:S(2)}, u32[]{:S(2)}) collective-permute-start(f32[3,32,512]{2,1,0:T(8,128)S(1)} %get-tuple-element.120), channel_id=1, source_target_pairs={{0,4},{8,12},{16,20},{24,28},{4,0},{12,8},{20,16},{28,24},{1,5},{9... | collective-permute-start | bytes 589832 | tf_op jit(solution)/shard_map/ppermute | solution.py:371
  53.6 14.1 %collective-permute-start.11 = (f32[3,32,512]{2,1,0:T(8,128)S(1)}, f32[3,32,512]{2,1,0:T(8,128)S(1)}, u32[]{:S(2)}, u32[]{:S(2)}) collective-permute-start(f32[3,32,512]{2,1,0:T(8,128)S(1)} %get-tuple-element.121), channel_id=1, source_target_pairs={{4,8},{12,16},{20,24},{8,4},{16,12},{24,20},{5,9},{13,17},{21,25},... | collective-permute-start | bytes 589832 | tf_op jit(solution)/shard_map/ppermute | solution.py:371
  54.3 9.5 %collective-permute-start.12 = (f32[1,240,128]{2,1,0:T(8,128)S(1)}, f32[1,240,128]{2,1,0:T(8,128)S(1)}, u32[]{:S(2)}, u32[]{:S(2)}) collective-permute-start(f32[1,240,128]{2,1,0:T(8,128)S(1)} %get-tuple-element.122), channel_id=1, source_target_pairs={{0,8},{4,12},{8,16},{12,20},{16,24},{20,28},{1,9},{5,13},{9,17},{1... | collective-permute-start | bytes 368648 | tf_op jit(solution)/shard_map/ppermute | solution.py:517
  55.6 8.7 %collective-permute-start.13 = (f32[1,240,128]{2,1,0:T(8,128)S(1)}, f32[1,240,128]{2,1,0:T(8,128)S(1)}, u32[]{:S(2)}, u32[]{:S(2)}) collective-permute-start(f32[1,240,128]{2,1,0:T(8,128)S(1)} %get-tuple-element.123), channel_id=1, source_target_pairs={{0,12},{4,16},{8,20},{12,24},{16,28},{1,13},{5,17},{9,21},{13,25},... | collective-permute-start | bytes 368648 | tf_op jit(solution)/shard_map/ppermute | solution.py:517
  56.9 10.8 %collective-permute-start.14 = (f32[1,240,128]{2,1,0:T(8,128)S(1)}, f32[1,240,128]{2,1,0:T(8,128)S(1)}, u32[]{:S(2)}, u32[]{:S(2)}) collective-permute-start(f32[1,240,128]{2,1,0:T(8,128)S(1)} %get-tuple-element.124), channel_id=1, source_target_pairs={{0,24},{4,28},{1,25},{5,29},{2,26},{6,30},{3,27},{7,31}} | collective-permute-start | bytes 368648 | tf_op jit(solution)/shard_map/ppermute | solution.py:517
  71.4 8.5 %collective-permute-start.15 = (f32[1,240,128]{2,1,0:T(8,128)S(1)}, f32[1,240,128]{2,1,0:T(8,128)S(1)}, u32[]{:S(2)}, u32[]{:S(2)}) collective-permute-start(f32[1,240,128]{2,1,0:T(8,128)S(1)} %get-tuple-element.134), channel_id=1, source_target_pairs={{0,16},{4,20},{8,24},{12,28},{1,17},{5,21},{9,25},{13,29},{2,18},{... | collective-permute-start | bytes 368648 | tf_op jit(solution)/shard_map/ppermute | solution.py:517
  72.7 19.0 %collective-permute-start.16 = (f32[1,240,128]{2,1,0:T(8,128)S(1)}, f32[1,240,128]{2,1,0:T(8,128)S(1)}, u32[]{:S(2)}, u32[]{:S(2)}) collective-permute-start(f32[1,240,128]{2,1,0:T(8,128)S(1)} %get-tuple-element.135), channel_id=1, source_target_pairs={{0,20},{4,24},{8,28},{1,21},{5,25},{9,29},{2,22},{6,26},{10,30},{3... | collective-permute-start | bytes 368648 | tf_op jit(solution)/shard_map/ppermute | solution.py:517
  74.0 23.9 %collective-permute-start.20 = (f32[2,384,128]{2,1,0:T(8,128)S(1)}, f32[2,384,128]{2,1,0:T(8,128)S(1)}, u32[]{:S(2)}, u32[]{:S(2)}) collective-permute-start(f32[2,384,128]{2,1,0:T(8,128)S(1)} %get-tuple-element.139), channel_id=1, source_target_pairs={{0,4},{4,8},{8,12},{12,16},{16,20},{20,24},{24,28},{1,5},{5,9},{9,... | collective-permute-start | bytes 1179656 | tf_op jit(solution)/shard_map/ppermute | solution.py:517
  75.3 22.6 %collective-permute-start.21 = (f32[1,576,128]{2,1,0:T(8,128)S(1)}, f32[1,576,128]{2,1,0:T(8,128)S(1)}, u32[]{:S(2)}, u32[]{:S(2)}) collective-permute-start(f32[1,576,128]{2,1,0:T(8,128)S(1)} %get-tuple-element.140), channel_id=1, source_target_pairs={{0,28},{1,29},{2,30},{3,31}} | collective-permute-start | bytes 884744 | tf_op jit(solution)/shard_map/ppermute | solution.py:517
  76.6 18.8 %collective-permute-start.17 = (f32[1,240,128]{2,1,0:T(8,128)S(1)}, f32[1,240,128]{2,1,0:T(8,128)S(1)}, u32[]{:S(2)}, u32[]{:S(2)}) collective-permute-start(f32[1,240,128]{2,1,0:T(8,128)S(1)} %get-tuple-element.136), channel_id=1, source_target_pairs={{0,12},{4,16},{8,20},{12,24},{16,28},{1,13},{5,17},{9,21},{13,25},... | collective-permute-start | bytes 368648 | tf_op jit(solution)/shard_map/ppermute | solution.py:517
  79.9 15.5 %collective-permute-start.18 = (f32[1,240,128]{2,1,0:T(8,128)S(1)}, f32[1,240,128]{2,1,0:T(8,128)S(1)}, u32[]{:S(2)}, u32[]{:S(2)}) collective-permute-start(f32[1,240,128]{2,1,0:T(8,128)S(1)} %get-tuple-element.137), channel_id=1, source_target_pairs={{0,24},{4,28},{1,25},{5,29},{2,26},{6,30},{3,27},{7,31}} | collective-permute-start | bytes 368648 | tf_op jit(solution)/shard_map/ppermute | solution.py:517
  91.7 6.3 %collective-permute-start.19 = (f32[1,240,128]{2,1,0:T(8,128)S(1)}, f32[1,240,128]{2,1,0:T(8,128)S(1)}, u32[]{:S(2)}, u32[]{:S(2)}) collective-permute-start(f32[1,240,128]{2,1,0:T(8,128)S(1)} %get-tuple-element.138), channel_id=1, source_target_pairs={{0,8},{4,12},{8,16},{12,20},{16,24},{20,28},{1,9},{5,13},{9,17},{1... | collective-permute-start | bytes 368648 | tf_op jit(solution)/shard_map/ppermute | solution.py:517
  (9 other events, 40.7 us)
